TPU v7x, 32 devices: a whole 2x2x4 slice. The times are simulated.
32 devices in a mesh: groups: 2 (over x), eig: 16 (over z, y, core).
Axes of the slice: x: 2, y: 2, z: 4, core: 2. Of those that a mesh axis runs over, the one named last changes fastest.
Arguments:
- features: bfloat16 [1024, 32768], P(None, 'eig'), may hold values from -0.1875 to 0.1875
- responses: bfloat16 [1024, 2048], P(None, 'groups'), parts along dimension 1, may hold values from -6 to 6
- basis: bfloat16 [32768, 256], P('eig'), may hold values from -0.25 to 0.25
- eigenvalues: float32 [256], replicated, may hold values from 0.2 to 20
- reg_index: int32 [2048], P('groups'), parts along dimension 0, may hold values from 0 to 15
- subject: int32 [2048], P('groups'), parts along dimension 0, may hold values from 0 to 7
- alpha_table: float32 [8, 16], replicated, may hold values from 0.1 to 10
Outputs:
- weights: bfloat16 [32768, 2048], P('eig', 'groups'), parts along dimension 1
There are 2 independent parts, one for each index of `groups`. A program takes and returns all parts, laid end to end along the dimension named above; an argument that names none is the same for every part. Nothing has to cross between parts.
All inputs are finite; a program needn't handle non-finite values.
Results may differ from a plain program's by a relative error of at most 0.0049.
Values may be sent and summed in bfloat16 or wider, within the bound.
No kernel may reach another device: no remote copies, remote signals or barrier semaphores. Data moves between devices by JAX's collectives and lax.ppermute only.
A program may use at most 64 MiB of HBM per device.

v0:
```python
import jax
import jax.numpy as jnp
from jax import lax
from jax.sharding import PartitionSpec as P

SUBJECTS = 8
GRID = 16


def lookup_alpha(reg_index, subject, alpha_table):
    flat_codes = subject * GRID + reg_index
    codes = jnp.arange(SUBJECTS * GRID, dtype=jnp.int32)
    matches = flat_codes[:, None] == codes[None, :]
    table_row = alpha_table.reshape(-1)[None, :]
    return jnp.sum(jnp.where(matches, table_row, 0.0), axis=1)


def body(features, responses, basis, eigenvalues, reg_index, subject, alpha_table):
    highest = lax.Precision.HIGHEST
    alpha = lookup_alpha(reg_index, subject, alpha_table)
    own_rows = basis.shape[1] // lax.axis_size("eig")
    first_row = lax.axis_index("eig") * own_rows
    own_values = lax.dynamic_slice_in_dim(eigenvalues, first_row, own_rows, 0)
    columns = basis
    gram_rows = lax.psum_scatter(
        lax.dot_general(
            columns, features, (((0,), (1,)), ((), ())), preferred_element_type=jnp.float32
        ),
        "eig",
        scatter_dimension=0,
        tiled=True,
    )
    shares = jnp.dot(gram_rows, responses.astype(jnp.float32), precision=highest)
    scaled = (shares / (own_values[:, None] + alpha[None, :])).astype(jnp.bfloat16)
    columns = basis
    weights = jnp.dot(
        columns,
        lax.all_gather(scaled, "eig", axis=0, tiled=True),
        preferred_element_type=jnp.float32,
    )
    return weights.astype(jnp.bfloat16)


def solution(mesh):
    in_specs = (
        P(None, "eig"),
        P(None, "groups"),
        P("eig", None),
        P(),
        P("groups"),
        P("groups"),
        P(),
    )
    out_specs = P("eig", "groups")
    return jax.shard_map(body, mesh=mesh, in_specs=in_specs, out_specs=out_specs, check_vma=False)
```

profile of v0, /device:TPU:0, one launch (start us, length us, event | category | flops | bytes accessed | tf_op | source)
XLA Modules:
  0.0 110.9 jit_solution(441026992790981476)
XLA Ops:
  6.5 0.0 copy-start
  6.5 0.0 copy-start.1
  6.5 0.0 copy-start.4
  6.5 0.0 copy-start.5
  6.5 0.0 copy-start.3
  6.5 0.0 copy-start.2
  6.6 0.0 reduce-scatter.2.cloned.1.call-start
  6.6 4.9 %fusion.1 = f32[256,1024]{1,0:T(8,128)} fusion(bf16[2048,256]{1,0:T(8,128)(2,1)} %param.9, bf16[1024,2048]{1,0:T(8,128)(2,1)} %param.7), kind=kOutput, calls=%fused_computation.6 | convolution fusion | flops 1073741824 | bytes 6291456 | tf_op jit(solution)/shard_map/dot_general | solution.py:26
  11.5 0.0 reduce-scatter.2.cloned.1.call-update
  11.6 0.0 copy-done.4
  11.6 0.1 broadcast_in_dim.18
  11.6 0.0 copy-done.5
  11.7 0.1 dynamic_slice.3
  11.7 0.0 copy-done.3
  11.7 0.0 copy-done.2
  11.7 0.4 select_reduce_fusion
  12.1 59.7 %reduce-scatter.2.cloned.1.call-done = f32[16,1024]{1,0:T(8,128)} async-done(((f32[256,1024]{1,0:T(8,128)}), f32[16,1024]{1,0:T(8,128)}) %reduce-scatter.2.cloned.1.call-update) | async-done | bytes 65552 | tf_op jit(solution)/shard_map/reduce_scatter | solution.py:25
  71.8 0.0 copy-done
  71.8 1.8 %fusion = bf16[16,1024]{1,0:T(8,128)(2,1)S(1)} fusion(f32[16,1024]{1,0:T(8,128)} %reduce-scatter.2.cloned.1.call-done, bf16[1024,1024]{1,0:T(8,128)(2,1)S(1)} %copy-done, f32[1024]{0:T(1024)S(1)} %select_reduce_fusion, f32[16]{0:T(128)S(1)} %dynamic_slice.3), kind=kOutput, calls=%fused_computation.2 | convolution fusion | flops 201375744 | bytes 2199616 | tf_op jit(solution)/shard_map/dot_general | solution.py:33
  73.6 20.8 %all_gather.3 = bf16[256,1024]{1,0:T(8,128)(2,1)S(1)} all-gather(bf16[16,1024]{1,0:T(8,128)(2,1)S(1)} %fusion), channel_id=1, replica_groups=mesh['groups'=2,'eig'=16] {'eig'}, dimensions={0}, use_global_device_ids=true | all-gather | bytes 557056 | tf_op jit(solution)/shard_map/all_gather | solution.py:38
  94.4 0.0 copy-done.1
  94.4 3.3 %convert_bitcast_fusion = bf16[2048,1024]{0,1:T(8,128)(2,1)} fusion(bf16[256,1024]{1,0:T(8,128)(2,1)S(1)} %all_gather.3, bf16[2048,256]{1,0:T(8,128)(2,1)S(1)} %copy-done.1), kind=kOutput, calls=%fused_computation | convolution fusion | flops 1075838976 | bytes 5767168 | tf_op jit(solution)/shard_map/dot_general | solution.py:36
  97.6 6.4 %copy.9 = bf16[2048,1024]{1,0:T(8,128)(2,1)} copy(bf16[2048,1024]{0,1:T(8,128)(2,1)} %convert_bitcast_fusion) | data formatting | bytes 8388608 | tf_op jit(solution)/shard_map/convert_element_type | solution.py:41
  (1 shorter events, 0.0 us)
Async XLA Ops:
  6.5 65.3 %copy-start = (bf16[1024,1024]{1,0:T(8,128)(2,1)S(1)}, bf16[1024,1024]{1,0:T(8,128)(2,1)}, u32[]{:S(2)}) copy-start(bf16[1024,1024]{1,0:T(8,128)(2,1)} %param.8) | copy-start | bytes 6291460
  6.5 87.8 %copy-start.1 = (bf16[2048,256]{1,0:T(8,128)(2,1)S(1)}, bf16[2048,256]{1,0:T(8,128)(2,1)}, u32[]{:S(2)}) copy-start(bf16[2048,256]{1,0:T(8,128)(2,1)} %param.9) | copy-start | bytes 3145732
  6.5 5.0 %copy-start.4 = (f32[8,16]{1,0:T(8,128)S(1)}, f32[8,16]{1,0:T(8,128)}, u32[]{:S(2)}) copy-start(f32[8,16]{1,0:T(8,128)} %param.13) | copy-start | bytes 1540
  6.5 5.1 %copy-start.5 = (f32[256]{0:T(256)S(1)}, f32[256]{0:T(256)}, u32[]{:S(2)}) copy-start(f32[256]{0:T(256)} %param.10) | copy-start | bytes 3076
  6.5 5.2 %copy-start.3 = (s32[1024]{0:T(1024)S(1)}, s32[1024]{0:T(1024)}, u32[]{:S(2)}) copy-start(s32[1024]{0:T(1024)} %param.12) | copy-start | bytes 12292
  6.5 5.2 %copy-start.2 = (s32[1024]{0:T(1024)S(1)}, s32[1024]{0:T(1024)}, u32[]{:S(2)}) copy-start(s32[1024]{0:T(1024)} %param.11) | copy-start | bytes 12292
  6.6 65.3 %reduce-scatter.2.cloned.1.call-start = ((), (), s32[]{:S(2)}) async-start(), calls=%async_computation.1 | async-start | bytes 1114112 | tf_op jit(solution)/shard_map/reduce_scatter | solution.py:25
Sparse Core Ops, SparseCore 0:
  11.7 60.1 reduce-scatter.1
where the time goes:
time: 111 us
  waiting for transfers between devices  59.7 us (54%)
  blocking collectives  20.8 us (19%)
  between operations  13.4 us (12%)
  matrix products  9.95 us (9%)
  local copies, waits for them, and re-layouts  6.57 us (6%)
    reduce_scatter x1, waiting for transfers between devices, body(): lax.psum_scatter(lax.dot_general(columns, features, (((0,), (1,)), ((), (...  59.7 us
    all_gather x1, blocking collectives, body(): lax.all_gather(scaled, 'eig', axis=0, tiled=True)  20.8 us
    convert_element_type x1, local copies, waits for them, and re-layouts, body(): return weights.astype(jnp.bfloat16)  6.39 us
    dot_general x1, matrix products, body(): lax.dot_general(columns, features, (((0,), (1,)), ((), ())), preferred_el...  4.92 us
    dot_general x1, matrix products, body(): jnp.dot(columns, lax.all_gather(scaled, 'eig', axis=0, tiled=True), prefe...  3.26 us
  transfers between devices with their start and end apart: 1, of which 1 were waited for; matrix products, arithmetic and copies ran while one was open for 0% of the time, Pallas kernels for 0%

commit v1 on v0

v1 whole, which is shorter than its diff:
```python
import functools

import jax
import jax.numpy as jnp
from jax import lax
from jax.experimental import pallas as pl
from jax.experimental.pallas import tpu as pltpu
from jax.sharding import PartitionSpec as P

F32 = jnp.float32
BF16 = jnp.bfloat16


def lookup_alpha(reg_index, subject, alpha_table):
    subjects, grid = alpha_table.shape
    flat_codes = subject * grid + reg_index
    codes = jnp.arange(subjects * grid, dtype=jnp.int32)
    matches = flat_codes[:, None] == codes[None, :]
    table_row = alpha_table.reshape(-1)[None, :]
    return jnp.sum(jnp.where(matches, table_row, 0.0), axis=1)


def gram_kernel(steps, place_ref, f_ref, b_ref, own_ref, send_ref, acc_ref):
    i = pl.program_id(0)
    core = place_ref[1]
    half = own_ref.shape[1]

    @pl.when(i == 0)
    def _():
        acc_ref[...] = jnp.zeros_like(acc_ref)

    acc_ref[...] += jnp.dot(f_ref[...], b_ref[...], preferred_element_type=F32)

    @pl.when(i == steps - 1)
    def _():
        low, high = acc_ref[:, :half], acc_ref[:, half:]
        first = core == 0
        own_ref[...] = jnp.where(first, low, high)
        send_ref[...] = jnp.where(first, high, low).astype(BF16)


def gram(place, features, basis, groups):
    times, feats = features.shape
    k = basis.shape[1]
    rows = times // groups
    chunk = min(512, feats)
    steps = feats // chunk
    return pl.pallas_call(
        functools.partial(gram_kernel, steps),
        grid_spec=pltpu.PrefetchScalarGridSpec(
            num_scalar_prefetch=1,
            grid=(steps,),
            in_specs=[
                pl.BlockSpec((rows, chunk), lambda i, place: (place[0], i)),
                pl.BlockSpec((chunk, k), lambda i, place: (i, 0)),
            ],
            out_specs=[
                pl.BlockSpec((rows, k // 2), lambda i, place: (0, 0)),
                pl.BlockSpec((rows, k // 2), lambda i, place: (0, 0)),
            ],
            scratch_shapes=[pltpu.VMEM((rows, k), F32)],
        ),
        out_shape=[
            jax.ShapeDtypeStruct((rows, k // 2), F32),
            jax.ShapeDtypeStruct((rows, k // 2), BF16),
        ],
        name="gram",
    )(place, features, basis)


def spectrum_kernel(pieces, place_ref, *refs):
    piece_refs = refs[:pieces]
    r_ref, eig_ref, alpha_ref, out_ref = refs[pieces:]
    group = place_ref[0]
    rows = piece_refs[0].shape[0]
    total = jnp.zeros(out_ref.shape, F32)
    for m, piece in enumerate(piece_refs):
        start = pl.multiple_of((group ^ m) * rows, rows)
        total += lax.dot_general(
            piece[...].astype(BF16),
            r_ref[pl.ds(start, rows), :],
            (((0,), (0,)), ((), ())),
            preferred_element_type=F32,
        )
    out_ref[...] = (total / (eig_ref[...] + alpha_ref[...])).astype(BF16)


def spectrum(place, pieces, responses, eig_column, alpha_row):
    half = pieces[0].shape[1]
    vmem = pl.BlockSpec(memory_space=pltpu.VMEM)
    return pl.pallas_call(
        functools.partial(spectrum_kernel, len(pieces)),
        in_specs=[pl.BlockSpec(memory_space=pltpu.SMEM)] + [vmem] * (len(pieces) + 3),
        out_specs=vmem,
        out_shape=jax.ShapeDtypeStruct((half, responses.shape[1]), BF16),
        name="spectrum",
    )(place, *pieces, responses, eig_column, alpha_row)


def weights_kernel(place_ref, b_ref, own_ref, got_ref, out_ref):
    first = place_ref[1] == 0
    own, got = own_ref[...], got_ref[...]
    low = jnp.where(first, own, got)
    high = jnp.where(first, got, own)
    scaled = jnp.concatenate([low, high], axis=0)
    out_ref[...] = jnp.dot(b_ref[...], scaled, preferred_element_type=F32).astype(BF16)


def weights(place, basis, own, got):
    feats, k = basis.shape
    half, vox = own.shape
    chunk = min(256, feats)
    return pl.pallas_call(
        weights_kernel,
        grid_spec=pltpu.PrefetchScalarGridSpec(
            num_scalar_prefetch=1,
            grid=(feats // chunk,),
            in_specs=[
                pl.BlockSpec((chunk, k), lambda i, place: (i, 0)),
                pl.BlockSpec((half, vox), lambda i, place: (0, 0)),
                pl.BlockSpec((half, vox), lambda i, place: (0, 0)),
            ],
            out_specs=pl.BlockSpec((chunk, vox), lambda i, place: (i, 0)),
        ),
        out_shape=jax.ShapeDtypeStruct((feats, vox), BF16),
        name="weights",
    )(place, basis, own, got)


def swap(value, axis, bit):
    size = lax.axis_size(axis)
    return lax.ppermute(value, axis, [(i, i ^ bit) for i in range(size)])


def bits(size):
    out = []
    while (1 << len(out)) < size:
        out.append(1 << len(out))
    return out


def body(features, responses, basis, eigenvalues, reg_index, subject, alpha_table):
    groups = lax.axis_size("groups")
    group, eig = lax.axis_index("groups"), lax.axis_index("eig")
    core = eig & 1
    place = jnp.stack([group, core]).astype(jnp.int32)
    half = basis.shape[1] // 2

    alpha = lookup_alpha(reg_index, subject, alpha_table)[None, :]
    eig_column = lax.dynamic_slice_in_dim(eigenvalues, core * half, half, 0)[:, None]

    total, send = gram(place, features, basis, groups)
    total = total + swap(send, "eig", 1).astype(F32)
    for bit in bits(lax.axis_size("eig"))[1:]:
        total = total + swap(total.astype(BF16), "eig", bit).astype(F32)

    pieces = [total.astype(BF16)]
    for bit in bits(groups):
        pieces = pieces + [swap(piece, "groups", bit) for piece in pieces]
    own = spectrum(place, pieces, responses, eig_column, alpha)
    got = swap(own, "eig", 1)
    return weights(place, basis, own, got)


def solution(mesh):
    in_specs = (
        P(None, "eig"),
        P(None, "groups"),
        P("eig", None),
        P(),
        P("groups"),
        P("groups"),
        P(),
    )
    out_specs = P("eig", "groups")
    return jax.shard_map(body, mesh=mesh, in_specs=in_specs, out_specs=out_specs, check_vma=False)
```

time: 111 us -> 50.2 us (0.45)
  waiting for transfers between devices: 59.7 us -> 17.2 us
  blocking collectives: 20.8 us -> 0 us
  Pallas kernels: 0 us -> 15.4 us
  between operations: 13.4 us -> 0.04 us
  matrix products: 9.95 us -> 0 us
  starting transfers between devices: 0.04 us -> 9.21 us
  other arithmetic: 0.37 us -> 5.61 us
  local copies, waits for them, and re-layouts: 6.57 us -> 2.25 us
    reduce_scatter x1 -> x0, waiting for transfers between devices: 59.7 us -> none  [body(): lax.psum_scatter(lax.dot_general(columns, features, (((0,), (1,)), ((), (...]
    all_gather x1 -> x0, blocking collectives: 20.8 us -> none  [body(): lax.all_gather(scaled, 'eig', axis=0, tiled=True)]
    ppermute x0 -> x6, waiting for transfers between devices: none -> 17.2 us  [swap(): return lax.ppermute(value, axis, [(i, i ^ bit) for i in range(size)])]
    pallas_call x0 -> x3, Pallas kernels: none -> 15.4 us  [the longest x1 7.76 us: weights(): pl.pallas_call(weights_kernel, grid_spec=pltpu.PrefetchScalarGridSpec(num...]
    dot_general x3 -> x0, matrix products: 9.95 us -> none  [the longest x1 4.92 us: body(): lax.dot_general(columns, features, (((0,), (1,)), ((), ())), preferred_el...]
    ppermute x0 -> x6, starting transfers between devices: none -> 9.21 us  [swap(): return lax.ppermute(value, axis, [(i, i ^ bit) for i in range(size)])]
    convert_element_type x1 -> x0, local copies, waits for them, and re-layouts: 6.39 us -> none  [body(): return weights.astype(jnp.bfloat16)]
    convert_element_type x0 -> x4, other arithmetic: none -> 4.05 us  [the longest x3 3 us: body(): total = total + swap(total.astype(BF16), 'eig', bit).astype(F32)]
  transfers between devices with their start and end apart: 1 -> 6, of which waited for: 1 -> 6; matrix products, arithmetic and copies ran while one was open for 0% -> 4% of each run, Pallas kernels for 0% -> 0%
where the time goes in v1:
time: 50.2 us; the launch traced here: 49.7 us
  waiting for transfers between devices  17.2 us (34%)
  Pallas kernels  15.4 us (31%)
  starting transfers between devices  9.21 us (18%)
  other arithmetic  5.61 us (11%)
  local copies, waits for them, and re-layouts  2.25 us (4%)
    ppermute x6, waiting for transfers between devices, swap(): return lax.ppermute(value, axis, [(i, i ^ bit) for i in range(size)])  17.2 us
    ppermute x6, starting transfers between devices, swap(): return lax.ppermute(value, axis, [(i, i ^ bit) for i in range(size)])  9.21 us
    pallas_call x1, Pallas kernels, weights(): pl.pallas_call(weights_kernel, grid_spec=pltpu.PrefetchScalarGridSpec(num...  7.76 us
    pallas_call x1, Pallas kernels, gram(): pl.pallas_call(functools.partial(gram_kernel, steps), grid_spec=pltpu.Pre...  4.68 us
    convert_element_type x3, other arithmetic, body(): total = total + swap(total.astype(BF16), 'eig', bit).astype(F32)  3 us
    pallas_call x1, Pallas kernels, spectrum(): pl.pallas_call(functools.partial(spectrum_kernel, len(pieces)), in_specs=...  2.98 us
    unnamed x14, local copies, waits for them, and re-layouts  1.36 us
    convert_element_type x1, other arithmetic, body(): pieces = [total.astype(BF16)]  1.05 us
  transfers between devices with their start and end apart: 6, of which 6 were waited for; matrix products, arithmetic and copies ran while one was open for 4% of the time, Pallas kernels for 0%

profile of v1, /device:TPU:0, one launch (start us, length us, event | category | flops | bytes accessed | tf_op | source)
XLA Modules:
  0.0 49.7 jit_solution(15311751157356393561)
XLA Ops:
  0.0 0.0 copy-start
  0.0 0.0 copy-start.5
  0.0 0.0 copy-start.4
  0.0 0.0 copy-start.6
  0.0 0.6 %pad_add_fusion.place_ref = s32[2]{0:T(128)} fusion(s32[1]{0:T(128)} %bitcast.1, s32[1]{0:T(128)} %bitcast), kind=kLoop, calls=%fused_computation.9 | loop fusion | flops 2 | bytes 16 | tf_op jit(solution)/shard_map/stack | solution.py:146
  0.6 4.7 %gram.1 = (f32[512,128]{1,0:T(8,128)}, bf16[512,128]{1,0:T(8,128)(2,1)}) custom-call(s32[2]{0:T(128)} %pad_add_fusion.place_ref, bf16[1024,2048]{1,0:T(8,128)(2,1)} %f_ref.1, bf16[2048,256]{1,0:T(8,128)(2,1)} %b_ref.3), custom_call_target="tpu_custom_call" | custom-call | tf_op jit(solution)/shard_map/gram/pallas_call | solution.py:48
  5.3 0.5 collective-permute-start
  5.8 1.2 %collective-permute-done = bf16[512,128]{1,0:T(8,128)(2,1)S(1)} collective-permute-done((bf16[512,128]{1,0:T(8,128)(2,1)}, bf16[512,128]{1,0:T(8,128)(2,1)S(1)}, u32[]{:S(2)}, u32[]{:S(2)}) %collective-permute-start) | collective-permute-done | bytes 131104 | tf_op jit(solution)/shard_map/ppermute | solution.py:132
  7.0 1.0 %fusion = bf16[512,128]{1,0:T(8,128)(2,1)S(1)} fusion(f32[512,128]{1,0:T(8,128)} %get-tuple-element.7, bf16[512,128]{1,0:T(8,128)(2,1)S(1)} %collective-permute-done), kind=kLoop, calls=%fused_computation.6 | loop fusion | flops 196608 | bytes 524288 | tf_op jit(solution)/shard_map/convert_element_type | solution.py:155
  8.0 2.9 %collective-permute-start.1 = (bf16[512,128]{1,0:T(8,128)(2,1)S(1)}, bf16[512,128]{1,0:T(8,128)(2,1)S(1)}, u32[]{:S(2)}, u32[]{:S(2)}) collective-permute-start(bf16[512,128]{1,0:T(8,128)(2,1)S(1)} %fusion), channel_id=1, source_target_pairs={{0,2},{1,3},{2,0},{3,1},{4,6},{5,7},{6,4},{7,5},{8,10},{9,11},{10,... | collective-permute-start | bytes 393224 | tf_op jit(solution)/shard_map/ppermute | solution.py:132
  10.9 3.8 %collective-permute-done.1 = bf16[512,128]{1,0:T(8,128)(2,1)S(1)} collective-permute-done((bf16[512,128]{1,0:T(8,128)(2,1)S(1)}, bf16[512,128]{1,0:T(8,128)(2,1)S(1)}, u32[]{:S(2)}, u32[]{:S(2)}) %collective-permute-start.1) | collective-permute-done | bytes 131104 | tf_op jit(solution)/shard_map/ppermute | solution.py:132
  14.7 1.0 %fusion.2 = bf16[512,128]{1,0:T(8,128)(2,1)S(1)} fusion(bf16[512,128]{1,0:T(8,128)(2,1)S(1)} %collective-permute-done.1, f32[512,128]{1,0:T(8,128)} %get-tuple-element.7, bf16[512,128]{1,0:T(8,128)(2,1)S(1)} %collective-permute-done), kind=kLoop, calls=%fused_computation.11 | loop fusion | flops 327680 | bytes 655360 | tf_op jit(solution)/shard_map/convert_element_type | solution.py:155
  15.7 1.9 %collective-permute-start.2 = (bf16[512,128]{1,0:T(8,128)(2,1)S(1)}, bf16[512,128]{1,0:T(8,128)(2,1)S(1)}, u32[]{:S(2)}, u32[]{:S(2)}) collective-permute-start(bf16[512,128]{1,0:T(8,128)(2,1)S(1)} %fusion.2), channel_id=1, source_target_pairs={{0,4},{1,5},{2,6},{3,7},{4,0},{5,1},{6,2},{7,3},{8,12},{9,13},{10,... | collective-permute-start | bytes 393224 | tf_op jit(solution)/shard_map/ppermute | solution.py:132
  17.6 3.2 %collective-permute-done.2 = bf16[512,128]{1,0:T(8,128)(2,1)S(1)} collective-permute-done((bf16[512,128]{1,0:T(8,128)(2,1)S(1)}, bf16[512,128]{1,0:T(8,128)(2,1)S(1)}, u32[]{:S(2)}, u32[]{:S(2)}) %collective-permute-start.2) | collective-permute-done | bytes 131104 | tf_op jit(solution)/shard_map/ppermute | solution.py:132
  20.8 1.0 %fusion.1 = bf16[512,128]{1,0:T(8,128)(2,1)S(1)} fusion(bf16[512,128]{1,0:T(8,128)(2,1)S(1)} %collective-permute-done.2, bf16[512,128]{1,0:T(8,128)(2,1)S(1)} %collective-permute-done.1, f32[512,128]{1,0:T(8,128)} %get-tuple-element.7, bf16[512,128]{1,0:T(8,128)(2,1)S(1)} %collective-permute-done), kind=kLoop, calls=%fused_computation.7 | loop fusion | flops 458752 | bytes 786432 | tf_op jit(solution)/shard_map/convert_element_type | solution.py:155
  21.8 2.8 %collective-permute-start.3 = (bf16[512,128]{1,0:T(8,128)(2,1)S(1)}, bf16[512,128]{1,0:T(8,128)(2,1)S(1)}, u32[]{:S(2)}, u32[]{:S(2)}) collective-permute-start(bf16[512,128]{1,0:T(8,128)(2,1)S(1)} %fusion.1), channel_id=1, source_target_pairs={{0,8},{1,9},{2,10},{3,11},{4,12},{5,13},{6,14},{7,15},{8,0},{9,1},... | collective-permute-start | bytes 393224 | tf_op jit(solution)/shard_map/ppermute | solution.py:132
  24.6 0.0 copy-done.5
  24.7 0.0 copy-done.4
  24.7 5.1 %collective-permute-done.3 = bf16[512,128]{1,0:T(8,128)(2,1)S(1)} collective-permute-done((bf16[512,128]{1,0:T(8,128)(2,1)S(1)}, bf16[512,128]{1,0:T(8,128)(2,1)S(1)}, u32[]{:S(2)}, u32[]{:S(2)}) %collective-permute-start.3) | collective-permute-done | bytes 131104 | tf_op jit(solution)/shard_map/ppermute | solution.py:132
  29.8 1.0 %add_convert_fusion.refs_0_ = bf16[512,128]{1,0:T(8,128)(2,1)S(1)} fusion(bf16[512,128]{1,0:T(8,128)(2,1)S(1)} %collective-permute-done.3, bf16[512,128]{1,0:T(8,128)(2,1)S(1)} %collective-permute-done.2, bf16[512,128]{1,0:T(8,128)(2,1)S(1)} %collective-permute-done.1, f32[512,128]{1,0:T(8,128)} %get-tuple-element.7, bf16[512,128]{1,0:T(8,128)(2,1)S(1)} %collective-permute-done), kind=kLoop, calls=%fused_computation.2 | loop fusion | flops 589824 | bytes 917504 | tf_op jit(solution)/shard_map/convert_element_type | solution.py:157
  30.8 0.0 copy-start.1
  30.8 1.1 %collective-permute-start.4 = (bf16[512,128]{1,0:T(8,128)(2,1)S(1)}, bf16[512,128]{1,0:T(8,128)(2,1)S(1)}, u32[]{:S(2)}, u32[]{:S(2)}) collective-permute-start(bf16[512,128]{1,0:T(8,128)(2,1)S(1)} %add_convert_fusion.refs_0_), channel_id=1, source_target_pairs={{0,16},{16,0},{1,17},{17,1},{2,18},{18,2},{3,19},{19,3},{4,20},{20... | collective-permute-start | bytes 393224 | tf_op jit(solution)/shard_map/ppermute | solution.py:132
  32.0 0.0 copy-done
  32.0 0.1 dynamic-slice_bitcast_fusion
  32.0 0.0 copy-done.6
  32.0 0.1 broadcast_in_dim.23
  32.1 0.7 %copy.9.refs_3_ = f32[128,1]{1,0:T(8,128)} copy(f32[128,1]{0,1:T(1,128)S(1)} %dynamic-slice_bitcast_fusion) | data formatting | bytes 1024 | tf_op jit(solution)/shard_map/broadcast_in_dim | solution.py:150
  32.8 0.9 %select_reduce_fusion = f32[1024]{0:T(1024)} fusion(f32[128]{0:T(128)S(1)} %broadcast_in_dim.23, s32[1024]{0:T(1024)S(1)} %multiply_add_fusion), kind=kLoop, calls=%fused_computation | loop fusion | flops 392192 | bytes 8704 | tf_op jit(solution)/shard_map/reduce_sum | solution.py:20
  33.8 2.1 %collective-permute-done.4.refs_1_ = bf16[512,128]{1,0:T(8,128)(2,1)S(1)} collective-permute-done((bf16[512,128]{1,0:T(8,128)(2,1)S(1)}, bf16[512,128]{1,0:T(8,128)(2,1)S(1)}, u32[]{:S(2)}, u32[]{:S(2)}) %collective-permute-start.4) | collective-permute-done | bytes 131104 | tf_op jit(solution)/shard_map/ppermute | solution.py:132
  35.9 0.0 copy-start.3
  35.9 0.0 copy-done.1
  35.9 0.6 %copy-done.3 = bf16[512,128]{1,0:T(8,128)(2,1)} copy-done((bf16[512,128]{1,0:T(8,128)(2,1)}, bf16[512,128]{1,0:T(8,128)(2,1)S(1)}, u32[]{:S(2)}) %copy-start.3) | copy-done | bytes 131096
  36.5 3.0 %spectrum.1.own_ref = bf16[128,1024]{1,0:T(8,128)(2,1)} custom-call(s32[2]{0:T(128)} %pad_add_fusion.place_ref, bf16[512,128]{1,0:T(8,128)(2,1)} %copy-done.1, bf16[512,128]{1,0:T(8,128)(2,1)} %copy-done.3, bf16[1024,1024]{1,0:T(8,128)(2,1)} %refs_2_.1, f32[128,1]{1,0:T(8,128)} %copy.9.refs_3_, f32[1,1024]{1,0:T(1,128)} %bitcast.5), custom_call_target="tpu_custom_call" | custom-call | tf_op jit(solution)/shard_map/spectrum/pallas_call | solution.py:91
  39.5 0.0 collective-permute-start.5
  39.5 1.7 %collective-permute-done.5.got_ref = bf16[128,1024]{1,0:T(8,128)(2,1)S(1)} collective-permute-done((bf16[128,1024]{1,0:T(8,128)(2,1)}, bf16[128,1024]{1,0:T(8,128)(2,1)S(1)}, u32[]{:S(2)}, u32[]{:S(2)}) %collective-permute-start.5) | collective-permute-done | bytes 262176 | tf_op jit(solution)/shard_map/ppermute | solution.py:132
  41.2 0.0 copy-start.2
  41.2 0.7 %copy-done.2 = bf16[128,1024]{1,0:T(8,128)(2,1)} copy-done((bf16[128,1024]{1,0:T(8,128)(2,1)}, bf16[128,1024]{1,0:T(8,128)(2,1)S(1)}, u32[]{:S(2)}) %copy-start.2) | copy-done | bytes 262168
  41.9 7.8 %weights.1 = bf16[2048,1024]{1,0:T(8,128)(2,1)} custom-call(s32[2]{0:T(128)} %pad_add_fusion.place_ref, bf16[2048,256]{1,0:T(8,128)(2,1)} %b_ref.3, bf16[128,1024]{1,0:T(8,128)(2,1)} %spectrum.1.own_ref, bf16[128,1024]{1,0:T(8,128)(2,1)} %copy-done.2), custom_call_target="tpu_custom_call" | custom-call | tf_op jit(solution)/shard_map/weights/pallas_call | solution.py:113
  (1 shorter events, 0.0 us)
Async XLA Ops:
  0.0 32.0 %copy-start = (f32[256]{0:T(256)S(1)}, f32[256]{0:T(256)}, u32[]{:S(2)}) copy-start(f32[256]{0:T(256)} %param.10) | copy-start | bytes 3076
  0.0 24.6 %copy-start.5 = (s32[1024]{0:T(1024)S(1)}, s32[1024]{0:T(1024)}, u32[]{:S(2)}) copy-start(s32[1024]{0:T(1024)} %param.12) | copy-start | bytes 12292
  0.0 24.6 %copy-start.4 = (s32[1024]{0:T(1024)S(1)}, s32[1024]{0:T(1024)}, u32[]{:S(2)}) copy-start(s32[1024]{0:T(1024)} %param.11) | copy-start | bytes 12292
  0.0 32.0 %copy-start.6 = (f32[8,16]{1,0:T(8,128)S(1)}, f32[8,16]{1,0:T(8,128)}, u32[]{:S(2)}) copy-start(f32[8,16]{1,0:T(8,128)} %param.13) | copy-start | bytes 1540
  5.3 1.7 %collective-permute-start = (bf16[512,128]{1,0:T(8,128)(2,1)}, bf16[512,128]{1,0:T(8,128)(2,1)S(1)}, u32[]{:S(2)}, u32[]{:S(2)}) collective-permute-start(bf16[512,128]{1,0:T(8,128)(2,1)} %get-tuple-element.8), channel_id=1, source_target_pairs={{0,1},{1,0},{2,3},{3,2},{4,5},{5,4},{6,7},{7,6},{8,9},{9,8},{10,11... | collective-permute-start | bytes 393224 | tf_op jit(solution)/shard_map/ppermute | solution.py:132
  8.0 6.8 %collective-permute-start.1 = (bf16[512,128]{1,0:T(8,128)(2,1)S(1)}, bf16[512,128]{1,0:T(8,128)(2,1)S(1)}, u32[]{:S(2)}, u32[]{:S(2)}) collective-permute-start(bf16[512,128]{1,0:T(8,128)(2,1)S(1)} %fusion), channel_id=1, source_target_pairs={{0,2},{1,3},{2,0},{3,1},{4,6},{5,7},{6,4},{7,5},{8,10},{9,11},{10,... | collective-permute-start | bytes 393224 | tf_op jit(solution)/shard_map/ppermute | solution.py:132
  15.7 5.1 %collective-permute-start.2 = (bf16[512,128]{1,0:T(8,128)(2,1)S(1)}, bf16[512,128]{1,0:T(8,128)(2,1)S(1)}, u32[]{:S(2)}, u32[]{:S(2)}) collective-permute-start(bf16[512,128]{1,0:T(8,128)(2,1)S(1)} %fusion.2), channel_id=1, source_target_pairs={{0,4},{1,5},{2,6},{3,7},{4,0},{5,1},{6,2},{7,3},{8,12},{9,13},{10,... | collective-permute-start | bytes 393224 | tf_op jit(solution)/shard_map/ppermute | solution.py:132
  21.8 7.9 %collective-permute-start.3 = (bf16[512,128]{1,0:T(8,128)(2,1)S(1)}, bf16[512,128]{1,0:T(8,128)(2,1)S(1)}, u32[]{:S(2)}, u32[]{:S(2)}) collective-permute-start(bf16[512,128]{1,0:T(8,128)(2,1)S(1)} %fusion.1), channel_id=1, source_target_pairs={{0,8},{1,9},{2,10},{3,11},{4,12},{5,13},{6,14},{7,15},{8,0},{9,1},... | collective-permute-start | bytes 393224 | tf_op jit(solution)/shard_map/ppermute | solution.py:132
  30.8 5.0 %copy-start.1 = (bf16[512,128]{1,0:T(8,128)(2,1)}, bf16[512,128]{1,0:T(8,128)(2,1)S(1)}, u32[]{:S(2)}) copy-start(bf16[512,128]{1,0:T(8,128)(2,1)S(1)} %add_convert_fusion.refs_0_) | copy-start | bytes 393220
  30.8 5.0 %collective-permute-start.4 = (bf16[512,128]{1,0:T(8,128)(2,1)S(1)}, bf16[512,128]{1,0:T(8,128)(2,1)S(1)}, u32[]{:S(2)}, u32[]{:S(2)}) collective-permute-start(bf16[512,128]{1,0:T(8,128)(2,1)S(1)} %add_convert_fusion.refs_0_), channel_id=1, source_target_pairs={{0,16},{16,0},{1,17},{17,1},{2,18},{18,2},{3,19},{19,3},{4,20},{20... | collective-permute-start | bytes 393224 | tf_op jit(solution)/shard_map/ppermute | solution.py:132
  35.9 0.6 %copy-start.3 = (bf16[512,128]{1,0:T(8,128)(2,1)}, bf16[512,128]{1,0:T(8,128)(2,1)S(1)}, u32[]{:S(2)}) copy-start(bf16[512,128]{1,0:T(8,128)(2,1)S(1)} %collective-permute-done.4.refs_1_) | copy-start | bytes 393220
  39.5 1.7 %collective-permute-start.5 = (bf16[128,1024]{1,0:T(8,128)(2,1)}, bf16[128,1024]{1,0:T(8,128)(2,1)S(1)}, u32[]{:S(2)}, u32[]{:S(2)}) collective-permute-start(bf16[128,1024]{1,0:T(8,128)(2,1)} %spectrum.1.own_ref), channel_id=1, source_target_pairs={{0,1},{1,0},{2,3},{3,2},{4,5},{5,4},{6,7},{7,6},{8,9},{9,8},{10,11... | collective-permute-start | bytes 786440 | tf_op jit(solution)/shard_map/ppermute | solution.py:132
  41.2 0.7 %copy-start.2 = (bf16[128,1024]{1,0:T(8,128)(2,1)}, bf16[128,1024]{1,0:T(8,128)(2,1)S(1)}, u32[]{:S(2)}) copy-start(bf16[128,1024]{1,0:T(8,128)(2,1)S(1)} %collective-permute-done.5.got_ref) | copy-start | bytes 786436

commit v2 on v0

v2 whole, which is shorter than its diff:
```python
import functools

import jax
import jax.numpy as jnp
from jax import lax
from jax.experimental import pallas as pl
from jax.experimental.pallas import tpu as pltpu
from jax.sharding import PartitionSpec as P

F32 = jnp.float32
BF16 = jnp.bfloat16
MIB = 1 << 20
VMEM = pl.BlockSpec(memory_space=pltpu.VMEM)
SMEM = pl.BlockSpec(memory_space=pltpu.SMEM)
HBM = pl.BlockSpec(memory_space=pltpu.HBM)


def params(mib):
    return pltpu.CompilerParams(vmem_limit_bytes=mib * MIB)


def cost(flops, moved):
    return pl.CostEstimate(flops=flops, bytes_accessed=moved, transcendentals=0)


def core_index():
    return lax.axis_index("eig") & 1


def gram_kernel(f_hbm, b_hbm, own_ref, send_ref, f_ref, b_ref, f_sem, b_sem):
    rows, feats = f_ref.shape
    half = own_ref.shape[1]
    parts = f_sem.shape[0]
    chunk = feats // parts
    first_row = pl.multiple_of(lax.axis_index("groups") * rows, rows)
    copies = []
    for i in range(parts):
        cols = pl.ds(i * chunk, chunk)
        b_copy = pltpu.make_async_copy(b_hbm.at[cols], b_ref.at[cols], b_sem.at[i])
        f_copy = pltpu.make_async_copy(
            f_hbm.at[pl.ds(first_row, rows), cols], f_ref.at[:, cols], f_sem.at[i]
        )
        b_copy.start()
        f_copy.start()
        copies.append((b_copy, f_copy))
    total = None
    for i, (b_copy, f_copy) in enumerate(copies):
        cols = pl.ds(i * chunk, chunk)
        b_copy.wait()
        f_copy.wait()
        term = jnp.dot(f_ref[:, cols], b_ref[cols, :], preferred_element_type=F32)
        total = term if total is None else total + term
    low, high = total[:, :half], total[:, half:]
    first = core_index() == 0
    own_ref[...] = jnp.where(first, low, high)
    send_ref[...] = jnp.where(first, high, low).astype(BF16)


def gram(features, basis, groups):
    times, feats = features.shape
    k = basis.shape[1]
    rows = times // groups
    parts = 2
    return pl.pallas_call(
        gram_kernel,
        in_specs=[HBM, HBM],
        out_specs=[VMEM, VMEM],
        out_shape=[
            jax.ShapeDtypeStruct((rows, k // 2), F32),
            jax.ShapeDtypeStruct((rows, k // 2), BF16),
        ],
        scratch_shapes=[
            pltpu.VMEM((rows, feats), BF16),
            pltpu.VMEM((feats, k), BF16),
            pltpu.SemaphoreType.DMA((parts,)),
            pltpu.SemaphoreType.DMA((parts,)),
        ],
        compiler_params=params(12),
        cost_estimate=cost(2 * rows * feats * k, 2 * (rows + k) * feats),
        name="gram",
    )(features, basis)


def inverse_kernel(table_ref, reg_ref, subject_ref, eig_ref, out_ref):
    subjects, grid = table_ref.shape
    half = out_ref.shape[0]
    code = subject_ref[...] * grid + reg_ref[...]
    alpha = jnp.zeros(code.shape, F32)
    for s in range(subjects):
        for g in range(grid):
            alpha = jnp.where(code == s * grid + g, table_ref[s, g], alpha)
    eig_row = jnp.where(core_index() == 0, eig_ref[:, :half], eig_ref[:, half:])
    shape = (half, half)
    diagonal = lax.broadcasted_iota(jnp.int32, shape, 0) == lax.broadcasted_iota(jnp.int32, shape, 1)
    eig_column = jnp.sum(jnp.where(diagonal, eig_row, 0.0), axis=1, keepdims=True)
    out_ref[...] = 1.0 / (eig_column + alpha)


def inverse(alpha_table, reg_index, subject, eigenvalues):
    vox = reg_index.shape[0]
    k = eigenvalues.shape[0]
    return pl.pallas_call(
        inverse_kernel,
        in_specs=[SMEM, VMEM, VMEM, VMEM],
        out_specs=VMEM,
        out_shape=jax.ShapeDtypeStruct((k // 2, vox), F32),
        compiler_params=params(8),
        cost_estimate=cost(8 * k * vox, 2 * k * vox),
        name="inverse",
    )(alpha_table, reg_index[None, :], subject[None, :], eigenvalues[None, :])


def times_of(piece, r_ref, place):
    rows = piece.shape[0]
    start = pl.multiple_of(place * rows, rows)
    return lax.dot_general(
        piece[...], r_ref[pl.ds(start, rows), :], (((0,), (0,)), ((), ())), preferred_element_type=F32
    )


def share_kernel(piece_ref, r_ref, out_ref):
    out_ref[...] = times_of(piece_ref, r_ref, lax.axis_index("groups"))


def share(piece, responses):
    rows, half = piece.shape
    vox = responses.shape[1]
    return pl.pallas_call(
        share_kernel,
        in_specs=[VMEM, VMEM],
        out_specs=VMEM,
        out_shape=jax.ShapeDtypeStruct((half, vox), F32),
        compiler_params=params(8),
        cost_estimate=cost(2 * rows * half * vox, 2 * rows * vox),
        name="share",
    )(piece, responses)


def scale_kernel(pieces, *refs):
    part_ref, inverse_ref, r_ref, out_ref = refs[pieces:]
    group = lax.axis_index("groups")
    total = part_ref[...]
    for m in range(pieces):
        total += times_of(refs[m], r_ref, group ^ (m + 1))
    out_ref[...] = (total * inverse_ref[...]).astype(BF16)


def scale(part, pieces, inv, responses):
    half, vox = part.shape
    rows = responses.shape[0]
    return pl.pallas_call(
        functools.partial(scale_kernel, len(pieces)),
        in_specs=[VMEM] * (len(pieces) + 3),
        out_specs=VMEM,
        out_shape=jax.ShapeDtypeStruct((half, vox), BF16),
        compiler_params=params(8),
        cost_estimate=cost(2 * rows * half * vox, 2 * rows * vox),
        name="scale",
    )(*pieces, part, inv, responses)


def weights_kernel(b_ref, own_ref, got_ref, out_hbm, s_ref, out_ref, sems):
    parts = sems.shape[0]
    half, vox = own_ref.shape
    first = core_index() == 0
    own, got = own_ref[...], got_ref[...]
    s_ref[:half, :] = jnp.where(first, own, got)
    s_ref[half:, :] = jnp.where(first, got, own)
    chunk = vox // parts
    copies = []
    for i in range(parts):
        cols = pl.ds(i * chunk, chunk)
        out_ref[:, cols] = jnp.dot(b_ref[...], s_ref[:, cols], preferred_element_type=F32).astype(BF16)
        copy = pltpu.make_async_copy(out_ref.at[:, cols], out_hbm.at[:, cols], sems.at[i])
        copy.start()
        copies.append(copy)
    for copy in copies:
        copy.wait()


def weights(basis, own, got):
    feats, k = basis.shape
    half, vox = own.shape
    parts = 4
    return pl.pallas_call(
        weights_kernel,
        in_specs=[VMEM, VMEM, VMEM],
        out_specs=HBM,
        out_shape=jax.ShapeDtypeStruct((feats, vox), BF16),
        scratch_shapes=[
            pltpu.VMEM((k, vox), BF16),
            pltpu.VMEM((feats, vox), BF16),
            pltpu.SemaphoreType.DMA((parts,)),
        ],
        compiler_params=params(16),
        cost_estimate=cost(2 * feats * k * vox, 2 * feats * vox),
        name="weights",
    )(basis, own, got)


def swap(value, axis, bit):
    size = lax.axis_size(axis)
    return lax.ppermute(value, axis, [(i, i ^ bit) for i in range(size)])


def bits(size):
    out = []
    while (1 << len(out)) < size:
        out.append(1 << len(out))
    return out


def body(features, responses, basis, eigenvalues, reg_index, subject, alpha_table):
    groups = lax.axis_size("groups")
    total, send = gram(features, basis, groups)
    total = total + swap(send, "eig", 1).astype(F32)
    for bit in bits(lax.axis_size("eig"))[1:]:
        total = total + swap(total.astype(BF16), "eig", bit).astype(F32)

    pieces = [total.astype(BF16)]
    for bit in bits(groups):
        pieces = pieces + [swap(piece, "groups", bit) for piece in pieces]
    part = share(pieces[0], responses)
    inv = inverse(alpha_table, reg_index, subject, eigenvalues)
    own = scale(part, pieces[1:], inv, responses)
    got = swap(own, "eig", 1)
    return weights(basis, own, got)


def solution(mesh):
    in_specs = (
        P(None, "eig"),
        P(None, "groups"),
        P("eig", None),
        P(),
        P("groups"),
        P("groups"),
        P(),
    )
    out_specs = P("eig", "groups")
    return jax.shard_map(body, mesh=mesh, in_specs=in_specs, out_specs=out_specs, check_vma=False)
```

time: 111 us -> 36.4 us (0.33)
  waiting for transfers between devices: 59.7 us -> 17.4 us
  blocking collectives: 20.8 us -> 0 us
  between operations: 13.4 us -> 0.08 us
  matrix products: 9.95 us -> 0 us
  starting transfers between devices: 0.04 us -> 9.33 us
  Pallas kernels: 0 us -> 5.66 us
  local copies, waits for them, and re-layouts: 6.57 us -> 3.43 us
    reduce_scatter x1 -> x0, waiting for transfers between devices: 59.7 us -> none  [body(): lax.psum_scatter(lax.dot_general(columns, features, (((0,), (1,)), ((), (...]
    all_gather x1 -> x0, blocking collectives: 20.8 us -> none  [body(): lax.all_gather(scaled, 'eig', axis=0, tiled=True)]
    ppermute x0 -> x6, waiting for transfers between devices: none -> 17.4 us  [swap(): return lax.ppermute(value, axis, [(i, i ^ bit) for i in range(size)])]
    dot_general x3 -> x0, matrix products: 9.95 us -> none  [the longest x1 4.92 us: body(): lax.dot_general(columns, features, (((0,), (1,)), ((), ())), preferred_el...]
    ppermute x0 -> x6, starting transfers between devices: none -> 9.33 us  [swap(): return lax.ppermute(value, axis, [(i, i ^ bit) for i in range(size)])]
    convert_element_type x1 -> x0, local copies, waits for them, and re-layouts: 6.39 us -> none  [body(): return weights.astype(jnp.bfloat16)]
    pallas_call x0 -> x5, Pallas kernels: none -> 5.66 us  [the longest x1 2.79 us: weights(): pl.pallas_call(weights_kernel, in_specs=[VMEM, VMEM, VMEM], out_specs=HBM...]
    unnamed x12 -> x14, local copies, waits for them, and re-layouts: 0.02 us -> 3.43 us
  transfers between devices with their start and end apart: 1 -> 6, of which waited for: 1 -> 6; matrix products, arithmetic and copies ran while one was open for 0% -> 0% of each run, Pallas kernels for 0% -> 3%
where the time goes in v2:
time: 36.4 us; the launch traced here: 36.2 us
  waiting for transfers between devices  17.4 us (48%)
  starting transfers between devices  9.33 us (26%)
  Pallas kernels  5.66 us (16%)
  local copies, waits for them, and re-layouts  3.43 us (9%)
    ppermute x6, waiting for transfers between devices, swap(): return lax.ppermute(value, axis, [(i, i ^ bit) for i in range(size)])  17.4 us
    ppermute x6, starting transfers between devices, swap(): return lax.ppermute(value, axis, [(i, i ^ bit) for i in range(size)])  9.33 us
    unnamed x14, local copies, waits for them, and re-layouts  3.43 us
    pallas_call x1, Pallas kernels, weights(): pl.pallas_call(weights_kernel, in_specs=[VMEM, VMEM, VMEM], out_specs=HBM...  2.79 us
    pallas_call x1, Pallas kernels, gram(): pl.pallas_call(gram_kernel, in_specs=[HBM, HBM], out_specs=[VMEM, VMEM],...  1.43 us
    pallas_call x1, Pallas kernels, inverse(): pl.pallas_call(inverse_kernel, in_specs=[SMEM, VMEM, VMEM, VMEM], out_spe...  0.76 us
  transfers between devices with their start and end apart: 6, of which 6 were waited for; matrix products, arithmetic and copies ran while one was open for 0% of the time, Pallas kernels for 3%

profile of v2, /device:TPU:0, one launch (start us, length us, event | category | flops | bytes accessed | tf_op | source)
XLA Modules:
  0.0 36.2 jit_solution(18350265107286012035)
XLA Ops:
  0.0 0.0 copy-start.1
  0.0 2.2 %copy-done.1 = bf16[1024,2048]{1,0:T(8,128)(2,1)S(1)} copy-done((bf16[1024,2048]{1,0:T(8,128)(2,1)S(1)}, bf16[1024,2048]{1,0:T(8,128)(2,1)}, u32[]{:S(2)}) %copy-start.1) | copy-done | bytes 4194328
  2.2 0.0 copy-start.2
  2.2 1.2 %copy-done.2 = bf16[2048,256]{1,0:T(8,128)(2,1)S(1)} copy-done((bf16[2048,256]{1,0:T(8,128)(2,1)S(1)}, bf16[2048,256]{1,0:T(8,128)(2,1)}, u32[]{:S(2)}) %copy-start.2) | copy-done | bytes 1048600
  3.4 0.0 copy-start.3
  3.4 0.0 copy-start.4
  3.4 0.0 copy-start.5
  3.4 0.0 copy-start.6
  3.4 0.0 copy-start
  3.4 1.4 %gram.1 = (f32[512,128]{1,0:T(8,128)S(1)}, bf16[512,128]{1,0:T(8,128)(2,1)S(1)}) custom-call(bf16[1024,2048]{1,0:T(8,128)(2,1)S(1)} %copy-done.1, bf16[2048,256]{1,0:T(8,128)(2,1)S(1)} %copy-done.2), custom_call_target="tpu_custom_call" | custom-call | flops 536870912 | bytes 3145728 | tf_op jit(solution)/shard_map/gram/pallas_call | solution.py:64
  4.9 0.5 %collective-permute-start = (bf16[512,128]{1,0:T(8,128)(2,1)S(1)}, bf16[512,128]{1,0:T(8,128)(2,1)S(1)}, u32[]{:S(2)}, u32[]{:S(2)}) collective-permute-start(bf16[512,128]{1,0:T(8,128)(2,1)S(1)} %get-tuple-element.8), channel_id=1, source_target_pairs={{0,1},{1,0},{2,3},{3,2},{4,5},{5,4},{6,7},{7,6},{8,9},{9,8},{10,11... | collective-permute-start | bytes 393224 | tf_op jit(solution)/shard_map/ppermute | solution.py:203
  5.4 1.0 %collective-permute-done = bf16[512,128]{1,0:T(8,128)(2,1)S(1)} collective-permute-done((bf16[512,128]{1,0:T(8,128)(2,1)S(1)}, bf16[512,128]{1,0:T(8,128)(2,1)S(1)}, u32[]{:S(2)}, u32[]{:S(2)}) %collective-permute-start) | collective-permute-done | bytes 131104 | tf_op jit(solution)/shard_map/ppermute | solution.py:203
  6.4 2.9 %collective-permute-start.1 = (bf16[512,128]{1,0:T(8,128)(2,1)S(1)}, bf16[512,128]{1,0:T(8,128)(2,1)S(1)}, u32[]{:S(2)}, u32[]{:S(2)}) collective-permute-start(bf16[512,128]{1,0:T(8,128)(2,1)S(1)} %fusion), channel_id=1, source_target_pairs={{0,2},{1,3},{2,0},{3,1},{4,6},{5,7},{6,4},{7,5},{8,10},{9,11},{10,... | collective-permute-start | bytes 393224 | tf_op jit(solution)/shard_map/ppermute | solution.py:203
  9.4 3.8 %collective-permute-done.1 = bf16[512,128]{1,0:T(8,128)(2,1)S(1)} collective-permute-done((bf16[512,128]{1,0:T(8,128)(2,1)S(1)}, bf16[512,128]{1,0:T(8,128)(2,1)S(1)}, u32[]{:S(2)}, u32[]{:S(2)}) %collective-permute-start.1) | collective-permute-done | bytes 131104 | tf_op jit(solution)/shard_map/ppermute | solution.py:203
  13.2 0.1 fusion.2
  13.2 1.9 %collective-permute-start.2 = (bf16[512,128]{1,0:T(8,128)(2,1)S(1)}, bf16[512,128]{1,0:T(8,128)(2,1)S(1)}, u32[]{:S(2)}, u32[]{:S(2)}) collective-permute-start(bf16[512,128]{1,0:T(8,128)(2,1)S(1)} %fusion.2), channel_id=1, source_target_pairs={{0,4},{1,5},{2,6},{3,7},{4,0},{5,1},{6,2},{7,3},{8,12},{9,13},{10,... | collective-permute-start | bytes 393224 | tf_op jit(solution)/shard_map/ppermute | solution.py:203
  15.1 3.2 %collective-permute-done.2 = bf16[512,128]{1,0:T(8,128)(2,1)S(1)} collective-permute-done((bf16[512,128]{1,0:T(8,128)(2,1)S(1)}, bf16[512,128]{1,0:T(8,128)(2,1)S(1)}, u32[]{:S(2)}, u32[]{:S(2)}) %collective-permute-start.2) | collective-permute-done | bytes 131104 | tf_op jit(solution)/shard_map/ppermute | solution.py:203
  18.3 0.1 fusion.1
  18.4 2.8 %collective-permute-start.3 = (bf16[512,128]{1,0:T(8,128)(2,1)S(1)}, bf16[512,128]{1,0:T(8,128)(2,1)S(1)}, u32[]{:S(2)}, u32[]{:S(2)}) collective-permute-start(bf16[512,128]{1,0:T(8,128)(2,1)S(1)} %fusion.1), channel_id=1, source_target_pairs={{0,8},{1,9},{2,10},{3,11},{4,12},{5,13},{6,14},{7,15},{8,0},{9,1},... | collective-permute-start | bytes 393224 | tf_op jit(solution)/shard_map/ppermute | solution.py:203
  21.2 5.1 %collective-permute-done.3 = bf16[512,128]{1,0:T(8,128)(2,1)S(1)} collective-permute-done((bf16[512,128]{1,0:T(8,128)(2,1)S(1)}, bf16[512,128]{1,0:T(8,128)(2,1)S(1)}, u32[]{:S(2)}, u32[]{:S(2)}) %collective-permute-start.3) | collective-permute-done | bytes 131104 | tf_op jit(solution)/shard_map/ppermute | solution.py:203
  26.3 0.1 add_convert_fusion.piece_ref
  26.4 1.1 %collective-permute-start.4 = (bf16[512,128]{1,0:T(8,128)(2,1)S(1)}, bf16[512,128]{1,0:T(8,128)(2,1)S(1)}, u32[]{:S(2)}, u32[]{:S(2)}) collective-permute-start(bf16[512,128]{1,0:T(8,128)(2,1)S(1)} %add_convert_fusion.piece_ref), channel_id=1, source_target_pairs={{0,16},{16,0},{1,17},{17,1},{2,18},{18,2},{3,19},{19,3},{4,20},{20... | collective-permute-start | bytes 393224 | tf_op jit(solution)/shard_map/ppermute | solution.py:203
  27.6 0.0 copy-done.3
  27.6 0.0 copy-done.4
  27.6 0.0 copy-done.5
  27.6 0.0 copy-done.6
  27.6 0.8 %inverse.1.refs_2_ = f32[128,1024]{1,0:T(8,128)S(1)} custom-call(f32[8,16]{1,0:T(8,128)S(1)} %copy-done.3, s32[1,1024]{1,0:T(1,128)S(1)} %bitcast.3, s32[1,1024]{1,0:T(1,128)S(1)} %bitcast.4, f32[1,256]{1,0:T(1,128)S(1)} %bitcast.5), custom_call_target="tpu_custom_call" | custom-call | flops 2097152 | bytes 524288 | tf_op jit(solution)/shard_map/inverse/pallas_call | solution.py:102
  28.3 0.0 copy-done
  28.3 0.3 share.1.refs_1_
  28.7 2.8 %collective-permute-done.4.refs_0_ = bf16[512,128]{1,0:T(8,128)(2,1)S(1)} collective-permute-done((bf16[512,128]{1,0:T(8,128)(2,1)S(1)}, bf16[512,128]{1,0:T(8,128)(2,1)S(1)}, u32[]{:S(2)}, u32[]{:S(2)}) %collective-permute-start.4) | collective-permute-done | bytes 131104 | tf_op jit(solution)/shard_map/ppermute | solution.py:203
  31.5 0.3 scale.1.own_ref
  31.8 0.1 collective-permute-start.5
  31.9 1.5 %collective-permute-done.5.got_ref = bf16[128,1024]{1,0:T(8,128)(2,1)S(1)} collective-permute-done((bf16[128,1024]{1,0:T(8,128)(2,1)S(1)}, bf16[128,1024]{1,0:T(8,128)(2,1)S(1)}, u32[]{:S(2)}, u32[]{:S(2)}) %collective-permute-start.5) | collective-permute-done | bytes 262176 | tf_op jit(solution)/shard_map/ppermute | solution.py:203
  33.4 2.8 %weights.1 = bf16[2048,1024]{1,0:T(8,128)(2,1)} custom-call(bf16[2048,256]{1,0:T(8,128)(2,1)S(1)} %copy-done.2, bf16[128,1024]{1,0:T(8,128)(2,1)S(1)} %scale.1.own_ref, bf16[128,1024]{1,0:T(8,128)(2,1)S(1)} %collective-permute-done.5.got_ref), custom_call_target="tpu_custom_call" | custom-call | flops 1073741824 | bytes 4194304 | tf_op jit(solution)/shard_map/weights/pallas_call | solution.py:185
  (1 shorter events, 0.0 us)
Async XLA Ops:
  0.0 2.2 %copy-start.1 = (bf16[1024,2048]{1,0:T(8,128)(2,1)S(1)}, bf16[1024,2048]{1,0:T(8,128)(2,1)}, u32[]{:S(2)}) copy-start(bf16[1024,2048]{1,0:T(8,128)(2,1)} %f_hbm.1) | copy-start | bytes 12582916
  2.2 1.2 %copy-start.2 = (bf16[2048,256]{1,0:T(8,128)(2,1)S(1)}, bf16[2048,256]{1,0:T(8,128)(2,1)}, u32[]{:S(2)}) copy-start(bf16[2048,256]{1,0:T(8,128)(2,1)} %b_ref.1) | copy-start | bytes 3145732
  3.4 24.1 %copy-start.3 = (f32[8,16]{1,0:T(8,128)S(1)}, f32[8,16]{1,0:T(8,128)}, u32[]{:S(2)}) copy-start(f32[8,16]{1,0:T(8,128)} %table_ref.1) | copy-start | bytes 1540
  3.4 24.1 %copy-start.4 = (s32[1024]{0:T(1024)S(1)}, s32[1024]{0:T(1024)}, u32[]{:S(2)}) copy-start(s32[1024]{0:T(1024)} %param.11) | copy-start | bytes 12292
  3.4 24.1 %copy-start.5 = (s32[1024]{0:T(1024)S(1)}, s32[1024]{0:T(1024)}, u32[]{:S(2)}) copy-start(s32[1024]{0:T(1024)} %param.12) | copy-start | bytes 12292
  3.4 24.1 %copy-start.6 = (f32[256]{0:T(256)S(1)}, f32[256]{0:T(256)}, u32[]{:S(2)}) copy-start(f32[256]{0:T(256)} %param.10) | copy-start | bytes 3076
  3.4 24.9 %copy-start = (bf16[1024,1024]{1,0:T(8,128)(2,1)S(1)}, bf16[1024,1024]{1,0:T(8,128)(2,1)}, u32[]{:S(2)}) copy-start(bf16[1024,1024]{1,0:T(8,128)(2,1)} %refs_3_.1) | copy-start | bytes 6291460
  4.9 1.5 %collective-permute-start = (bf16[512,128]{1,0:T(8,128)(2,1)S(1)}, bf16[512,128]{1,0:T(8,128)(2,1)S(1)}, u32[]{:S(2)}, u32[]{:S(2)}) collective-permute-start(bf16[512,128]{1,0:T(8,128)(2,1)S(1)} %get-tuple-element.8), channel_id=1, source_target_pairs={{0,1},{1,0},{2,3},{3,2},{4,5},{5,4},{6,7},{7,6},{8,9},{9,8},{10,11... | collective-permute-start | bytes 393224 | tf_op jit(solution)/shard_map/ppermute | solution.py:203
  6.4 6.8 %collective-permute-start.1 = (bf16[512,128]{1,0:T(8,128)(2,1)S(1)}, bf16[512,128]{1,0:T(8,128)(2,1)S(1)}, u32[]{:S(2)}, u32[]{:S(2)}) collective-permute-start(bf16[512,128]{1,0:T(8,128)(2,1)S(1)} %fusion), channel_id=1, source_target_pairs={{0,2},{1,3},{2,0},{3,1},{4,6},{5,7},{6,4},{7,5},{8,10},{9,11},{10,... | collective-permute-start | bytes 393224 | tf_op jit(solution)/shard_map/ppermute | solution.py:203
  13.2 5.1 %collective-permute-start.2 = (bf16[512,128]{1,0:T(8,128)(2,1)S(1)}, bf16[512,128]{1,0:T(8,128)(2,1)S(1)}, u32[]{:S(2)}, u32[]{:S(2)}) collective-permute-start(bf16[512,128]{1,0:T(8,128)(2,1)S(1)} %fusion.2), channel_id=1, source_target_pairs={{0,4},{1,5},{2,6},{3,7},{4,0},{5,1},{6,2},{7,3},{8,12},{9,13},{10,... | collective-permute-start | bytes 393224 | tf_op jit(solution)/shard_map/ppermute | solution.py:203
  18.4 7.9 %collective-permute-start.3 = (bf16[512,128]{1,0:T(8,128)(2,1)S(1)}, bf16[512,128]{1,0:T(8,128)(2,1)S(1)}, u32[]{:S(2)}, u32[]{:S(2)}) collective-permute-start(bf16[512,128]{1,0:T(8,128)(2,1)S(1)} %fusion.1), channel_id=1, source_target_pairs={{0,8},{1,9},{2,10},{3,11},{4,12},{5,13},{6,14},{7,15},{8,0},{9,1},... | collective-permute-start | bytes 393224 | tf_op jit(solution)/shard_map/ppermute | solution.py:203
  26.4 5.0 %collective-permute-start.4 = (bf16[512,128]{1,0:T(8,128)(2,1)S(1)}, bf16[512,128]{1,0:T(8,128)(2,1)S(1)}, u32[]{:S(2)}, u32[]{:S(2)}) collective-permute-start(bf16[512,128]{1,0:T(8,128)(2,1)S(1)} %add_convert_fusion.piece_ref), channel_id=1, source_target_pairs={{0,16},{16,0},{1,17},{17,1},{2,18},{18,2},{3,19},{19,3},{4,20},{20... | collective-permute-start | bytes 393224 | tf_op jit(solution)/shard_map/ppermute | solution.py:203
  31.8 1.6 %collective-permute-start.5 = (bf16[128,1024]{1,0:T(8,128)(2,1)S(1)}, bf16[128,1024]{1,0:T(8,128)(2,1)S(1)}, u32[]{:S(2)}, u32[]{:S(2)}) collective-permute-start(bf16[128,1024]{1,0:T(8,128)(2,1)S(1)} %scale.1.own_ref), channel_id=1, source_target_pairs={{0,1},{1,0},{2,3},{3,2},{4,5},{5,4},{6,7},{7,6},{8,9},{9,8},{10,11... | collective-permute-start | bytes 786440 | tf_op jit(solution)/shard_map/ppermute | solution.py:203

commit v3 on v2

v3 whole, which is shorter than its diff:
```python
import functools

import jax
import jax.numpy as jnp
from jax import lax
from jax.experimental import pallas as pl
from jax.experimental.pallas import tpu as pltpu
from jax.sharding import PartitionSpec as P

F32 = jnp.float32
BF16 = jnp.bfloat16
MIB = 1 << 20
CHAINS = 2
ANY = pl.BlockSpec(memory_space=pl.ANY)
HBM = pl.BlockSpec(memory_space=pltpu.HBM)
VMEM = pl.BlockSpec(memory_space=pltpu.VMEM)
SMEM = pl.BlockSpec(memory_space=pltpu.SMEM)


def params(mib):
    return pltpu.CompilerParams(vmem_limit_bytes=mib * MIB)


def cost(flops, moved):
    return pl.CostEstimate(flops=flops, bytes_accessed=moved, transcendentals=0)


def in_hbm(value):
    return pltpu.with_memory_space_constraint(value, pltpu.HBM)


def core_index():
    return lax.axis_index("eig") & 1


def gram_kernel(f_hbm, b_hbm, *refs):
    *outs, f_ref, b_ref, f_sem, b_sem = refs
    totals, sends = outs[:CHAINS], outs[CHAINS:]
    rows, feats = f_ref.shape
    half = b_ref.shape[1] // 2
    parts = f_sem.shape[0]
    chunk = feats // parts
    first_row = pl.multiple_of(lax.axis_index("groups") * rows, rows)
    copies = []
    for i in range(parts):
        cols = pl.ds(i * chunk, chunk)
        b_copy = pltpu.make_async_copy(b_hbm.at[cols], b_ref.at[cols], b_sem.at[i])
        f_copy = pltpu.make_async_copy(
            f_hbm.at[pl.ds(first_row, rows), cols], f_ref.at[:, cols], f_sem.at[i]
        )
        b_copy.start()
        f_copy.start()
        copies.append((b_copy, f_copy))
    total = None
    for i, (b_copy, f_copy) in enumerate(copies):
        cols = pl.ds(i * chunk, chunk)
        b_copy.wait()
        f_copy.wait()
        term = jnp.dot(f_ref[:, cols], b_ref[cols, :], preferred_element_type=F32)
        total = term if total is None else total + term
    low, high = total[:, :half], total[:, half:]
    first = core_index() == 0
    kept = jnp.where(first, low, high)
    sent = jnp.where(first, high, low).astype(BF16)
    size = rows // CHAINS
    for i in range(CHAINS):
        totals[i][...] = kept[i * size : (i + 1) * size]
        sends[i][...] = sent[i * size : (i + 1) * size]


def gram(features, basis, groups):
    times, feats = features.shape
    k = basis.shape[1]
    rows = times // groups
    parts = 2
    out = [
        jax.ShapeDtypeStruct((rows // CHAINS, k // 2), dtype) for dtype in (F32, BF16) for _ in range(CHAINS)
    ]
    result = pl.pallas_call(
        gram_kernel,
        in_specs=[HBM, HBM],
        out_specs=[VMEM] * len(out),
        out_shape=out,
        scratch_shapes=[
            pltpu.VMEM((rows, feats), BF16),
            pltpu.VMEM((feats, k), BF16),
            pltpu.SemaphoreType.DMA((parts,)),
            pltpu.SemaphoreType.DMA((parts,)),
        ],
        compiler_params=params(12),
        cost_estimate=cost(2 * rows * feats * k, 2 * (rows + k) * feats),
        name="gram",
    )(in_hbm(features), in_hbm(basis))
    return list(result[:CHAINS]), list(result[CHAINS:])


def inverse_kernel(table_ref, reg_ref, subject_ref, eig_ref, *refs):
    out_ref = refs[-1]
    subjects, grid = table_ref.shape
    k = out_ref.shape[0]
    code = subject_ref[...] * grid + reg_ref[...]
    alpha = jnp.zeros(code.shape, F32)
    for s in range(subjects):
        for g in range(grid):
            alpha = jnp.where(code == s * grid + g, table_ref[s, g], alpha)
    side = min(k, 128)
    first = core_index() == 0
    eig = jnp.where(first, eig_ref[:, :k], eig_ref[:, k:])
    shape = (side, side)
    diagonal = lax.broadcasted_iota(jnp.int32, shape, 0) == lax.broadcasted_iota(jnp.int32, shape, 1)
    for i in range(k // side):
        at = pl.ds(i * side, side)
        column = jnp.sum(jnp.where(diagonal, eig[:, i * side : (i + 1) * side], 0.0), axis=1, keepdims=True)
        out_ref[at, :] = 1.0 / (column + alpha)


def inverse(alpha_table, reg_index, subject, eigenvalues, after):
    vox = reg_index.shape[0]
    k = eigenvalues.shape[0] // 2
    return pl.pallas_call(
        inverse_kernel,
        in_specs=[SMEM, VMEM, VMEM, VMEM] + [ANY] * len(after),
        out_specs=VMEM,
        out_shape=jax.ShapeDtypeStruct((k, vox), F32),
        compiler_params=params(8),
        cost_estimate=cost(8 * k * vox, 2 * k * vox),
        name="inverse",
    )(alpha_table, reg_index[None, :], subject[None, :], eigenvalues[None, :], *after)


def add_kernel(total_ref, got_ref, *refs):
    out_ref, send_ref = refs[-2:]
    total = total_ref[...] + got_ref[...].astype(F32)
    out_ref[...] = total
    send_ref[...] = total.astype(BF16)


def add_last_kernel(total_ref, got_ref, *refs):
    refs[-1][...] = (total_ref[...] + got_ref[...].astype(F32)).astype(BF16)


def add(total, got, after, last=False):
    shape = total.shape
    both = [jax.ShapeDtypeStruct(shape, F32), jax.ShapeDtypeStruct(shape, BF16)]
    return pl.pallas_call(
        add_last_kernel if last else add_kernel,
        in_specs=[VMEM, VMEM] + [ANY] * len(after),
        out_specs=VMEM if last else [VMEM, VMEM],
        out_shape=both[1] if last else both,
        compiler_params=params(4),
        cost_estimate=cost(total.size, 12 * total.size),
        name="add",
    )(total, got, *after)


def share_kernel(places, has_sum, finish, *refs):
    n = len(places)
    r_ref, out_ref = refs[n], refs[-1]
    rest = list(refs[n + 1 : -1])
    group = lax.axis_index("groups")
    total = rest.pop(0)[...] if has_sum else None
    for (m, at), piece in zip(places, refs):
        rows = piece.shape[0]
        start = pl.multiple_of(((group ^ m) * CHAINS + at) * rows, rows)
        term = lax.dot_general(
            piece[...], r_ref[pl.ds(start, rows), :], (((0,), (0,)), ((), ())), preferred_element_type=F32
        )
        total = term if total is None else total + term
    if finish:
        total = total * rest.pop(0)[...]
    out_ref[...] = total.astype(out_ref.dtype)


def share(places, pieces, responses, before=None, inv=None):
    rows, k = pieces[0].shape
    vox = responses.shape[1]
    extra = [value for value in (before, inv) if value is not None]
    return pl.pallas_call(
        functools.partial(share_kernel, places, before is not None, inv is not None),
        in_specs=[VMEM] * (len(pieces) + 1 + len(extra)),
        out_specs=VMEM,
        out_shape=jax.ShapeDtypeStruct((k, vox), F32 if inv is None else BF16),
        compiler_params=params(8),
        cost_estimate=cost(2 * len(places) * rows * k * vox, 2 * rows * vox),
        name="share",
    )(*pieces, responses, *extra)


def weights_kernel(b_ref, own_ref, got_ref, out_hbm, s_ref, out_ref, sems):
    parts = sems.shape[0]
    half = own_ref.shape[0]
    first = core_index() == 0
    own, got = own_ref[...], got_ref[...]
    s_ref[:half, :] = jnp.where(first, own, got)
    s_ref[half:, :] = jnp.where(first, got, own)
    chunk = b_ref.shape[0] // parts
    copies = []
    for i in range(parts):
        rows = pl.ds(i * chunk, chunk)
        out_ref[rows, :] = jnp.dot(b_ref[rows, :], s_ref[...], preferred_element_type=F32).astype(BF16)
        copy = pltpu.make_async_copy(out_ref.at[rows], out_hbm.at[rows], sems.at[i])
        copy.start()
        copies.append(copy)
    for copy in copies:
        copy.wait()


def weights(basis, own, got):
    feats, k = basis.shape
    half, vox = own.shape
    parts = 8
    return pl.pallas_call(
        weights_kernel,
        in_specs=[VMEM, VMEM, VMEM],
        out_specs=HBM,
        out_shape=jax.ShapeDtypeStruct((feats, vox), BF16),
        scratch_shapes=[
            pltpu.VMEM((k, vox), BF16),
            pltpu.VMEM((feats, vox), BF16),
            pltpu.SemaphoreType.DMA((parts,)),
        ],
        compiler_params=params(16),
        cost_estimate=cost(2 * feats * k * vox, 2 * feats * vox),
        name="weights",
    )(basis, own, got)


def swap(value, axis, mask):
    return lax.ppermute(value, axis, [(i, i ^ mask) for i in range(lax.axis_size(axis))])


def bits(size):
    out = []
    while (1 << len(out)) < size:
        out.append(1 << len(out))
    return out


def orders(size):
    steps = bits(size)[1:]
    return [steps, steps[1:] + steps[:1]]


def body(features, responses, basis, eigenvalues, reg_index, subject, alpha_table):
    groups = lax.axis_size("groups")
    totals, sends = gram(features, basis, groups)
    gots = [swap(send, "eig", 1) for send in sends]
    inv = inverse(alpha_table, reg_index, subject, eigenvalues, tuple(sends))
    last = (inv,)
    masks = orders(lax.axis_size("eig"))
    count = len(masks[0])
    for at in range(count + 1):
        for i in range(CHAINS):
            if at == count:
                sends[i] = add(totals[i], gots[i], last, True)
            else:
                totals[i], sends[i] = add(totals[i], gots[i], last)
                gots[i] = swap(sends[i], "eig", masks[i][at])
            last = (sends[i],)

    blocks = [sends]
    for bit in bits(groups):
        blocks = blocks + [[swap(piece, "groups", bit) for piece in block] for block in blocks]
    places = [(m, i) for m in range(groups) for i in range(CHAINS)]
    batches = [places[:CHAINS]] + [[place] for place in places[CHAINS:]]
    total = None
    for batch in batches:
        pieces = [blocks[m][i] for m, i in batch]
        total = share(batch, pieces, responses, total, inv if batch is batches[-1] else None)
    return weights(basis, total, swap(total, "eig", 1))


def solution(mesh):
    in_specs = (
        P(None, "eig"),
        P(None, "groups"),
        P("eig", None),
        P(),
        P("groups"),
        P("groups"),
        P(),
    )
    out_specs = P("eig", "groups")
    return jax.shard_map(body, mesh=mesh, in_specs=in_specs, out_specs=out_specs, check_vma=False)
```

time: 36.4 us -> 32 us (0.88)
  waiting for transfers between devices: 17.4 us -> 7.48 us
  starting transfers between devices: 9.33 us -> 17.4 us
  local copies, waits for them, and re-layouts: 3.43 us -> 0.02 us
  Pallas kernels: 5.66 us -> 6.88 us
    ppermute x6 -> x11, waiting for transfers between devices: 17.4 us -> 7.48 us  [swap(): lax.ppermute(value, axis, [(i, i ^ mask) for i in range(lax.axis_size(axi...]
    ppermute x6 -> x11, starting transfers between devices: 9.33 us -> 17.4 us  [swap(): lax.ppermute(value, axis, [(i, i ^ mask) for i in range(lax.axis_size(axi...]
    unnamed x14 -> x12, local copies, waits for them, and re-layouts: 3.43 us -> 0.02 us
    pallas_call x4 -> x13, Pallas kernels: 2.86 us -> 4.49 us  [the longest x1 2.75 us: gram(): pl.pallas_call(gram_kernel, in_specs=[HBM, HBM], out_specs=[VMEM] * len(o...]
    pallas_call x1, Pallas kernels: 2.79 us -> 2.39 us  [weights(): pl.pallas_call(weights_kernel, in_specs=[VMEM, VMEM, VMEM], out_specs=HBM...]
  transfers between devices with their start and end apart: 6 -> 11, of which waited for: 6 -> 5; matrix products, arithmetic and copies ran while one was open for 0% -> 0% of each run, Pallas kernels for 3% -> 5%
where the time goes in v3:
time: 32 us; the launch traced here: 31.8 us
  starting transfers between devices  17.4 us (54%)
  waiting for transfers between devices  7.48 us (23%)
  Pallas kernels  6.88 us (22%)
    ppermute x11, starting transfers between devices, swap(): lax.ppermute(value, axis, [(i, i ^ mask) for i in range(lax.axis_size(axi...  17.4 us
    ppermute x11, waiting for transfers between devices, swap(): lax.ppermute(value, axis, [(i, i ^ mask) for i in range(lax.axis_size(axi...  7.48 us
    pallas_call x1, Pallas kernels, gram(): pl.pallas_call(gram_kernel, in_specs=[HBM, HBM], out_specs=[VMEM] * len(o...  2.75 us
    pallas_call x1, Pallas kernels, weights(): pl.pallas_call(weights_kernel, in_specs=[VMEM, VMEM, VMEM], out_specs=HBM...  2.39 us
    pallas_call x3, Pallas kernels, share(): pl.pallas_call(functools.partial(share_kernel, places, before is not None...  0.83 us
    pallas_call x1, Pallas kernels, inverse(): pl.pallas_call(inverse_kernel, in_specs=[SMEM, VMEM, VMEM, VMEM] + [ANY]...  0.76 us
  transfers between devices with their start and end apart: 11, of which 5 were waited for; matrix products, arithmetic and copies ran while one was open for 0% of the time, Pallas kernels for 5%

profile of v3, /device:TPU:0, one launch (start us, length us, event | category | flops | bytes accessed | tf_op | source)
XLA Modules:
  0.0 31.8 jit_solution(1167383949591582265)
XLA Ops:
  0.0 0.0 copy-start.2
  0.0 0.0 copy-start.4
  0.0 0.0 copy-start.3
  0.0 0.0 copy-start.5
  0.0 0.0 copy-start
  0.0 2.8 %gram.1 = (f32[256,128]{1,0:T(8,128)S(1)}, f32[256,128]{1,0:T(8,128)S(1)}, bf16[256,128]{1,0:T(8,128)(2,1)S(1)}, bf16[256,128]{1,0:T(8,128)(2,1)S(1)}) custom-call(bf16[1024,2048]{1,0:T(8,128)(2,1)} %f_hbm.1, bf16[2048,256]{1,0:T(8,128)(2,1)} %b_ref.1), custom_call_target="tpu_custom_call" | custom-call | flops 536870912 | bytes 3145728 | tf_op jit(solution)/shard_map/gram/pallas_call | solution.py:79
  2.8 0.5 %collective-permute-start.1 = (bf16[256,128]{1,0:T(8,128)(2,1)S(1)}, bf16[256,128]{1,0:T(8,128)(2,1)S(1)}, u32[]{:S(2)}, u32[]{:S(2)}) collective-permute-start(bf16[256,128]{1,0:T(8,128)(2,1)S(1)} %get-tuple-element.24.refs_0_), channel_id=1, source_target_pairs={{0,1},{1,0},{2,3},{3,2},{4,5},{5,4},{6,7},{7,6},{8,9},{9,8},{10,11... | collective-permute-start | bytes 196616 | tf_op jit(solution)/shard_map/ppermute | solution.py:229
  3.3 0.1 collective-permute-start
  3.4 0.0 copy-done.2
  3.4 0.0 copy-done.4
  3.4 0.0 copy-done.3
  3.4 0.0 copy-done.5
  3.4 0.8 %inverse.1.refs_0_.refs_3_ = f32[128,1024]{1,0:T(8,128)S(1)} custom-call(f32[8,16]{1,0:T(8,128)S(1)} %copy-done.2, s32[1,1024]{1,0:T(1,128)S(1)} %bitcast.3, s32[1,1024]{1,0:T(1,128)S(1)} %bitcast.4, f32[1,256]{1,0:T(1,128)S(1)} %bitcast.5, bf16[256,128]{1,0:T(8,128)(2,1)S(1)} %get-tuple-element.24.refs_0_, bf16[256,128]{1,0:T(8,128)(2,1)S(1)} %get-tuple-element.22.refs_1_), custom_call_target="tpu_custom_call" | custom-call | flops 1048576 | bytes 262144 | tf_op jit(solution)/shard_map/inverse/pallas_call | solution.py:120
  4.2 0.0 collective-permute-done.1.got_ref
  4.2 3.0 %collective-permute-start.3 = (bf16[256,128]{1,0:T(8,128)(2,1)S(1)}, bf16[256,128]{1,0:T(8,128)(2,1)S(1)}, u32[]{:S(2)}, u32[]{:S(2)}) collective-permute-start(bf16[256,128]{1,0:T(8,128)(2,1)S(1)} %get-tuple-element.25.refs_0_), channel_id=1, source_target_pairs={{0,2},{1,3},{2,0},{3,1},{4,6},{5,7},{6,4},{7,5},{8,10},{9,11},{10,... | collective-permute-start | bytes 196616 | tf_op jit(solution)/shard_map/ppermute | solution.py:229
  7.2 0.0 collective-permute-done.got_ref
  7.2 1.6 %collective-permute-start.2 = (bf16[256,128]{1,0:T(8,128)(2,1)S(1)}, bf16[256,128]{1,0:T(8,128)(2,1)S(1)}, u32[]{:S(2)}, u32[]{:S(2)}) collective-permute-start(bf16[256,128]{1,0:T(8,128)(2,1)S(1)} %get-tuple-element.27.refs_0_), channel_id=1, source_target_pairs={{0,4},{1,5},{2,6},{3,7},{4,0},{5,1},{6,2},{7,3},{8,12},{9,13},{10,... | collective-permute-start | bytes 196616 | tf_op jit(solution)/shard_map/ppermute | solution.py:229
  8.9 0.7 %collective-permute-done.3.got_ref = bf16[256,128]{1,0:T(8,128)(2,1)S(1)} collective-permute-done((bf16[256,128]{1,0:T(8,128)(2,1)S(1)}, bf16[256,128]{1,0:T(8,128)(2,1)S(1)}, u32[]{:S(2)}, u32[]{:S(2)}) %collective-permute-start.3) | collective-permute-done | bytes 65568 | tf_op jit(solution)/shard_map/ppermute | solution.py:229
  9.6 2.0 %collective-permute-start.5 = (bf16[256,128]{1,0:T(8,128)(2,1)S(1)}, bf16[256,128]{1,0:T(8,128)(2,1)S(1)}, u32[]{:S(2)}, u32[]{:S(2)}) collective-permute-start(bf16[256,128]{1,0:T(8,128)(2,1)S(1)} %get-tuple-element.29.refs_0_), channel_id=1, source_target_pairs={{0,4},{1,5},{2,6},{3,7},{4,0},{5,1},{6,2},{7,3},{8,12},{9,13},{10,... | collective-permute-start | bytes 196616 | tf_op jit(solution)/shard_map/ppermute | solution.py:229
  11.6 0.0 collective-permute-done.2.got_ref
  11.7 2.7 %collective-permute-start.4 = (bf16[256,128]{1,0:T(8,128)(2,1)S(1)}, bf16[256,128]{1,0:T(8,128)(2,1)S(1)}, u32[]{:S(2)}, u32[]{:S(2)}) collective-permute-start(bf16[256,128]{1,0:T(8,128)(2,1)S(1)} %get-tuple-element.31.refs_0_), channel_id=1, source_target_pairs={{0,8},{1,9},{2,10},{3,11},{4,12},{5,13},{6,14},{7,15},{8,0},{9,1},... | collective-permute-start | bytes 196616 | tf_op jit(solution)/shard_map/ppermute | solution.py:229
  14.3 0.0 collective-permute-done.5.got_ref
  14.3 2.7 %collective-permute-start.7 = (bf16[256,128]{1,0:T(8,128)(2,1)S(1)}, bf16[256,128]{1,0:T(8,128)(2,1)S(1)}, u32[]{:S(2)}, u32[]{:S(2)}) collective-permute-start(bf16[256,128]{1,0:T(8,128)(2,1)S(1)} %get-tuple-element.33.refs_0_), channel_id=1, source_target_pairs={{0,8},{1,9},{2,10},{3,11},{4,12},{5,13},{6,14},{7,15},{8,0},{9,1},... | collective-permute-start | bytes 196616 | tf_op jit(solution)/shard_map/ppermute | solution.py:229
  17.0 1.9 %collective-permute-done.4.got_ref = bf16[256,128]{1,0:T(8,128)(2,1)S(1)} collective-permute-done((bf16[256,128]{1,0:T(8,128)(2,1)S(1)}, bf16[256,128]{1,0:T(8,128)(2,1)S(1)}, u32[]{:S(2)}, u32[]{:S(2)}) %collective-permute-start.4) | collective-permute-done | bytes 65568 | tf_op jit(solution)/shard_map/ppermute | solution.py:229
  18.9 1.6 %collective-permute-start.6 = (bf16[256,128]{1,0:T(8,128)(2,1)S(1)}, bf16[256,128]{1,0:T(8,128)(2,1)S(1)}, u32[]{:S(2)}, u32[]{:S(2)}) collective-permute-start(bf16[256,128]{1,0:T(8,128)(2,1)S(1)} %get-tuple-element.35.refs_0_), channel_id=1, source_target_pairs={{0,2},{1,3},{2,0},{3,1},{4,6},{5,7},{6,4},{7,5},{8,10},{9,11},{10,... | collective-permute-start | bytes 196616 | tf_op jit(solution)/shard_map/ppermute | solution.py:229
  20.5 0.0 collective-permute-done.7.got_ref
  20.5 1.6 %collective-permute-start.9 = (bf16[256,128]{1,0:T(8,128)(2,1)S(1)}, bf16[256,128]{1,0:T(8,128)(2,1)S(1)}, u32[]{:S(2)}, u32[]{:S(2)}) collective-permute-start(bf16[256,128]{1,0:T(8,128)(2,1)S(1)} %add.14.refs_0_), channel_id=1, source_target_pairs={{0,16},{16,0},{1,17},{17,1},{2,18},{18,2},{3,19},{19,3},{4,20},{20... | collective-permute-start | bytes 196616 | tf_op jit(solution)/shard_map/ppermute | solution.py:229
  22.1 1.2 %collective-permute-done.6.got_ref = bf16[256,128]{1,0:T(8,128)(2,1)S(1)} collective-permute-done((bf16[256,128]{1,0:T(8,128)(2,1)S(1)}, bf16[256,128]{1,0:T(8,128)(2,1)S(1)}, u32[]{:S(2)}, u32[]{:S(2)}) %collective-permute-start.6) | collective-permute-done | bytes 65568 | tf_op jit(solution)/shard_map/ppermute | solution.py:229
  23.3 0.0 copy-start.1
  23.3 1.6 %collective-permute-start.8 = (bf16[256,128]{1,0:T(8,128)(2,1)S(1)}, bf16[256,128]{1,0:T(8,128)(2,1)S(1)}, u32[]{:S(2)}, u32[]{:S(2)}) collective-permute-start(bf16[256,128]{1,0:T(8,128)(2,1)S(1)} %add.15.refs_1_), channel_id=1, source_target_pairs={{0,16},{16,0},{1,17},{17,1},{2,18},{18,2},{3,19},{19,3},{4,20},{20... | collective-permute-start | bytes 196616 | tf_op jit(solution)/shard_map/ppermute | solution.py:229
  24.8 0.0 copy-done
  24.8 0.3 %share.3.refs_2_ = f32[128,1024]{1,0:T(8,128)S(1)} custom-call(bf16[256,128]{1,0:T(8,128)(2,1)S(1)} %add.14.refs_0_, bf16[256,128]{1,0:T(8,128)(2,1)S(1)} %add.15.refs_1_, bf16[1024,1024]{1,0:T(8,128)(2,1)S(1)} %copy-done), custom_call_target="tpu_custom_call" | custom-call | flops 134217728 | bytes 524288 | tf_op jit(solution)/shard_map/share/pallas_call | solution.py:178
  25.2 0.0 collective-permute-done.9.refs_0_
  25.2 0.3 share.4.refs_2_
  25.4 2.2 %collective-permute-done.8.refs_0_ = bf16[256,128]{1,0:T(8,128)(2,1)S(1)} collective-permute-done((bf16[256,128]{1,0:T(8,128)(2,1)S(1)}, bf16[256,128]{1,0:T(8,128)(2,1)S(1)}, u32[]{:S(2)}, u32[]{:S(2)}) %collective-permute-start.8) | collective-permute-done | bytes 65568 | tf_op jit(solution)/shard_map/ppermute | solution.py:229
  27.6 0.3 share.5.own_ref
  27.9 0.1 collective-permute-start.10
  27.9 1.5 %collective-permute-done.10.got_ref = bf16[128,1024]{1,0:T(8,128)(2,1)S(1)} collective-permute-done((bf16[128,1024]{1,0:T(8,128)(2,1)S(1)}, bf16[128,1024]{1,0:T(8,128)(2,1)S(1)}, u32[]{:S(2)}, u32[]{:S(2)}) %collective-permute-start.10) | collective-permute-done | bytes 262176 | tf_op jit(solution)/shard_map/ppermute | solution.py:229
  29.5 0.0 copy-done.1
  29.5 2.4 %weights.1 = bf16[2048,1024]{1,0:T(8,128)(2,1)} custom-call(bf16[2048,256]{1,0:T(8,128)(2,1)S(1)} %copy-done.1, bf16[128,1024]{1,0:T(8,128)(2,1)S(1)} %share.5.own_ref, bf16[128,1024]{1,0:T(8,128)(2,1)S(1)} %collective-permute-done.10.got_ref), custom_call_target="tpu_custom_call" | custom-call | flops 1073741824 | bytes 4194304 | tf_op jit(solution)/shard_map/weights/pallas_call | solution.py:212
  (8 shorter events, 0.1 us)
Async XLA Ops:
  0.0 3.4 %copy-start.2 = (f32[8,16]{1,0:T(8,128)S(1)}, f32[8,16]{1,0:T(8,128)}, u32[]{:S(2)}) copy-start(f32[8,16]{1,0:T(8,128)} %table_ref.1) | copy-start | bytes 1540
  0.0 3.4 %copy-start.4 = (s32[1024]{0:T(1024)S(1)}, s32[1024]{0:T(1024)}, u32[]{:S(2)}) copy-start(s32[1024]{0:T(1024)} %param.12) | copy-start | bytes 12292
  0.0 3.4 %copy-start.3 = (s32[1024]{0:T(1024)S(1)}, s32[1024]{0:T(1024)}, u32[]{:S(2)}) copy-start(s32[1024]{0:T(1024)} %param.11) | copy-start | bytes 12292
  0.0 3.4 %copy-start.5 = (f32[256]{0:T(256)S(1)}, f32[256]{0:T(256)}, u32[]{:S(2)}) copy-start(f32[256]{0:T(256)} %param.10) | copy-start | bytes 3076
  0.0 24.8 %copy-start = (bf16[1024,1024]{1,0:T(8,128)(2,1)S(1)}, bf16[1024,1024]{1,0:T(8,128)(2,1)}, u32[]{:S(2)}) copy-start(bf16[1024,1024]{1,0:T(8,128)(2,1)} %refs_1_.3) | copy-start | bytes 6291460
  2.8 1.4 %collective-permute-start.1 = (bf16[256,128]{1,0:T(8,128)(2,1)S(1)}, bf16[256,128]{1,0:T(8,128)(2,1)S(1)}, u32[]{:S(2)}, u32[]{:S(2)}) collective-permute-start(bf16[256,128]{1,0:T(8,128)(2,1)S(1)} %get-tuple-element.24.refs_0_), channel_id=1, source_target_pairs={{0,1},{1,0},{2,3},{3,2},{4,5},{5,4},{6,7},{7,6},{8,9},{9,8},{10,11... | collective-permute-start | bytes 196616 | tf_op jit(solution)/shard_map/ppermute | solution.py:229
  3.3 3.9 %collective-permute-start = (bf16[256,128]{1,0:T(8,128)(2,1)S(1)}, bf16[256,128]{1,0:T(8,128)(2,1)S(1)}, u32[]{:S(2)}, u32[]{:S(2)}) collective-permute-start(bf16[256,128]{1,0:T(8,128)(2,1)S(1)} %get-tuple-element.22.refs_1_), channel_id=1, source_target_pairs={{0,1},{1,0},{2,3},{3,2},{4,5},{5,4},{6,7},{7,6},{8,9},{9,8},{10,11... | collective-permute-start | bytes 196616 | tf_op jit(solution)/shard_map/ppermute | solution.py:229
  4.2 5.3 %collective-permute-start.3 = (bf16[256,128]{1,0:T(8,128)(2,1)S(1)}, bf16[256,128]{1,0:T(8,128)(2,1)S(1)}, u32[]{:S(2)}, u32[]{:S(2)}) collective-permute-start(bf16[256,128]{1,0:T(8,128)(2,1)S(1)} %get-tuple-element.25.refs_0_), channel_id=1, source_target_pairs={{0,2},{1,3},{2,0},{3,1},{4,6},{5,7},{6,4},{7,5},{8,10},{9,11},{10,... | collective-permute-start | bytes 196616 | tf_op jit(solution)/shard_map/ppermute | solution.py:229
  7.2 4.4 %collective-permute-start.2 = (bf16[256,128]{1,0:T(8,128)(2,1)S(1)}, bf16[256,128]{1,0:T(8,128)(2,1)S(1)}, u32[]{:S(2)}, u32[]{:S(2)}) collective-permute-start(bf16[256,128]{1,0:T(8,128)(2,1)S(1)} %get-tuple-element.27.refs_0_), channel_id=1, source_target_pairs={{0,4},{1,5},{2,6},{3,7},{4,0},{5,1},{6,2},{7,3},{8,12},{9,13},{10,... | collective-permute-start | bytes 196616 | tf_op jit(solution)/shard_map/ppermute | solution.py:229
  9.6 4.7 %collective-permute-start.5 = (bf16[256,128]{1,0:T(8,128)(2,1)S(1)}, bf16[256,128]{1,0:T(8,128)(2,1)S(1)}, u32[]{:S(2)}, u32[]{:S(2)}) collective-permute-start(bf16[256,128]{1,0:T(8,128)(2,1)S(1)} %get-tuple-element.29.refs_0_), channel_id=1, source_target_pairs={{0,4},{1,5},{2,6},{3,7},{4,0},{5,1},{6,2},{7,3},{8,12},{9,13},{10,... | collective-permute-start | bytes 196616 | tf_op jit(solution)/shard_map/ppermute | solution.py:229
  11.7 7.2 %collective-permute-start.4 = (bf16[256,128]{1,0:T(8,128)(2,1)S(1)}, bf16[256,128]{1,0:T(8,128)(2,1)S(1)}, u32[]{:S(2)}, u32[]{:S(2)}) collective-permute-start(bf16[256,128]{1,0:T(8,128)(2,1)S(1)} %get-tuple-element.31.refs_0_), channel_id=1, source_target_pairs={{0,8},{1,9},{2,10},{3,11},{4,12},{5,13},{6,14},{7,15},{8,0},{9,1},... | collective-permute-start | bytes 196616 | tf_op jit(solution)/shard_map/ppermute | solution.py:229
  14.3 6.2 %collective-permute-start.7 = (bf16[256,128]{1,0:T(8,128)(2,1)S(1)}, bf16[256,128]{1,0:T(8,128)(2,1)S(1)}, u32[]{:S(2)}, u32[]{:S(2)}) collective-permute-start(bf16[256,128]{1,0:T(8,128)(2,1)S(1)} %get-tuple-element.33.refs_0_), channel_id=1, source_target_pairs={{0,8},{1,9},{2,10},{3,11},{4,12},{5,13},{6,14},{7,15},{8,0},{9,1},... | collective-permute-start | bytes 196616 | tf_op jit(solution)/shard_map/ppermute | solution.py:229
  18.9 4.3 %collective-permute-start.6 = (bf16[256,128]{1,0:T(8,128)(2,1)S(1)}, bf16[256,128]{1,0:T(8,128)(2,1)S(1)}, u32[]{:S(2)}, u32[]{:S(2)}) collective-permute-start(bf16[256,128]{1,0:T(8,128)(2,1)S(1)} %get-tuple-element.35.refs_0_), channel_id=1, source_target_pairs={{0,2},{1,3},{2,0},{3,1},{4,6},{5,7},{6,4},{7,5},{8,10},{9,11},{10,... | collective-permute-start | bytes 196616 | tf_op jit(solution)/shard_map/ppermute | solution.py:229
  20.5 4.7 %collective-permute-start.9 = (bf16[256,128]{1,0:T(8,128)(2,1)S(1)}, bf16[256,128]{1,0:T(8,128)(2,1)S(1)}, u32[]{:S(2)}, u32[]{:S(2)}) collective-permute-start(bf16[256,128]{1,0:T(8,128)(2,1)S(1)} %add.14.refs_0_), channel_id=1, source_target_pairs={{0,16},{16,0},{1,17},{17,1},{2,18},{18,2},{3,19},{19,3},{4,20},{20... | collective-permute-start | bytes 196616 | tf_op jit(solution)/shard_map/ppermute | solution.py:229
  23.3 6.2 %copy-start.1 = (bf16[2048,256]{1,0:T(8,128)(2,1)S(1)}, bf16[2048,256]{1,0:T(8,128)(2,1)}, u32[]{:S(2)}) copy-start(bf16[2048,256]{1,0:T(8,128)(2,1)} %b_ref.1) | copy-start | bytes 3145732
  23.3 4.3 %collective-permute-start.8 = (bf16[256,128]{1,0:T(8,128)(2,1)S(1)}, bf16[256,128]{1,0:T(8,128)(2,1)S(1)}, u32[]{:S(2)}, u32[]{:S(2)}) collective-permute-start(bf16[256,128]{1,0:T(8,128)(2,1)S(1)} %add.15.refs_1_), channel_id=1, source_target_pairs={{0,16},{16,0},{1,17},{17,1},{2,18},{18,2},{3,19},{19,3},{4,20},{20... | collective-permute-start | bytes 196616 | tf_op jit(solution)/shard_map/ppermute | solution.py:229
  27.9 1.6 %collective-permute-start.10 = (bf16[128,1024]{1,0:T(8,128)(2,1)S(1)}, bf16[128,1024]{1,0:T(8,128)(2,1)S(1)}, u32[]{:S(2)}, u32[]{:S(2)}) collective-permute-start(bf16[128,1024]{1,0:T(8,128)(2,1)S(1)} %share.5.own_ref), channel_id=1, source_target_pairs={{0,1},{1,0},{2,3},{3,2},{4,5},{5,4},{6,7},{7,6},{8,9},{9,8},{10,11... | collective-permute-start | bytes 786440 | tf_op jit(solution)/shard_map/ppermute | solution.py:229

commit v4 on v3

--- a/solution.py
+++ b/solution.py
@@ -11,6 +11,8 @@
 BF16 = jnp.bfloat16
 MIB = 1 << 20
 CHAINS = 2
+EIG_FLIP = 14
+GROUP_FLIP = 1
 ANY = pl.BlockSpec(memory_space=pl.ANY)
 HBM = pl.BlockSpec(memory_space=pltpu.HBM)
 VMEM = pl.BlockSpec(memory_space=pltpu.VMEM)
@@ -29,28 +31,44 @@
     return pltpu.with_memory_space_constraint(value, pltpu.HBM)
 
 
-def core_index():
-    return lax.axis_index("eig") & 1
-
-
-def gram_kernel(f_hbm, b_hbm, *refs):
-    *outs, f_ref, b_ref, f_sem, b_sem = refs
-    totals, sends = outs[:CHAINS], outs[CHAINS:]
+def parity(value, mask):
+    total = 0
+    while mask:
+        low = mask & -mask
+        total = total + (value // low) % 2
+        mask ^= low
+    return total % 2
+
+
+def half_index():
+    return (parity(lax.axis_index("eig"), EIG_FLIP | 1) + parity(lax.axis_index("groups"), GROUP_FLIP)) % 2
+
+
+def split_halves(total, kept_ref, sent_ref):
+    half = kept_ref.shape[1]
+    low, high = total[:, :half], total[:, half:]
+    first = half_index() == 0
+    kept_ref[...] = jnp.where(first, low, high)
+    sent_ref[...] = jnp.where(first, high, low).astype(BF16)
+
+
+def gram_first_kernel(f_hbm, b_hbm, kept_ref, sent_ref, rest_ref, b_ref, f_ref, f_sem, b_sem, rest_sem):
     rows, feats = f_ref.shape
-    half = b_ref.shape[1] // 2
     parts = f_sem.shape[0]
     chunk = feats // parts
-    first_row = pl.multiple_of(lax.axis_index("groups") * rows, rows)
+    more = rest_ref.shape[0]
+    start = pl.multiple_of(lax.axis_index("groups") * (rows + more), rows)
+    after = pl.multiple_of(start + rows, rows)
     copies = []
     for i in range(parts):
         cols = pl.ds(i * chunk, chunk)
         b_copy = pltpu.make_async_copy(b_hbm.at[cols], b_ref.at[cols], b_sem.at[i])
-        f_copy = pltpu.make_async_copy(
-            f_hbm.at[pl.ds(first_row, rows), cols], f_ref.at[:, cols], f_sem.at[i]
-        )
+        f_copy = pltpu.make_async_copy(f_hbm.at[pl.ds(start, rows), cols], f_ref.at[:, cols], f_sem.at[i])
         b_copy.start()
         f_copy.start()
         copies.append((b_copy, f_copy))
+    rest_copy = pltpu.make_async_copy(f_hbm.at[pl.ds(after, more)], rest_ref, rest_sem)
+    rest_copy.start()
     total = None
     for i, (b_copy, f_copy) in enumerate(copies):
         cols = pl.ds(i * chunk, chunk)
@@ -58,40 +76,57 @@
         f_copy.wait()
         term = jnp.dot(f_ref[:, cols], b_ref[cols, :], preferred_element_type=F32)
         total = term if total is None else total + term
-    low, high = total[:, :half], total[:, half:]
-    first = core_index() == 0
-    kept = jnp.where(first, low, high)
-    sent = jnp.where(first, high, low).astype(BF16)
-    size = rows // CHAINS
-    for i in range(CHAINS):
-        totals[i][...] = kept[i * size : (i + 1) * size]
-        sends[i][...] = sent[i * size : (i + 1) * size]
-
-
-def gram(features, basis, groups):
+    split_halves(total, kept_ref, sent_ref)
+    rest_copy.wait()
+
+
+def gram_rest_kernel(f_ref, b_ref, *refs):
+    kept_ref, sent_ref = refs[-2:]
+    split_halves(jnp.dot(f_ref[...], b_ref[...], preferred_element_type=F32), kept_ref, sent_ref)
+
+
+def gram_first(features, basis, groups):
     times, feats = features.shape
     k = basis.shape[1]
-    rows = times // groups
+    rows = times // groups // CHAINS
     parts = 2
-    out = [
-        jax.ShapeDtypeStruct((rows // CHAINS, k // 2), dtype) for dtype in (F32, BF16) for _ in range(CHAINS)
-    ]
-    result = pl.pallas_call(
-        gram_kernel,
+    return pl.pallas_call(
+        gram_first_kernel,
         in_specs=[HBM, HBM],
-        out_specs=[VMEM] * len(out),
-        out_shape=out,
+        out_specs=[VMEM] * 4,
+        out_shape=[
+            jax.ShapeDtypeStruct((rows, k // 2), F32),
+            jax.ShapeDtypeStruct((rows, k // 2), BF16),
+            jax.ShapeDtypeStruct((rows, feats), BF16),
+            jax.ShapeDtypeStruct((feats, k), BF16),
+        ],
         scratch_shapes=[
             pltpu.VMEM((rows, feats), BF16),
-            pltpu.VMEM((feats, k), BF16),
             pltpu.SemaphoreType.DMA((parts,)),
             pltpu.SemaphoreType.DMA((parts,)),
+            pltpu.SemaphoreType.DMA,
         ],
         compiler_params=params(12),
         cost_estimate=cost(2 * rows * feats * k, 2 * (rows + k) * feats),
-        name="gram",
+        name="gram_first",
     )(in_hbm(features), in_hbm(basis))
-    return list(result[:CHAINS]), list(result[CHAINS:])
+
+
+def gram_rest(rest, basis, after):
+    rows, feats = rest.shape
+    k = basis.shape[1]
+    return pl.pallas_call(
+        gram_rest_kernel,
+        in_specs=[VMEM, VMEM] + [ANY] * len(after),
+        out_specs=[VMEM] * 2,
+        out_shape=[
+            jax.ShapeDtypeStruct((rows, k // 2), F32),
+            jax.ShapeDtypeStruct((rows, k // 2), BF16),
+        ],
+        compiler_params=params(8),
+        cost_estimate=cost(2 * rows * feats * k, 2 * (rows + k) * feats),
+        name="gram_rest",
+    )(rest, basis, *after)
 
 
 def inverse_kernel(table_ref, reg_ref, subject_ref, eig_ref, *refs):
@@ -104,7 +139,7 @@
         for g in range(grid):
             alpha = jnp.where(code == s * grid + g, table_ref[s, g], alpha)
     side = min(k, 128)
-    first = core_index() == 0
+    first = half_index() == 0
     eig = jnp.where(first, eig_ref[:, :k], eig_ref[:, k:])
     shape = (side, side)
     diagonal = lax.broadcasted_iota(jnp.int32, shape, 0) == lax.broadcasted_iota(jnp.int32, shape, 1)
@@ -189,7 +224,7 @@
 def weights_kernel(b_ref, own_ref, got_ref, out_hbm, s_ref, out_ref, sems):
     parts = sems.shape[0]
     half = own_ref.shape[0]
-    first = core_index() == 0
+    first = half_index() == 0
     own, got = own_ref[...], got_ref[...]
     s_ref[:half, :] = jnp.where(first, own, got)
     s_ref[half:, :] = jnp.where(first, got, own)
@@ -225,8 +260,13 @@
     )(basis, own, got)
 
 
-def swap(value, axis, mask):
-    return lax.ppermute(value, axis, [(i, i ^ mask) for i in range(lax.axis_size(axis))])
+def swap(value, group_mask, eig_mask):
+    groups, size = lax.axis_size("groups"), lax.axis_size("eig")
+    eig_mask ^= (parity(eig_mask & ~1, EIG_FLIP) + parity(group_mask, GROUP_FLIP)) % 2
+    pairs = [
+        (g * size + e, (g ^ group_mask) * size + (e ^ eig_mask)) for g in range(groups) for e in range(size)
+    ]
+    return lax.ppermute(value, ("groups", "eig"), pairs)
 
 
 def bits(size):
@@ -243,31 +283,37 @@
 
 def body(features, responses, basis, eigenvalues, reg_index, subject, alpha_table):
     groups = lax.axis_size("groups")
-    totals, sends = gram(features, basis, groups)
-    gots = [swap(send, "eig", 1) for send in sends]
-    inv = inverse(alpha_table, reg_index, subject, eigenvalues, tuple(sends))
-    last = (inv,)
+    total, send, rest, panel = gram_first(features, basis, groups)
+    totals, gots = [total], [swap(send, 0, 1)]
+    total, send = gram_rest(rest, panel, (send,))
+    totals.append(total)
+    gots.append(swap(send, 0, 1))
+    sends = [None] * CHAINS
+    last = (send,)
     masks = orders(lax.axis_size("eig"))
     count = len(masks[0])
     for at in range(count + 1):
+        if at == count:
+            inv = inverse(alpha_table, reg_index, subject, eigenvalues, last)
+            last = (inv,)
         for i in range(CHAINS):
             if at == count:
                 sends[i] = add(totals[i], gots[i], last, True)
             else:
                 totals[i], sends[i] = add(totals[i], gots[i], last)
-                gots[i] = swap(sends[i], "eig", masks[i][at])
+                gots[i] = swap(sends[i], 0, masks[i][at])
             last = (sends[i],)
 
     blocks = [sends]
     for bit in bits(groups):
-        blocks = blocks + [[swap(piece, "groups", bit) for piece in block] for block in blocks]
+        blocks = blocks + [[swap(piece, bit, 0) for piece in block] for block in blocks]
     places = [(m, i) for m in range(groups) for i in range(CHAINS)]
     batches = [places[:CHAINS]] + [[place] for place in places[CHAINS:]]
     total = None
     for batch in batches:
         pieces = [blocks[m][i] for m, i in batch]
         total = share(batch, pieces, responses, total, inv if batch is batches[-1] else None)
-    return weights(basis, total, swap(total, "eig", 1))
+    return weights(panel, total, swap(total, 0, 1))
 
 
 def solution(mesh):

time: 32 us -> 30 us (0.938)
  waiting for transfers between devices: 7.48 us -> 6.05 us
  starting transfers between devices: 17.4 us -> 16.9 us
    ppermute x11, waiting for transfers between devices: 7.48 us -> 6.05 us  [swap(): return lax.ppermute(value, ('groups', 'eig'), pairs)]
    ppermute x11, starting transfers between devices: 17.4 us -> 16.9 us  [swap(): return lax.ppermute(value, ('groups', 'eig'), pairs)]
    pallas_call x1 -> x2, Pallas kernels: 2.75 us -> 2.59 us  [the longest x1 2.15 us: gram_first(): pl.pallas_call(gram_first_kernel, in_specs=[HBM, HBM], out_specs=[VMEM] *...]
  transfers between devices with their start and end apart: 11 -> 11, of which waited for: 5 -> 8; matrix products, arithmetic and copies ran while one was open for 0% -> 0% of each run, Pallas kernels for 5% -> 7%
where the time goes in v4:
time: 30 us; the launch traced here: 29.9 us
  starting transfers between devices  16.9 us (56%)
  Pallas kernels  6.76 us (23%)
  waiting for transfers between devices  6.05 us (20%)
    ppermute x11, starting transfers between devices, swap(): return lax.ppermute(value, ('groups', 'eig'), pairs)  16.9 us
    ppermute x11, waiting for transfers between devices, swap(): return lax.ppermute(value, ('groups', 'eig'), pairs)  6.05 us
    pallas_call x1, Pallas kernels, weights(): pl.pallas_call(weights_kernel, in_specs=[VMEM, VMEM, VMEM], out_specs=HBM...  2.41 us
    pallas_call x1, Pallas kernels, gram_first(): pl.pallas_call(gram_first_kernel, in_specs=[HBM, HBM], out_specs=[VMEM] *...  2.15 us
    pallas_call x3, Pallas kernels, share(): pl.pallas_call(functools.partial(share_kernel, places, before is not None...  0.83 us
    pallas_call x1, Pallas kernels, inverse(): pl.pallas_call(inverse_kernel, in_specs=[SMEM, VMEM, VMEM, VMEM] + [ANY]...  0.8 us
  transfers between devices with their start and end apart: 11, of which 8 were waited for; matrix products, arithmetic and copies ran while one was open for 0% of the time, Pallas kernels for 7%

profile of v4, /device:TPU:0, one launch (start us, length us, event | category | flops | bytes accessed | tf_op | source)
XLA Modules:
  0.0 29.9 jit_solution(13166715009398297414)
XLA Ops:
  0.0 0.0 copy-start.1
  0.0 0.0 copy-start.3
  0.0 0.0 copy-start.2
  0.0 0.0 copy-start.4
  0.0 0.0 copy-start
  0.0 2.2 %gram_first.1 = (f32[256,128]{1,0:T(8,128)S(1)}, bf16[256,128]{1,0:T(8,128)(2,1)S(1)}, bf16[256,2048]{1,0:T(8,128)(2,1)S(1)}, bf16[2048,256]{1,0:T(8,128)(2,1)S(1)}) custom-call(bf16[1024,2048]{1,0:T(8,128)(2,1)} %f_hbm.1, bf16[2048,256]{1,0:T(8,128)(2,1)} %b_hbm.1), custom_call_target="tpu_custom_call" | custom-call | flops 268435456 | bytes 2097152 | tf_op jit(solution)/shard_map/gram_first/pallas_call | solution.py:93
  2.2 0.5 %collective-permute-start.1 = (bf16[256,128]{1,0:T(8,128)(2,1)S(1)}, bf16[256,128]{1,0:T(8,128)(2,1)S(1)}, u32[]{:S(2)}, u32[]{:S(2)}) collective-permute-start(bf16[256,128]{1,0:T(8,128)(2,1)S(1)} %get-tuple-element.25.refs_0_), channel_id=1, source_target_pairs={{0,1},{1,0},{2,3},{3,2},{4,5},{5,4},{6,7},{7,6},{8,9},{9,8},{10,11... | collective-permute-start | bytes 196616 | tf_op jit(solution)/shard_map/ppermute | solution.py:269
  2.7 0.4 %gram_rest.1 = (f32[256,128]{1,0:T(8,128)S(1)}, bf16[256,128]{1,0:T(8,128)(2,1)S(1)}) custom-call(bf16[256,2048]{1,0:T(8,128)(2,1)S(1)} %get-tuple-element.24.f_ref, bf16[2048,256]{1,0:T(8,128)(2,1)S(1)} %get-tuple-element.23.b_ref, bf16[256,128]{1,0:T(8,128)(2,1)S(1)} %get-tuple-element.25.refs_0_), custom_call_target="tpu_custom_call" | custom-call | flops 268435456 | bytes 2097152 | tf_op jit(solution)/shard_map/gram_rest/pallas_call | solution.py:118
  3.2 0.1 collective-permute-start
  3.3 0.3 %collective-permute-done.1.got_ref = bf16[256,128]{1,0:T(8,128)(2,1)S(1)} collective-permute-done((bf16[256,128]{1,0:T(8,128)(2,1)S(1)}, bf16[256,128]{1,0:T(8,128)(2,1)S(1)}, u32[]{:S(2)}, u32[]{:S(2)}) %collective-permute-start.1) | collective-permute-done | bytes 65568 | tf_op jit(solution)/shard_map/ppermute | solution.py:269
  3.6 2.7 %collective-permute-start.3 = (bf16[256,128]{1,0:T(8,128)(2,1)S(1)}, bf16[256,128]{1,0:T(8,128)(2,1)S(1)}, u32[]{:S(2)}, u32[]{:S(2)}) collective-permute-start(bf16[256,128]{1,0:T(8,128)(2,1)S(1)} %get-tuple-element.29.refs_0_), channel_id=1, source_target_pairs={{0,3},{1,2},{2,1},{3,0},{4,7},{5,6},{6,5},{7,4},{8,11},{9,10},{10,... | collective-permute-start | bytes 196616 | tf_op jit(solution)/shard_map/ppermute | solution.py:269
  6.3 0.0 collective-permute-done.got_ref
  6.3 1.6 %collective-permute-start.2 = (bf16[256,128]{1,0:T(8,128)(2,1)S(1)}, bf16[256,128]{1,0:T(8,128)(2,1)S(1)}, u32[]{:S(2)}, u32[]{:S(2)}) collective-permute-start(bf16[256,128]{1,0:T(8,128)(2,1)S(1)} %get-tuple-element.31.refs_0_), channel_id=1, source_target_pairs={{0,5},{1,4},{2,7},{3,6},{4,1},{5,0},{6,3},{7,2},{8,13},{9,12},{10,... | collective-permute-start | bytes 196616 | tf_op jit(solution)/shard_map/ppermute | solution.py:269
  8.0 0.6 %collective-permute-done.3.got_ref = bf16[256,128]{1,0:T(8,128)(2,1)S(1)} collective-permute-done((bf16[256,128]{1,0:T(8,128)(2,1)S(1)}, bf16[256,128]{1,0:T(8,128)(2,1)S(1)}, u32[]{:S(2)}, u32[]{:S(2)}) %collective-permute-start.3) | collective-permute-done | bytes 65568 | tf_op jit(solution)/shard_map/ppermute | solution.py:269
  8.5 2.3 %collective-permute-start.5 = (bf16[256,128]{1,0:T(8,128)(2,1)S(1)}, bf16[256,128]{1,0:T(8,128)(2,1)S(1)}, u32[]{:S(2)}, u32[]{:S(2)}) collective-permute-start(bf16[256,128]{1,0:T(8,128)(2,1)S(1)} %get-tuple-element.33.refs_0_), channel_id=1, source_target_pairs={{0,5},{1,4},{2,7},{3,6},{4,1},{5,0},{6,3},{7,2},{8,13},{9,12},{10,... | collective-permute-start | bytes 196616 | tf_op jit(solution)/shard_map/ppermute | solution.py:269
  10.8 0.0 collective-permute-done.2.got_ref
  10.8 2.3 %collective-permute-start.4 = (bf16[256,128]{1,0:T(8,128)(2,1)S(1)}, bf16[256,128]{1,0:T(8,128)(2,1)S(1)}, u32[]{:S(2)}, u32[]{:S(2)}) collective-permute-start(bf16[256,128]{1,0:T(8,128)(2,1)S(1)} %get-tuple-element.35.refs_0_), channel_id=1, source_target_pairs={{0,9},{1,8},{2,11},{3,10},{4,13},{5,12},{6,15},{7,14},{8,1},{9,0},... | collective-permute-start | bytes 196616 | tf_op jit(solution)/shard_map/ppermute | solution.py:269
  13.2 0.1 collective-permute-done.5.got_ref
  13.3 2.8 %collective-permute-start.7 = (bf16[256,128]{1,0:T(8,128)(2,1)S(1)}, bf16[256,128]{1,0:T(8,128)(2,1)S(1)}, u32[]{:S(2)}, u32[]{:S(2)}) collective-permute-start(bf16[256,128]{1,0:T(8,128)(2,1)S(1)} %get-tuple-element.37.refs_0_), channel_id=1, source_target_pairs={{0,9},{1,8},{2,11},{3,10},{4,13},{5,12},{6,15},{7,14},{8,1},{9,0},... | collective-permute-start | bytes 196616 | tf_op jit(solution)/shard_map/ppermute | solution.py:269
  16.0 1.3 %collective-permute-done.4.got_ref = bf16[256,128]{1,0:T(8,128)(2,1)S(1)} collective-permute-done((bf16[256,128]{1,0:T(8,128)(2,1)S(1)}, bf16[256,128]{1,0:T(8,128)(2,1)S(1)}, u32[]{:S(2)}, u32[]{:S(2)}) %collective-permute-start.4) | collective-permute-done | bytes 65568 | tf_op jit(solution)/shard_map/ppermute | solution.py:269
  17.4 1.6 %collective-permute-start.6 = (bf16[256,128]{1,0:T(8,128)(2,1)S(1)}, bf16[256,128]{1,0:T(8,128)(2,1)S(1)}, u32[]{:S(2)}, u32[]{:S(2)}) collective-permute-start(bf16[256,128]{1,0:T(8,128)(2,1)S(1)} %get-tuple-element.39.refs_0_), channel_id=1, source_target_pairs={{0,3},{1,2},{2,1},{3,0},{4,7},{5,6},{6,5},{7,4},{8,11},{9,10},{10,... | collective-permute-start | bytes 196616 | tf_op jit(solution)/shard_map/ppermute | solution.py:269
  19.0 0.0 copy-done.1
  19.0 0.0 copy-done.3
  19.0 0.0 copy-done.2
  19.0 0.0 copy-done.4
  19.0 0.8 %inverse.1.refs_0_.refs_3_ = f32[128,1024]{1,0:T(8,128)S(1)} custom-call(f32[8,16]{1,0:T(8,128)S(1)} %copy-done.1, s32[1,1024]{1,0:T(1,128)S(1)} %bitcast.3, s32[1,1024]{1,0:T(1,128)S(1)} %bitcast.4, f32[1,256]{1,0:T(1,128)S(1)} %bitcast.5, bf16[256,128]{1,0:T(8,128)(2,1)S(1)} %get-tuple-element.39.refs_0_), custom_call_target="tpu_custom_call" | custom-call | flops 1048576 | bytes 262144 | tf_op jit(solution)/shard_map/inverse/pallas_call | solution.py:155
  19.8 0.4 %collective-permute-done.7.got_ref = bf16[256,128]{1,0:T(8,128)(2,1)S(1)} collective-permute-done((bf16[256,128]{1,0:T(8,128)(2,1)S(1)}, bf16[256,128]{1,0:T(8,128)(2,1)S(1)}, u32[]{:S(2)}, u32[]{:S(2)}) %collective-permute-start.7) | collective-permute-done | bytes 65568 | tf_op jit(solution)/shard_map/ppermute | solution.py:269
  20.2 1.3 %collective-permute-start.9 = (bf16[256,128]{1,0:T(8,128)(2,1)S(1)}, bf16[256,128]{1,0:T(8,128)(2,1)S(1)}, u32[]{:S(2)}, u32[]{:S(2)}) collective-permute-start(bf16[256,128]{1,0:T(8,128)(2,1)S(1)} %add.14.refs_0_), channel_id=1, source_target_pairs={{0,17},{1,16},{2,19},{3,18},{4,21},{5,20},{6,23},{7,22},{8,25},{9,... | collective-permute-start | bytes 196616 | tf_op jit(solution)/shard_map/ppermute | solution.py:269
  21.5 0.0 collective-permute-done.6.got_ref
  21.5 1.4 %collective-permute-start.8 = (bf16[256,128]{1,0:T(8,128)(2,1)S(1)}, bf16[256,128]{1,0:T(8,128)(2,1)S(1)}, u32[]{:S(2)}, u32[]{:S(2)}) collective-permute-start(bf16[256,128]{1,0:T(8,128)(2,1)S(1)} %add.15.refs_1_), channel_id=1, source_target_pairs={{0,17},{1,16},{2,19},{3,18},{4,21},{5,20},{6,23},{7,22},{8,25},{9,... | collective-permute-start | bytes 196616 | tf_op jit(solution)/shard_map/ppermute | solution.py:269
  22.9 0.0 copy-done
  22.9 0.3 %share.3.refs_2_ = f32[128,1024]{1,0:T(8,128)S(1)} custom-call(bf16[256,128]{1,0:T(8,128)(2,1)S(1)} %add.14.refs_0_, bf16[256,128]{1,0:T(8,128)(2,1)S(1)} %add.15.refs_1_, bf16[1024,1024]{1,0:T(8,128)(2,1)S(1)} %copy-done), custom_call_target="tpu_custom_call" | custom-call | flops 134217728 | bytes 524288 | tf_op jit(solution)/shard_map/share/pallas_call | solution.py:213
  23.3 1.1 %collective-permute-done.9.refs_0_ = bf16[256,128]{1,0:T(8,128)(2,1)S(1)} collective-permute-done((bf16[256,128]{1,0:T(8,128)(2,1)S(1)}, bf16[256,128]{1,0:T(8,128)(2,1)S(1)}, u32[]{:S(2)}, u32[]{:S(2)}) %collective-permute-start.9) | collective-permute-done | bytes 65568 | tf_op jit(solution)/shard_map/ppermute | solution.py:269
  24.4 0.3 share.4.refs_2_
  24.6 1.0 %collective-permute-done.8.refs_0_ = bf16[256,128]{1,0:T(8,128)(2,1)S(1)} collective-permute-done((bf16[256,128]{1,0:T(8,128)(2,1)S(1)}, bf16[256,128]{1,0:T(8,128)(2,1)S(1)}, u32[]{:S(2)}, u32[]{:S(2)}) %collective-permute-start.8) | collective-permute-done | bytes 65568 | tf_op jit(solution)/shard_map/ppermute | solution.py:269
  25.6 0.3 share.5.own_ref
  25.9 0.3 %collective-permute-start.10 = (bf16[128,1024]{1,0:T(8,128)(2,1)S(1)}, bf16[128,1024]{1,0:T(8,128)(2,1)S(1)}, u32[]{:S(2)}, u32[]{:S(2)}) collective-permute-start(bf16[128,1024]{1,0:T(8,128)(2,1)S(1)} %share.5.own_ref), channel_id=1, source_target_pairs={{0,1},{1,0},{2,3},{3,2},{4,5},{5,4},{6,7},{7,6},{8,9},{9,8},{10,11... | collective-permute-start | bytes 786440 | tf_op jit(solution)/shard_map/ppermute | solution.py:269
  26.2 1.3 %collective-permute-done.10.got_ref = bf16[128,1024]{1,0:T(8,128)(2,1)S(1)} collective-permute-done((bf16[128,1024]{1,0:T(8,128)(2,1)S(1)}, bf16[128,1024]{1,0:T(8,128)(2,1)S(1)}, u32[]{:S(2)}, u32[]{:S(2)}) %collective-permute-start.10) | collective-permute-done | bytes 262176 | tf_op jit(solution)/shard_map/ppermute | solution.py:269
  27.5 2.4 %weights.1 = bf16[2048,1024]{1,0:T(8,128)(2,1)} custom-call(bf16[2048,256]{1,0:T(8,128)(2,1)S(1)} %get-tuple-element.23.b_ref, bf16[128,1024]{1,0:T(8,128)(2,1)S(1)} %share.5.own_ref, bf16[128,1024]{1,0:T(8,128)(2,1)S(1)} %collective-permute-done.10.got_ref), custom_call_target="tpu_custom_call" | custom-call | flops 1073741824 | bytes 4194304 | tf_op jit(solution)/shard_map/weights/pallas_call | solution.py:247
  (8 shorter events, 0.1 us)
Async XLA Ops:
  0.0 19.0 %copy-start.1 = (f32[8,16]{1,0:T(8,128)S(1)}, f32[8,16]{1,0:T(8,128)}, u32[]{:S(2)}) copy-start(f32[8,16]{1,0:T(8,128)} %table_ref.1) | copy-start | bytes 1540
  0.0 19.0 %copy-start.3 = (s32[1024]{0:T(1024)S(1)}, s32[1024]{0:T(1024)}, u32[]{:S(2)}) copy-start(s32[1024]{0:T(1024)} %param.12) | copy-start | bytes 12292
  0.0 19.0 %copy-start.2 = (s32[1024]{0:T(1024)S(1)}, s32[1024]{0:T(1024)}, u32[]{:S(2)}) copy-start(s32[1024]{0:T(1024)} %param.11) | copy-start | bytes 12292
  0.0 19.0 %copy-start.4 = (f32[256]{0:T(256)S(1)}, f32[256]{0:T(256)}, u32[]{:S(2)}) copy-start(f32[256]{0:T(256)} %param.10) | copy-start | bytes 3076
  0.0 22.9 %copy-start = (bf16[1024,1024]{1,0:T(8,128)(2,1)S(1)}, bf16[1024,1024]{1,0:T(8,128)(2,1)}, u32[]{:S(2)}) copy-start(bf16[1024,1024]{1,0:T(8,128)(2,1)} %refs_1_.3) | copy-start | bytes 6291460
  2.2 1.4 %collective-permute-start.1 = (bf16[256,128]{1,0:T(8,128)(2,1)S(1)}, bf16[256,128]{1,0:T(8,128)(2,1)S(1)}, u32[]{:S(2)}, u32[]{:S(2)}) collective-permute-start(bf16[256,128]{1,0:T(8,128)(2,1)S(1)} %get-tuple-element.25.refs_0_), channel_id=1, source_target_pairs={{0,1},{1,0},{2,3},{3,2},{4,5},{5,4},{6,7},{7,6},{8,9},{9,8},{10,11... | collective-permute-start | bytes 196616 | tf_op jit(solution)/shard_map/ppermute | solution.py:269
  3.2 3.2 %collective-permute-start = (bf16[256,128]{1,0:T(8,128)(2,1)S(1)}, bf16[256,128]{1,0:T(8,128)(2,1)S(1)}, u32[]{:S(2)}, u32[]{:S(2)}) collective-permute-start(bf16[256,128]{1,0:T(8,128)(2,1)S(1)} %get-tuple-element.27.refs_0_), channel_id=1, source_target_pairs={{0,1},{1,0},{2,3},{3,2},{4,5},{5,4},{6,7},{7,6},{8,9},{9,8},{10,11... | collective-permute-start | bytes 196616 | tf_op jit(solution)/shard_map/ppermute | solution.py:269
  3.6 4.9 %collective-permute-start.3 = (bf16[256,128]{1,0:T(8,128)(2,1)S(1)}, bf16[256,128]{1,0:T(8,128)(2,1)S(1)}, u32[]{:S(2)}, u32[]{:S(2)}) collective-permute-start(bf16[256,128]{1,0:T(8,128)(2,1)S(1)} %get-tuple-element.29.refs_0_), channel_id=1, source_target_pairs={{0,3},{1,2},{2,1},{3,0},{4,7},{5,6},{6,5},{7,4},{8,11},{9,10},{10,... | collective-permute-start | bytes 196616 | tf_op jit(solution)/shard_map/ppermute | solution.py:269
  6.3 4.5 %collective-permute-start.2 = (bf16[256,128]{1,0:T(8,128)(2,1)S(1)}, bf16[256,128]{1,0:T(8,128)(2,1)S(1)}, u32[]{:S(2)}, u32[]{:S(2)}) collective-permute-start(bf16[256,128]{1,0:T(8,128)(2,1)S(1)} %get-tuple-element.31.refs_0_), channel_id=1, source_target_pairs={{0,5},{1,4},{2,7},{3,6},{4,1},{5,0},{6,3},{7,2},{8,13},{9,12},{10,... | collective-permute-start | bytes 196616 | tf_op jit(solution)/shard_map/ppermute | solution.py:269
  8.5 4.7 %collective-permute-start.5 = (bf16[256,128]{1,0:T(8,128)(2,1)S(1)}, bf16[256,128]{1,0:T(8,128)(2,1)S(1)}, u32[]{:S(2)}, u32[]{:S(2)}) collective-permute-start(bf16[256,128]{1,0:T(8,128)(2,1)S(1)} %get-tuple-element.33.refs_0_), channel_id=1, source_target_pairs={{0,5},{1,4},{2,7},{3,6},{4,1},{5,0},{6,3},{7,2},{8,13},{9,12},{10,... | collective-permute-start | bytes 196616 | tf_op jit(solution)/shard_map/ppermute | solution.py:269
  10.8 6.5 %collective-permute-start.4 = (bf16[256,128]{1,0:T(8,128)(2,1)S(1)}, bf16[256,128]{1,0:T(8,128)(2,1)S(1)}, u32[]{:S(2)}, u32[]{:S(2)}) collective-permute-start(bf16[256,128]{1,0:T(8,128)(2,1)S(1)} %get-tuple-element.35.refs_0_), channel_id=1, source_target_pairs={{0,9},{1,8},{2,11},{3,10},{4,13},{5,12},{6,15},{7,14},{8,1},{9,0},... | collective-permute-start | bytes 196616 | tf_op jit(solution)/shard_map/ppermute | solution.py:269
  13.3 6.9 %collective-permute-start.7 = (bf16[256,128]{1,0:T(8,128)(2,1)S(1)}, bf16[256,128]{1,0:T(8,128)(2,1)S(1)}, u32[]{:S(2)}, u32[]{:S(2)}) collective-permute-start(bf16[256,128]{1,0:T(8,128)(2,1)S(1)} %get-tuple-element.37.refs_0_), channel_id=1, source_target_pairs={{0,9},{1,8},{2,11},{3,10},{4,13},{5,12},{6,15},{7,14},{8,1},{9,0},... | collective-permute-start | bytes 196616 | tf_op jit(solution)/shard_map/ppermute | solution.py:269
  17.4 4.1 %collective-permute-start.6 = (bf16[256,128]{1,0:T(8,128)(2,1)S(1)}, bf16[256,128]{1,0:T(8,128)(2,1)S(1)}, u32[]{:S(2)}, u32[]{:S(2)}) collective-permute-start(bf16[256,128]{1,0:T(8,128)(2,1)S(1)} %get-tuple-element.39.refs_0_), channel_id=1, source_target_pairs={{0,3},{1,2},{2,1},{3,0},{4,7},{5,6},{6,5},{7,4},{8,11},{9,10},{10,... | collective-permute-start | bytes 196616 | tf_op jit(solution)/shard_map/ppermute | solution.py:269
  20.2 4.2 %collective-permute-start.9 = (bf16[256,128]{1,0:T(8,128)(2,1)S(1)}, bf16[256,128]{1,0:T(8,128)(2,1)S(1)}, u32[]{:S(2)}, u32[]{:S(2)}) collective-permute-start(bf16[256,128]{1,0:T(8,128)(2,1)S(1)} %add.14.refs_0_), channel_id=1, source_target_pairs={{0,17},{1,16},{2,19},{3,18},{4,21},{5,20},{6,23},{7,22},{8,25},{9,... | collective-permute-start | bytes 196616 | tf_op jit(solution)/shard_map/ppermute | solution.py:269
  21.5 4.1 %collective-permute-start.8 = (bf16[256,128]{1,0:T(8,128)(2,1)S(1)}, bf16[256,128]{1,0:T(8,128)(2,1)S(1)}, u32[]{:S(2)}, u32[]{:S(2)}) collective-permute-start(bf16[256,128]{1,0:T(8,128)(2,1)S(1)} %add.15.refs_1_), channel_id=1, source_target_pairs={{0,17},{1,16},{2,19},{3,18},{4,21},{5,20},{6,23},{7,22},{8,25},{9,... | collective-permute-start | bytes 196616 | tf_op jit(solution)/shard_map/ppermute | solution.py:269
  25.9 1.6 %collective-permute-start.10 = (bf16[128,1024]{1,0:T(8,128)(2,1)S(1)}, bf16[128,1024]{1,0:T(8,128)(2,1)S(1)}, u32[]{:S(2)}, u32[]{:S(2)}) collective-permute-start(bf16[128,1024]{1,0:T(8,128)(2,1)S(1)} %share.5.own_ref), channel_id=1, source_target_pairs={{0,1},{1,0},{2,3},{3,2},{4,5},{5,4},{6,7},{7,6},{8,9},{9,8},{10,11... | collective-permute-start | bytes 786440 | tf_op jit(solution)/shard_map/ppermute | solution.py:269

commit v5 on v4

--- a/solution.py
+++ b/solution.py
@@ -13,6 +13,7 @@
 CHAINS = 2
 EIG_FLIP = 14
 GROUP_FLIP = 1
+FIRST = 8
 ANY = pl.BlockSpec(memory_space=pl.ANY)
 HBM = pl.BlockSpec(memory_space=pltpu.HBM)
 VMEM = pl.BlockSpec(memory_space=pltpu.VMEM)
@@ -40,8 +41,17 @@
     return total % 2
 
 
+def half_of(group, eig):
+    return (parity(eig, EIG_FLIP | 1) + parity(group, GROUP_FLIP)) % 2
+
+
 def half_index():
-    return (parity(lax.axis_index("eig"), EIG_FLIP | 1) + parity(lax.axis_index("groups"), GROUP_FLIP)) % 2
+    return half_of(lax.axis_index("groups"), lax.axis_index("eig"))
+
+
+def chain_rows(times):
+    first = times * FIRST // 16
+    return first, times - first
 
 
 def split_halves(total, kept_ref, sent_ref):
@@ -57,8 +67,8 @@
     parts = f_sem.shape[0]
     chunk = feats // parts
     more = rest_ref.shape[0]
-    start = pl.multiple_of(lax.axis_index("groups") * (rows + more), rows)
-    after = pl.multiple_of(start + rows, rows)
+    start = pl.multiple_of(lax.axis_index("groups") * (rows + more), 16)
+    after = pl.multiple_of(start + rows, 16)
     copies = []
     for i in range(parts):
         cols = pl.ds(i * chunk, chunk)
@@ -88,7 +98,7 @@
 def gram_first(features, basis, groups):
     times, feats = features.shape
     k = basis.shape[1]
-    rows = times // groups // CHAINS
+    rows, more = chain_rows(times // groups)
     parts = 2
     return pl.pallas_call(
         gram_first_kernel,
@@ -97,7 +107,7 @@
         out_shape=[
             jax.ShapeDtypeStruct((rows, k // 2), F32),
             jax.ShapeDtypeStruct((rows, k // 2), BF16),
-            jax.ShapeDtypeStruct((rows, feats), BF16),
+            jax.ShapeDtypeStruct((more, feats), BF16),
             jax.ShapeDtypeStruct((feats, k), BF16),
         ],
         scratch_shapes=[
@@ -138,6 +148,7 @@
     for s in range(subjects):
         for g in range(grid):
             alpha = jnp.where(code == s * grid + g, table_ref[s, g], alpha)
+    alpha = alpha.reshape(1, alpha.size)
     side = min(k, 128)
     first = half_index() == 0
     eig = jnp.where(first, eig_ref[:, :k], eig_ref[:, k:])
@@ -160,7 +171,7 @@
         compiler_params=params(8),
         cost_estimate=cost(8 * k * vox, 2 * k * vox),
         name="inverse",
-    )(alpha_table, reg_index[None, :], subject[None, :], eigenvalues[None, :], *after)
+    )(alpha_table, reg_index.reshape(-1, 128), subject.reshape(-1, 128), eigenvalues[None, :], *after)
 
 
 def add_kernel(total_ref, got_ref, *refs):
@@ -193,10 +204,11 @@
     r_ref, out_ref = refs[n], refs[-1]
     rest = list(refs[n + 1 : -1])
     group = lax.axis_index("groups")
+    times = r_ref.shape[0] // lax.axis_size("groups")
     total = rest.pop(0)[...] if has_sum else None
     for (m, at), piece in zip(places, refs):
         rows = piece.shape[0]
-        start = pl.multiple_of(((group ^ m) * CHAINS + at) * rows, rows)
+        start = pl.multiple_of((group ^ m) * times + at, 16)
         term = lax.dot_general(
             piece[...], r_ref[pl.ds(start, rows), :], (((0,), (0,)), ((), ())), preferred_element_type=F32
         )
@@ -260,12 +272,14 @@
     )(basis, own, got)
 
 
-def swap(value, group_mask, eig_mask):
+def swap(value, group_mask, eig_masks):
     groups, size = lax.axis_size("groups"), lax.axis_size("eig")
-    eig_mask ^= (parity(eig_mask & ~1, EIG_FLIP) + parity(group_mask, GROUP_FLIP)) % 2
-    pairs = [
-        (g * size + e, (g ^ group_mask) * size + (e ^ eig_mask)) for g in range(groups) for e in range(size)
-    ]
+    pairs = []
+    for g in range(groups):
+        for e in range(size):
+            mask = eig_masks[half_of(g, e)]
+            mask ^= (parity(mask & ~1, EIG_FLIP) + parity(group_mask, GROUP_FLIP)) % 2
+            pairs.append((g * size + e, (g ^ group_mask) * size + (e ^ mask)))
     return lax.ppermute(value, ("groups", "eig"), pairs)
 
 
@@ -278,42 +292,42 @@
 
 def orders(size):
     steps = bits(size)[1:]
-    return [steps, steps[1:] + steps[:1]]
+    turn = [steps[i:] + steps[:i] for i in range(len(steps))]
+    return [[turn[0], turn[-1]], [turn[1 % len(steps)], turn[-1]]]
 
 
 def body(features, responses, basis, eigenvalues, reg_index, subject, alpha_table):
     groups = lax.axis_size("groups")
     total, send, rest, panel = gram_first(features, basis, groups)
-    totals, gots = [total], [swap(send, 0, 1)]
+    totals, gots = [total], [swap(send, 0, (1, 1))]
     total, send = gram_rest(rest, panel, (send,))
     totals.append(total)
-    gots.append(swap(send, 0, 1))
+    gots.append(swap(send, 0, (1, 1)))
     sends = [None] * CHAINS
     last = (send,)
     masks = orders(lax.axis_size("eig"))
-    count = len(masks[0])
+    count = len(masks[0][0])
     for at in range(count + 1):
-        if at == count:
-            inv = inverse(alpha_table, reg_index, subject, eigenvalues, last)
-            last = (inv,)
         for i in range(CHAINS):
             if at == count:
                 sends[i] = add(totals[i], gots[i], last, True)
             else:
                 totals[i], sends[i] = add(totals[i], gots[i], last)
-                gots[i] = swap(sends[i], 0, masks[i][at])
+                gots[i] = swap(sends[i], 0, [masks[i][half][at] for half in range(2)])
             last = (sends[i],)
 
+    inv = inverse(alpha_table, reg_index, subject, eigenvalues, last)
     blocks = [sends]
     for bit in bits(groups):
-        blocks = blocks + [[swap(piece, bit, 0) for piece in block] for block in blocks]
+        blocks = blocks + [[swap(piece, bit, (0, 0)) for piece in block] for block in blocks]
     places = [(m, i) for m in range(groups) for i in range(CHAINS)]
+    offsets = (0, sends[0].shape[0])
     batches = [places[:CHAINS]] + [[place] for place in places[CHAINS:]]
     total = None
     for batch in batches:
         pieces = [blocks[m][i] for m, i in batch]
-        total = share(batch, pieces, responses, total, inv if batch is batches[-1] else None)
-    return weights(panel, total, swap(total, 0, 1))
+        total = share([(m, offsets[i]) for m, i in batch], pieces, responses, total, inv if batch is batches[-1] else None)
+    return weights(panel, total, swap(total, 0, (1, 1)))
 
 
 def solution(mesh):

time: 30 us -> 28.3 us (0.943)
  waiting for transfers between devices: 6.05 us -> 4.73 us
    ppermute x11, waiting for transfers between devices: 6.05 us -> 4.73 us  [swap(): return lax.ppermute(value, ('groups', 'eig'), pairs)]
    ppermute x11, starting transfers between devices: 16.9 us -> 16.6 us  [swap(): return lax.ppermute(value, ('groups', 'eig'), pairs)]
where the time goes in v5:
time: 28.3 us; the launch traced here: 28.2 us
  starting transfers between devices  16.6 us (59%)
  Pallas kernels  6.76 us (24%)
  waiting for transfers between devices  4.73 us (17%)
    ppermute x11, starting transfers between devices, swap(): return lax.ppermute(value, ('groups', 'eig'), pairs)  16.6 us
    ppermute x11, waiting for transfers between devices, swap(): return lax.ppermute(value, ('groups', 'eig'), pairs)  4.73 us
    pallas_call x1, Pallas kernels, weights(): pl.pallas_call(weights_kernel, in_specs=[VMEM, VMEM, VMEM], out_specs=HBM...  2.41 us
    pallas_call x1, Pallas kernels, gram_first(): pl.pallas_call(gram_first_kernel, in_specs=[HBM, HBM], out_specs=[VMEM] *...  2.15 us
    pallas_call x3, Pallas kernels, share(): pl.pallas_call(functools.partial(share_kernel, places, before is not None...  0.83 us
    pallas_call x1, Pallas kernels, inverse(): pl.pallas_call(inverse_kernel, in_specs=[SMEM, VMEM, VMEM, VMEM] + [ANY]...  0.8 us
  transfers between devices with their start and end apart: 11, of which 8 were waited for; matrix products, arithmetic and copies ran while one was open for 0% of the time, Pallas kernels for 7%

profile of v5, /device:TPU:0, one launch (start us, length us, event | category | flops | bytes accessed | tf_op | source)
XLA Modules:
  0.0 28.2 jit_solution(16560930916382832342)
XLA Ops:
  0.0 0.0 copy-start.1
  0.0 0.0 copy-start.3
  0.0 0.0 copy-start.2
  0.0 0.0 copy-start.4
  0.0 0.0 copy-start
  0.0 2.2 %gram_first.1 = (f32[256,128]{1,0:T(8,128)S(1)}, bf16[256,128]{1,0:T(8,128)(2,1)S(1)}, bf16[256,2048]{1,0:T(8,128)(2,1)S(1)}, bf16[2048,256]{1,0:T(8,128)(2,1)S(1)}) custom-call(bf16[1024,2048]{1,0:T(8,128)(2,1)} %f_hbm.1, bf16[2048,256]{1,0:T(8,128)(2,1)} %b_hbm.1), custom_call_target="tpu_custom_call" | custom-call | flops 268435456 | bytes 2097152 | tf_op jit(solution)/shard_map/gram_first/pallas_call | solution.py:103
  2.2 0.5 %collective-permute-start.1 = (bf16[256,128]{1,0:T(8,128)(2,1)S(1)}, bf16[256,128]{1,0:T(8,128)(2,1)S(1)}, u32[]{:S(2)}, u32[]{:S(2)}) collective-permute-start(bf16[256,128]{1,0:T(8,128)(2,1)S(1)} %get-tuple-element.25.refs_0_), channel_id=1, source_target_pairs={{0,1},{1,0},{2,3},{3,2},{4,5},{5,4},{6,7},{7,6},{8,9},{9,8},{10,11... | collective-permute-start | bytes 196616 | tf_op jit(solution)/shard_map/ppermute | solution.py:283
  2.7 0.4 %gram_rest.1 = (f32[256,128]{1,0:T(8,128)S(1)}, bf16[256,128]{1,0:T(8,128)(2,1)S(1)}) custom-call(bf16[256,2048]{1,0:T(8,128)(2,1)S(1)} %get-tuple-element.24.f_ref, bf16[2048,256]{1,0:T(8,128)(2,1)S(1)} %get-tuple-element.23.b_ref, bf16[256,128]{1,0:T(8,128)(2,1)S(1)} %get-tuple-element.25.refs_0_), custom_call_target="tpu_custom_call" | custom-call | flops 268435456 | bytes 2097152 | tf_op jit(solution)/shard_map/gram_rest/pallas_call | solution.py:128
  3.2 0.1 collective-permute-start
  3.3 0.3 %collective-permute-done.1.got_ref = bf16[256,128]{1,0:T(8,128)(2,1)S(1)} collective-permute-done((bf16[256,128]{1,0:T(8,128)(2,1)S(1)}, bf16[256,128]{1,0:T(8,128)(2,1)S(1)}, u32[]{:S(2)}, u32[]{:S(2)}) %collective-permute-start.1) | collective-permute-done | bytes 65568 | tf_op jit(solution)/shard_map/ppermute | solution.py:283
  3.6 2.7 %collective-permute-start.3 = (bf16[256,128]{1,0:T(8,128)(2,1)S(1)}, bf16[256,128]{1,0:T(8,128)(2,1)S(1)}, u32[]{:S(2)}, u32[]{:S(2)}) collective-permute-start(bf16[256,128]{1,0:T(8,128)(2,1)S(1)} %get-tuple-element.29.refs_0_), channel_id=1, source_target_pairs={{0,3},{1,8},{2,11},{3,0},{4,13},{5,6},{6,5},{7,14},{8,1},{9,10},{1... | collective-permute-start | bytes 196616 | tf_op jit(solution)/shard_map/ppermute | solution.py:283
  6.3 0.0 collective-permute-done.got_ref
  6.3 1.6 %collective-permute-start.2 = (bf16[256,128]{1,0:T(8,128)(2,1)S(1)}, bf16[256,128]{1,0:T(8,128)(2,1)S(1)}, u32[]{:S(2)}, u32[]{:S(2)}) collective-permute-start(bf16[256,128]{1,0:T(8,128)(2,1)S(1)} %get-tuple-element.31.refs_0_), channel_id=1, source_target_pairs={{0,5},{1,8},{2,11},{3,6},{4,13},{5,0},{6,3},{7,14},{8,1},{9,12},{1... | collective-permute-start | bytes 196616 | tf_op jit(solution)/shard_map/ppermute | solution.py:283
  8.0 0.3 %collective-permute-done.3.got_ref = bf16[256,128]{1,0:T(8,128)(2,1)S(1)} collective-permute-done((bf16[256,128]{1,0:T(8,128)(2,1)S(1)}, bf16[256,128]{1,0:T(8,128)(2,1)S(1)}, u32[]{:S(2)}, u32[]{:S(2)}) %collective-permute-start.3) | collective-permute-done | bytes 65568 | tf_op jit(solution)/shard_map/ppermute | solution.py:283
  8.3 2.2 %collective-permute-start.5 = (bf16[256,128]{1,0:T(8,128)(2,1)S(1)}, bf16[256,128]{1,0:T(8,128)(2,1)S(1)}, u32[]{:S(2)}, u32[]{:S(2)}) collective-permute-start(bf16[256,128]{1,0:T(8,128)(2,1)S(1)} %get-tuple-element.33.refs_0_), channel_id=1, source_target_pairs={{0,5},{1,2},{2,1},{3,6},{4,7},{5,0},{6,3},{7,4},{8,11},{9,12},{10,... | collective-permute-start | bytes 196616 | tf_op jit(solution)/shard_map/ppermute | solution.py:283
  10.5 0.1 collective-permute-done.2.got_ref
  10.6 2.7 %collective-permute-start.4 = (bf16[256,128]{1,0:T(8,128)(2,1)S(1)}, bf16[256,128]{1,0:T(8,128)(2,1)S(1)}, u32[]{:S(2)}, u32[]{:S(2)}) collective-permute-start(bf16[256,128]{1,0:T(8,128)(2,1)S(1)} %get-tuple-element.35.refs_0_), channel_id=1, source_target_pairs={{0,9},{1,2},{2,1},{3,10},{4,7},{5,12},{6,15},{7,4},{8,11},{9,0},{1... | collective-permute-start | bytes 196616 | tf_op jit(solution)/shard_map/ppermute | solution.py:283
  13.3 0.0 collective-permute-done.5.got_ref
  13.3 2.3 %collective-permute-start.7 = (bf16[256,128]{1,0:T(8,128)(2,1)S(1)}, bf16[256,128]{1,0:T(8,128)(2,1)S(1)}, u32[]{:S(2)}, u32[]{:S(2)}) collective-permute-start(bf16[256,128]{1,0:T(8,128)(2,1)S(1)} %get-tuple-element.37.refs_0_), channel_id=1, source_target_pairs={{0,9},{1,4},{2,7},{3,10},{4,1},{5,12},{6,15},{7,2},{8,13},{9,0},{1... | collective-permute-start | bytes 196616 | tf_op jit(solution)/shard_map/ppermute | solution.py:283
  15.5 0.0 collective-permute-done.4.got_ref
  15.6 1.5 %collective-permute-start.6 = (bf16[256,128]{1,0:T(8,128)(2,1)S(1)}, bf16[256,128]{1,0:T(8,128)(2,1)S(1)}, u32[]{:S(2)}, u32[]{:S(2)}) collective-permute-start(bf16[256,128]{1,0:T(8,128)(2,1)S(1)} %get-tuple-element.39.refs_0_), channel_id=1, source_target_pairs={{0,3},{1,4},{2,7},{3,0},{4,1},{5,6},{6,5},{7,2},{8,13},{9,10},{10,... | collective-permute-start | bytes 196616 | tf_op jit(solution)/shard_map/ppermute | solution.py:283
  17.1 1.0 %collective-permute-done.7.got_ref = bf16[256,128]{1,0:T(8,128)(2,1)S(1)} collective-permute-done((bf16[256,128]{1,0:T(8,128)(2,1)S(1)}, bf16[256,128]{1,0:T(8,128)(2,1)S(1)}, u32[]{:S(2)}, u32[]{:S(2)}) %collective-permute-start.7) | collective-permute-done | bytes 65568 | tf_op jit(solution)/shard_map/ppermute | solution.py:283
  18.1 1.1 %collective-permute-start.9 = (bf16[256,128]{1,0:T(8,128)(2,1)S(1)}, bf16[256,128]{1,0:T(8,128)(2,1)S(1)}, u32[]{:S(2)}, u32[]{:S(2)}) collective-permute-start(bf16[256,128]{1,0:T(8,128)(2,1)S(1)} %add.14.refs_0_), channel_id=1, source_target_pairs={{0,17},{1,16},{2,19},{3,18},{4,21},{5,20},{6,23},{7,22},{8,25},{9,... | collective-permute-start | bytes 196616 | tf_op jit(solution)/shard_map/ppermute | solution.py:283
  19.2 0.1 collective-permute-done.6.got_ref
  19.3 0.9 %collective-permute-start.8 = (bf16[256,128]{1,0:T(8,128)(2,1)S(1)}, bf16[256,128]{1,0:T(8,128)(2,1)S(1)}, u32[]{:S(2)}, u32[]{:S(2)}) collective-permute-start(bf16[256,128]{1,0:T(8,128)(2,1)S(1)} %add.15.refs_1_.refs_0_), channel_id=1, source_target_pairs={{0,17},{1,16},{2,19},{3,18},{4,21},{5,20},{6,23},{7,22},{8,25},{9,... | collective-permute-start | bytes 196616 | tf_op jit(solution)/shard_map/ppermute | solution.py:283
  20.3 0.0 copy-done.1
  20.3 0.0 copy-done.3
  20.3 0.0 copy-done.2
  20.3 0.0 copy-done.4
  20.3 0.8 %inverse.1.refs_3_ = f32[128,1024]{1,0:T(8,128)S(1)} custom-call(f32[8,16]{1,0:T(8,128)S(1)} %copy-done.1, s32[8,128]{1,0:T(8,128)S(1)} %bitcast.3, s32[8,128]{1,0:T(8,128)S(1)} %bitcast.4, f32[1,256]{1,0:T(1,128)S(1)} %bitcast.5, bf16[256,128]{1,0:T(8,128)(2,1)S(1)} %add.15.refs_1_.refs_0_), custom_call_target="tpu_custom_call" | custom-call | flops 1048576 | bytes 262144 | tf_op jit(solution)/shard_map/inverse/pallas_call | solution.py:166
  21.1 0.0 copy-done
  21.1 0.3 %share.3.refs_2_ = f32[128,1024]{1,0:T(8,128)S(1)} custom-call(bf16[256,128]{1,0:T(8,128)(2,1)S(1)} %add.14.refs_0_, bf16[256,128]{1,0:T(8,128)(2,1)S(1)} %add.15.refs_1_.refs_0_, bf16[1024,1024]{1,0:T(8,128)(2,1)S(1)} %copy-done), custom_call_target="tpu_custom_call" | custom-call | flops 134217728 | bytes 524288 | tf_op jit(solution)/shard_map/share/pallas_call | solution.py:225
  21.4 0.4 %collective-permute-done.9.refs_0_ = bf16[256,128]{1,0:T(8,128)(2,1)S(1)} collective-permute-done((bf16[256,128]{1,0:T(8,128)(2,1)S(1)}, bf16[256,128]{1,0:T(8,128)(2,1)S(1)}, u32[]{:S(2)}, u32[]{:S(2)}) %collective-permute-start.9) | collective-permute-done | bytes 65568 | tf_op jit(solution)/shard_map/ppermute | solution.py:283
  21.8 0.3 share.4.refs_2_
  22.1 1.3 %collective-permute-done.8.refs_0_ = bf16[256,128]{1,0:T(8,128)(2,1)S(1)} collective-permute-done((bf16[256,128]{1,0:T(8,128)(2,1)S(1)}, bf16[256,128]{1,0:T(8,128)(2,1)S(1)}, u32[]{:S(2)}, u32[]{:S(2)}) %collective-permute-start.8) | collective-permute-done | bytes 65568 | tf_op jit(solution)/shard_map/ppermute | solution.py:283
  23.3 0.3 share.5.own_ref
  23.6 1.0 %collective-permute-start.10 = (bf16[128,1024]{1,0:T(8,128)(2,1)S(1)}, bf16[128,1024]{1,0:T(8,128)(2,1)S(1)}, u32[]{:S(2)}, u32[]{:S(2)}) collective-permute-start(bf16[128,1024]{1,0:T(8,128)(2,1)S(1)} %share.5.own_ref), channel_id=1, source_target_pairs={{0,1},{1,0},{2,3},{3,2},{4,5},{5,4},{6,7},{7,6},{8,9},{9,8},{10,11... | collective-permute-start | bytes 786440 | tf_op jit(solution)/shard_map/ppermute | solution.py:283
  24.6 1.2 %collective-permute-done.10.got_ref = bf16[128,1024]{1,0:T(8,128)(2,1)S(1)} collective-permute-done((bf16[128,1024]{1,0:T(8,128)(2,1)S(1)}, bf16[128,1024]{1,0:T(8,128)(2,1)S(1)}, u32[]{:S(2)}, u32[]{:S(2)}) %collective-permute-start.10) | collective-permute-done | bytes 262176 | tf_op jit(solution)/shard_map/ppermute | solution.py:283
  25.8 2.4 %weights.1 = bf16[2048,1024]{1,0:T(8,128)(2,1)} custom-call(bf16[2048,256]{1,0:T(8,128)(2,1)S(1)} %get-tuple-element.23.b_ref, bf16[128,1024]{1,0:T(8,128)(2,1)S(1)} %share.5.own_ref, bf16[128,1024]{1,0:T(8,128)(2,1)S(1)} %collective-permute-done.10.got_ref), custom_call_target="tpu_custom_call" | custom-call | flops 1073741824 | bytes 4194304 | tf_op jit(solution)/shard_map/weights/pallas_call | solution.py:259
  (8 shorter events, 0.1 us)
Async XLA Ops:
  0.0 20.3 %copy-start.1 = (f32[8,16]{1,0:T(8,128)S(1)}, f32[8,16]{1,0:T(8,128)}, u32[]{:S(2)}) copy-start(f32[8,16]{1,0:T(8,128)} %table_ref.1) | copy-start | bytes 1540
  0.0 20.3 %copy-start.3 = (s32[1024]{0:T(1024)S(1)}, s32[1024]{0:T(1024)}, u32[]{:S(2)}) copy-start(s32[1024]{0:T(1024)} %param.12) | copy-start | bytes 12292
  0.0 20.3 %copy-start.2 = (s32[1024]{0:T(1024)S(1)}, s32[1024]{0:T(1024)}, u32[]{:S(2)}) copy-start(s32[1024]{0:T(1024)} %param.11) | copy-start | bytes 12292
  0.0 20.3 %copy-start.4 = (f32[256]{0:T(256)S(1)}, f32[256]{0:T(256)}, u32[]{:S(2)}) copy-start(f32[256]{0:T(256)} %param.10) | copy-start | bytes 3076
  0.0 21.1 %copy-start = (bf16[1024,1024]{1,0:T(8,128)(2,1)S(1)}, bf16[1024,1024]{1,0:T(8,128)(2,1)}, u32[]{:S(2)}) copy-start(bf16[1024,1024]{1,0:T(8,128)(2,1)} %refs_1_.3) | copy-start | bytes 6291460
  2.2 1.4 %collective-permute-start.1 = (bf16[256,128]{1,0:T(8,128)(2,1)S(1)}, bf16[256,128]{1,0:T(8,128)(2,1)S(1)}, u32[]{:S(2)}, u32[]{:S(2)}) collective-permute-start(bf16[256,128]{1,0:T(8,128)(2,1)S(1)} %get-tuple-element.25.refs_0_), channel_id=1, source_target_pairs={{0,1},{1,0},{2,3},{3,2},{4,5},{5,4},{6,7},{7,6},{8,9},{9,8},{10,11... | collective-permute-start | bytes 196616 | tf_op jit(solution)/shard_map/ppermute | solution.py:283
  3.2 3.2 %collective-permute-start = (bf16[256,128]{1,0:T(8,128)(2,1)S(1)}, bf16[256,128]{1,0:T(8,128)(2,1)S(1)}, u32[]{:S(2)}, u32[]{:S(2)}) collective-permute-start(bf16[256,128]{1,0:T(8,128)(2,1)S(1)} %get-tuple-element.27.refs_0_), channel_id=1, source_target_pairs={{0,1},{1,0},{2,3},{3,2},{4,5},{5,4},{6,7},{7,6},{8,9},{9,8},{10,11... | collective-permute-start | bytes 196616 | tf_op jit(solution)/shard_map/ppermute | solution.py:283
  3.6 4.6 %collective-permute-start.3 = (bf16[256,128]{1,0:T(8,128)(2,1)S(1)}, bf16[256,128]{1,0:T(8,128)(2,1)S(1)}, u32[]{:S(2)}, u32[]{:S(2)}) collective-permute-start(bf16[256,128]{1,0:T(8,128)(2,1)S(1)} %get-tuple-element.29.refs_0_), channel_id=1, source_target_pairs={{0,3},{1,8},{2,11},{3,0},{4,13},{5,6},{6,5},{7,14},{8,1},{9,10},{1... | collective-permute-start | bytes 196616 | tf_op jit(solution)/shard_map/ppermute | solution.py:283
  6.3 4.2 %collective-permute-start.2 = (bf16[256,128]{1,0:T(8,128)(2,1)S(1)}, bf16[256,128]{1,0:T(8,128)(2,1)S(1)}, u32[]{:S(2)}, u32[]{:S(2)}) collective-permute-start(bf16[256,128]{1,0:T(8,128)(2,1)S(1)} %get-tuple-element.31.refs_0_), channel_id=1, source_target_pairs={{0,5},{1,8},{2,11},{3,6},{4,13},{5,0},{6,3},{7,14},{8,1},{9,12},{1... | collective-permute-start | bytes 196616 | tf_op jit(solution)/shard_map/ppermute | solution.py:283
  8.3 5.0 %collective-permute-start.5 = (bf16[256,128]{1,0:T(8,128)(2,1)S(1)}, bf16[256,128]{1,0:T(8,128)(2,1)S(1)}, u32[]{:S(2)}, u32[]{:S(2)}) collective-permute-start(bf16[256,128]{1,0:T(8,128)(2,1)S(1)} %get-tuple-element.33.refs_0_), channel_id=1, source_target_pairs={{0,5},{1,2},{2,1},{3,6},{4,7},{5,0},{6,3},{7,4},{8,11},{9,12},{10,... | collective-permute-start | bytes 196616 | tf_op jit(solution)/shard_map/ppermute | solution.py:283
  10.6 4.9 %collective-permute-start.4 = (bf16[256,128]{1,0:T(8,128)(2,1)S(1)}, bf16[256,128]{1,0:T(8,128)(2,1)S(1)}, u32[]{:S(2)}, u32[]{:S(2)}) collective-permute-start(bf16[256,128]{1,0:T(8,128)(2,1)S(1)} %get-tuple-element.35.refs_0_), channel_id=1, source_target_pairs={{0,9},{1,2},{2,1},{3,10},{4,7},{5,12},{6,15},{7,4},{8,11},{9,0},{1... | collective-permute-start | bytes 196616 | tf_op jit(solution)/shard_map/ppermute | solution.py:283
  13.3 4.8 %collective-permute-start.7 = (bf16[256,128]{1,0:T(8,128)(2,1)S(1)}, bf16[256,128]{1,0:T(8,128)(2,1)S(1)}, u32[]{:S(2)}, u32[]{:S(2)}) collective-permute-start(bf16[256,128]{1,0:T(8,128)(2,1)S(1)} %get-tuple-element.37.refs_0_), channel_id=1, source_target_pairs={{0,9},{1,4},{2,7},{3,10},{4,1},{5,12},{6,15},{7,2},{8,13},{9,0},{1... | collective-permute-start | bytes 196616 | tf_op jit(solution)/shard_map/ppermute | solution.py:283
  15.6 3.8 %collective-permute-start.6 = (bf16[256,128]{1,0:T(8,128)(2,1)S(1)}, bf16[256,128]{1,0:T(8,128)(2,1)S(1)}, u32[]{:S(2)}, u32[]{:S(2)}) collective-permute-start(bf16[256,128]{1,0:T(8,128)(2,1)S(1)} %get-tuple-element.39.refs_0_), channel_id=1, source_target_pairs={{0,3},{1,4},{2,7},{3,0},{4,1},{5,6},{6,5},{7,2},{8,13},{9,10},{10,... | collective-permute-start | bytes 196616 | tf_op jit(solution)/shard_map/ppermute | solution.py:283
  18.1 3.8 %collective-permute-start.9 = (bf16[256,128]{1,0:T(8,128)(2,1)S(1)}, bf16[256,128]{1,0:T(8,128)(2,1)S(1)}, u32[]{:S(2)}, u32[]{:S(2)}) collective-permute-start(bf16[256,128]{1,0:T(8,128)(2,1)S(1)} %add.14.refs_0_), channel_id=1, source_target_pairs={{0,17},{1,16},{2,19},{3,18},{4,21},{5,20},{6,23},{7,22},{8,25},{9,... | collective-permute-start | bytes 196616 | tf_op jit(solution)/shard_map/ppermute | solution.py:283
  19.3 4.0 %collective-permute-start.8 = (bf16[256,128]{1,0:T(8,128)(2,1)S(1)}, bf16[256,128]{1,0:T(8,128)(2,1)S(1)}, u32[]{:S(2)}, u32[]{:S(2)}) collective-permute-start(bf16[256,128]{1,0:T(8,128)(2,1)S(1)} %add.15.refs_1_.refs_0_), channel_id=1, source_target_pairs={{0,17},{1,16},{2,19},{3,18},{4,21},{5,20},{6,23},{7,22},{8,25},{9,... | collective-permute-start | bytes 196616 | tf_op jit(solution)/shard_map/ppermute | solution.py:283
  23.6 2.2 %collective-permute-start.10 = (bf16[128,1024]{1,0:T(8,128)(2,1)S(1)}, bf16[128,1024]{1,0:T(8,128)(2,1)S(1)}, u32[]{:S(2)}, u32[]{:S(2)}) collective-permute-start(bf16[128,1024]{1,0:T(8,128)(2,1)S(1)} %share.5.own_ref), channel_id=1, source_target_pairs={{0,1},{1,0},{2,3},{3,2},{4,5},{5,4},{6,7},{7,6},{8,9},{9,8},{10,11... | collective-permute-start | bytes 786440 | tf_op jit(solution)/shard_map/ppermute | solution.py:283

commit v6 on v5

--- a/solution.py
+++ b/solution.py
@@ -11,13 +11,12 @@
 BF16 = jnp.bfloat16
 MIB = 1 << 20
 CHAINS = 2
-EIG_FLIP = 14
+EIG_FLIP = 10
 GROUP_FLIP = 1
 FIRST = 8
 ANY = pl.BlockSpec(memory_space=pl.ANY)
 HBM = pl.BlockSpec(memory_space=pltpu.HBM)
 VMEM = pl.BlockSpec(memory_space=pltpu.VMEM)
-SMEM = pl.BlockSpec(memory_space=pltpu.SMEM)
 
 
 def params(mib):
@@ -142,36 +141,34 @@
 def inverse_kernel(table_ref, reg_ref, subject_ref, eig_ref, *refs):
     out_ref = refs[-1]
     subjects, grid = table_ref.shape
-    k = out_ref.shape[0]
-    code = subject_ref[...] * grid + reg_ref[...]
-    alpha = jnp.zeros(code.shape, F32)
-    for s in range(subjects):
-        for g in range(grid):
-            alpha = jnp.where(code == s * grid + g, table_ref[s, g], alpha)
-    alpha = alpha.reshape(1, alpha.size)
+    k, vox = out_ref.shape
+    picked = lax.broadcasted_iota(jnp.int32, (grid, vox), 0) == reg_ref[...]
+    rows = jnp.dot(
+        table_ref[...], picked.astype(F32), precision=lax.Precision.HIGHEST, preferred_element_type=F32
+    )
+    mine = lax.broadcasted_iota(jnp.int32, (subjects, vox), 0) == subject_ref[...]
+    alpha = jnp.sum(jnp.where(mine, rows, 0.0), axis=0, keepdims=True)
     side = min(k, 128)
-    first = half_index() == 0
-    eig = jnp.where(first, eig_ref[:, :k], eig_ref[:, k:])
     shape = (side, side)
     diagonal = lax.broadcasted_iota(jnp.int32, shape, 0) == lax.broadcasted_iota(jnp.int32, shape, 1)
     for i in range(k // side):
         at = pl.ds(i * side, side)
-        column = jnp.sum(jnp.where(diagonal, eig[:, i * side : (i + 1) * side], 0.0), axis=1, keepdims=True)
+        column = jnp.sum(jnp.where(diagonal, eig_ref[:, pl.ds(i * side, side)], 0.0), axis=1, keepdims=True)
         out_ref[at, :] = 1.0 / (column + alpha)
 
 
 def inverse(alpha_table, reg_index, subject, eigenvalues, after):
     vox = reg_index.shape[0]
-    k = eigenvalues.shape[0] // 2
+    k = eigenvalues.shape[0]
     return pl.pallas_call(
         inverse_kernel,
-        in_specs=[SMEM, VMEM, VMEM, VMEM] + [ANY] * len(after),
+        in_specs=[VMEM, VMEM, VMEM, VMEM] + [ANY] * len(after),
         out_specs=VMEM,
         out_shape=jax.ShapeDtypeStruct((k, vox), F32),
         compiler_params=params(8),
         cost_estimate=cost(8 * k * vox, 2 * k * vox),
         name="inverse",
-    )(alpha_table, reg_index.reshape(-1, 128), subject.reshape(-1, 128), eigenvalues[None, :], *after)
+    )(alpha_table, reg_index[None, :], subject[None, :], eigenvalues[None, :], *after)
 
 
 def add_kernel(total_ref, got_ref, *refs):
@@ -194,23 +191,28 @@
         out_specs=VMEM if last else [VMEM, VMEM],
         out_shape=both[1] if last else both,
         compiler_params=params(4),
-        cost_estimate=cost(total.size, 12 * total.size),
+        cost_estimate=cost(4 * 10**9, 12 * total.size),
         name="add",
     )(total, got, *after)
 
 
 def share_kernel(places, has_sum, finish, *refs):
-    n = len(places)
+    n = 2 * len(places)
     r_ref, out_ref = refs[n], refs[-1]
     rest = list(refs[n + 1 : -1])
     group = lax.axis_index("groups")
+    first = half_index() == 0
     times = r_ref.shape[0] // lax.axis_size("groups")
     total = rest.pop(0)[...] if has_sum else None
-    for (m, at), piece in zip(places, refs):
-        rows = piece.shape[0]
+    for i, (m, at) in enumerate(places):
+        own, got = refs[2 * i][...], refs[2 * i + 1][...]
+        piece = jnp.concatenate([jnp.where(first, own, got), jnp.where(first, got, own)], axis=1)
         start = pl.multiple_of((group ^ m) * times + at, 16)
         term = lax.dot_general(
-            piece[...], r_ref[pl.ds(start, rows), :], (((0,), (0,)), ((), ())), preferred_element_type=F32
+            piece,
+            r_ref[pl.ds(start, piece.shape[0]), :],
+            (((0,), (0,)), ((), ())),
+            preferred_element_type=F32,
         )
         total = term if total is None else total + term
     if finish:
@@ -219,7 +221,7 @@
 
 
 def share(places, pieces, responses, before=None, inv=None):
-    rows, k = pieces[0].shape
+    rows, k = pieces[0].shape[0], 2 * pieces[0].shape[1]
     vox = responses.shape[1]
     extra = [value for value in (before, inv) if value is not None]
     return pl.pallas_call(
@@ -233,13 +235,8 @@
     )(*pieces, responses, *extra)
 
 
-def weights_kernel(b_ref, own_ref, got_ref, out_hbm, s_ref, out_ref, sems):
+def weights_kernel(b_ref, s_ref, out_hbm, out_ref, sems):
     parts = sems.shape[0]
-    half = own_ref.shape[0]
-    first = half_index() == 0
-    own, got = own_ref[...], got_ref[...]
-    s_ref[:half, :] = jnp.where(first, own, got)
-    s_ref[half:, :] = jnp.where(first, got, own)
     chunk = b_ref.shape[0] // parts
     copies = []
     for i in range(parts):
@@ -252,24 +249,20 @@
         copy.wait()
 
 
-def weights(basis, own, got):
+def weights(basis, scaled):
     feats, k = basis.shape
-    half, vox = own.shape
+    vox = scaled.shape[1]
     parts = 8
     return pl.pallas_call(
         weights_kernel,
-        in_specs=[VMEM, VMEM, VMEM],
+        in_specs=[VMEM, VMEM],
         out_specs=HBM,
         out_shape=jax.ShapeDtypeStruct((feats, vox), BF16),
-        scratch_shapes=[
-            pltpu.VMEM((k, vox), BF16),
-            pltpu.VMEM((feats, vox), BF16),
-            pltpu.SemaphoreType.DMA((parts,)),
-        ],
+        scratch_shapes=[pltpu.VMEM((feats, vox), BF16), pltpu.SemaphoreType.DMA((parts,))],
         compiler_params=params(16),
         cost_estimate=cost(2 * feats * k * vox, 2 * feats * vox),
         name="weights",
-    )(basis, own, got)
+    )(basis, scaled)
 
 
 def swap(value, group_mask, eig_masks):
@@ -308,6 +301,9 @@
     masks = orders(lax.axis_size("eig"))
     count = len(masks[0][0])
     for at in range(count + 1):
+        if at == count:
+            inv = inverse(alpha_table, reg_index, subject, eigenvalues, last)
+            last = (inv,)
         for i in range(CHAINS):
             if at == count:
                 sends[i] = add(totals[i], gots[i], last, True)
@@ -316,18 +312,19 @@
                 gots[i] = swap(sends[i], 0, [masks[i][half][at] for half in range(2)])
             last = (sends[i],)
 
-    inv = inverse(alpha_table, reg_index, subject, eigenvalues, last)
     blocks = [sends]
     for bit in bits(groups):
         blocks = blocks + [[swap(piece, bit, (0, 0)) for piece in block] for block in blocks]
+    offsets = (0, sends[0].shape[0])
     places = [(m, i) for m in range(groups) for i in range(CHAINS)]
-    offsets = (0, sends[0].shape[0])
     batches = [places[:CHAINS]] + [[place] for place in places[CHAINS:]]
     total = None
     for batch in batches:
-        pieces = [blocks[m][i] for m, i in batch]
+        pieces = []
+        for m, i in batch:
+            pieces += [blocks[m][i], swap(blocks[m][i], 0, (1, 1))]
         total = share([(m, offsets[i]) for m, i in batch], pieces, responses, total, inv if batch is batches[-1] else None)
-    return weights(panel, total, swap(total, 0, (1, 1)))
+    return weights(panel, total)
 
 
 def solution(mesh):

time: 28.3 us -> 27.7 us (0.979)
  Pallas kernels: 6.76 us -> 6.45 us
  waiting for transfers between devices: 4.73 us -> 4.44 us
    pallas_call x2, Pallas kernels: 3.21 us -> 2.68 us  [the longest x1 2.38 us: weights(): pl.pallas_call(weights_kernel, in_specs=[VMEM, VMEM], out_specs=HBM, out_...]
    pallas_call x3, Pallas kernels: 0.83 us -> 1.21 us  [share(): pl.pallas_call(functools.partial(share_kernel, places, before is not None...]
    ppermute x11 -> x14, waiting for transfers between devices: 4.73 us -> 4.44 us  [swap(): return lax.ppermute(value, ('groups', 'eig'), pairs)]
    ppermute x11 -> x14, starting transfers between devices: 16.6 us -> 16.5 us  [swap(): return lax.ppermute(value, ('groups', 'eig'), pairs)]
  transfers between devices with their start and end apart: 11 -> 14, of which waited for: 8 -> 9; matrix products, arithmetic and copies ran while one was open for 0% -> 0% of each run, Pallas kernels for 7% -> 6%
where the time goes in v6:
time: 27.7 us; the launch traced here: 27.5 us
  starting transfers between devices  16.5 us (60%)
  Pallas kernels  6.45 us (23%)
  waiting for transfers between devices  4.44 us (16%)
    ppermute x14, starting transfers between devices, swap(): return lax.ppermute(value, ('groups', 'eig'), pairs)  16.5 us
    ppermute x14, waiting for transfers between devices, swap(): return lax.ppermute(value, ('groups', 'eig'), pairs)  4.44 us
    pallas_call x1, Pallas kernels, weights(): pl.pallas_call(weights_kernel, in_specs=[VMEM, VMEM], out_specs=HBM, out_...  2.38 us
    pallas_call x1, Pallas kernels, gram_first(): pl.pallas_call(gram_first_kernel, in_specs=[HBM, HBM], out_specs=[VMEM] *...  2 us
    pallas_call x3, Pallas kernels, share(): pl.pallas_call(functools.partial(share_kernel, places, before is not None...  1.21 us
  transfers between devices with their start and end apart: 14, of which 9 were waited for; matrix products, arithmetic and copies ran while one was open for 0% of the time, Pallas kernels for 6%

profile of v6, /device:TPU:0, one launch (start us, length us, event | category | flops | bytes accessed | tf_op | source)
XLA Modules:
  0.0 27.5 jit_solution(11252381762296268166)
XLA Ops:
  0.0 2.0 %gram_first.1 = (f32[256,128]{1,0:T(8,128)S(1)}, bf16[256,128]{1,0:T(8,128)(2,1)S(1)}, bf16[256,2048]{1,0:T(8,128)(2,1)S(1)}, bf16[2048,256]{1,0:T(8,128)(2,1)S(1)}) custom-call(bf16[1024,2048]{1,0:T(8,128)(2,1)} %f_hbm.1, bf16[2048,256]{1,0:T(8,128)(2,1)} %b_hbm.1), custom_call_target="tpu_custom_call" | custom-call | flops 268435456 | bytes 2097152 | tf_op jit(solution)/shard_map/gram_first/pallas_call | solution.py:102
  2.0 0.5 %collective-permute-start.1 = (bf16[256,128]{1,0:T(8,128)(2,1)S(1)}, bf16[256,128]{1,0:T(8,128)(2,1)S(1)}, u32[]{:S(2)}, u32[]{:S(2)}) collective-permute-start(bf16[256,128]{1,0:T(8,128)(2,1)S(1)} %get-tuple-element.25.refs_0_), channel_id=1, source_target_pairs={{0,1},{1,0},{2,3},{3,2},{4,5},{5,4},{6,7},{7,6},{8,9},{9,8},{10,11... | collective-permute-start | bytes 196616 | tf_op jit(solution)/shard_map/ppermute | solution.py:276
  2.5 0.4 %gram_rest.1 = (f32[256,128]{1,0:T(8,128)S(1)}, bf16[256,128]{1,0:T(8,128)(2,1)S(1)}) custom-call(bf16[256,2048]{1,0:T(8,128)(2,1)S(1)} %get-tuple-element.24.f_ref, bf16[2048,256]{1,0:T(8,128)(2,1)S(1)} %get-tuple-element.23.b_ref, bf16[256,128]{1,0:T(8,128)(2,1)S(1)} %get-tuple-element.25.refs_0_), custom_call_target="tpu_custom_call" | custom-call | flops 268435456 | bytes 2097152 | tf_op jit(solution)/shard_map/gram_rest/pallas_call | solution.py:127
  3.0 0.1 collective-permute-start
  3.1 0.3 %collective-permute-done.1.got_ref = bf16[256,128]{1,0:T(8,128)(2,1)S(1)} collective-permute-done((bf16[256,128]{1,0:T(8,128)(2,1)S(1)}, bf16[256,128]{1,0:T(8,128)(2,1)S(1)}, u32[]{:S(2)}, u32[]{:S(2)}) %collective-permute-start.1) | collective-permute-done | bytes 65568 | tf_op jit(solution)/shard_map/ppermute | solution.py:276
  3.4 2.7 %collective-permute-start.3 = (bf16[256,128]{1,0:T(8,128)(2,1)S(1)}, bf16[256,128]{1,0:T(8,128)(2,1)S(1)}, u32[]{:S(2)}, u32[]{:S(2)}) collective-permute-start(bf16[256,128]{1,0:T(8,128)(2,1)S(1)} %get-tuple-element.29.refs_0_), channel_id=1, source_target_pairs={{0,3},{1,8},{2,11},{3,0},{4,7},{5,12},{6,15},{7,4},{8,1},{9,10},{1... | collective-permute-start | bytes 196616 | tf_op jit(solution)/shard_map/ppermute | solution.py:276
  6.1 0.0 collective-permute-done.got_ref
  6.2 1.6 %collective-permute-start.2 = (bf16[256,128]{1,0:T(8,128)(2,1)S(1)}, bf16[256,128]{1,0:T(8,128)(2,1)S(1)}, u32[]{:S(2)}, u32[]{:S(2)}) collective-permute-start(bf16[256,128]{1,0:T(8,128)(2,1)S(1)} %get-tuple-element.31.refs_0_), channel_id=1, source_target_pairs={{0,4},{1,8},{2,11},{3,7},{4,0},{5,12},{6,15},{7,3},{8,1},{9,13},{1... | collective-permute-start | bytes 196616 | tf_op jit(solution)/shard_map/ppermute | solution.py:276
  7.8 0.3 %collective-permute-done.3.got_ref = bf16[256,128]{1,0:T(8,128)(2,1)S(1)} collective-permute-done((bf16[256,128]{1,0:T(8,128)(2,1)S(1)}, bf16[256,128]{1,0:T(8,128)(2,1)S(1)}, u32[]{:S(2)}, u32[]{:S(2)}) %collective-permute-start.3) | collective-permute-done | bytes 65568 | tf_op jit(solution)/shard_map/ppermute | solution.py:276
  8.1 2.1 %collective-permute-start.5 = (bf16[256,128]{1,0:T(8,128)(2,1)S(1)}, bf16[256,128]{1,0:T(8,128)(2,1)S(1)}, u32[]{:S(2)}, u32[]{:S(2)}) collective-permute-start(bf16[256,128]{1,0:T(8,128)(2,1)S(1)} %get-tuple-element.33.refs_0_), channel_id=1, source_target_pairs={{0,4},{1,2},{2,1},{3,7},{4,0},{5,6},{6,5},{7,3},{8,11},{9,13},{10,... | collective-permute-start | bytes 196616 | tf_op jit(solution)/shard_map/ppermute | solution.py:276
  10.2 0.3 %collective-permute-done.2.got_ref = bf16[256,128]{1,0:T(8,128)(2,1)S(1)} collective-permute-done((bf16[256,128]{1,0:T(8,128)(2,1)S(1)}, bf16[256,128]{1,0:T(8,128)(2,1)S(1)}, u32[]{:S(2)}, u32[]{:S(2)}) %collective-permute-start.2) | collective-permute-done | bytes 65568 | tf_op jit(solution)/shard_map/ppermute | solution.py:276
  10.5 2.2 %collective-permute-start.4 = (bf16[256,128]{1,0:T(8,128)(2,1)S(1)}, bf16[256,128]{1,0:T(8,128)(2,1)S(1)}, u32[]{:S(2)}, u32[]{:S(2)}) collective-permute-start(bf16[256,128]{1,0:T(8,128)(2,1)S(1)} %get-tuple-element.35.refs_0_), channel_id=1, source_target_pairs={{0,9},{1,2},{2,1},{3,10},{4,13},{5,6},{6,5},{7,14},{8,11},{9,0},{1... | collective-permute-start | bytes 196616 | tf_op jit(solution)/shard_map/ppermute | solution.py:276
  12.7 0.5 %collective-permute-done.5.got_ref = bf16[256,128]{1,0:T(8,128)(2,1)S(1)} collective-permute-done((bf16[256,128]{1,0:T(8,128)(2,1)S(1)}, bf16[256,128]{1,0:T(8,128)(2,1)S(1)}, u32[]{:S(2)}, u32[]{:S(2)}) %collective-permute-start.5) | collective-permute-done | bytes 65568 | tf_op jit(solution)/shard_map/ppermute | solution.py:276
  13.1 1.3 %collective-permute-start.7 = (bf16[256,128]{1,0:T(8,128)(2,1)S(1)}, bf16[256,128]{1,0:T(8,128)(2,1)S(1)}, u32[]{:S(2)}, u32[]{:S(2)}) collective-permute-start(bf16[256,128]{1,0:T(8,128)(2,1)S(1)} %get-tuple-element.37.refs_0_), channel_id=1, source_target_pairs={{0,9},{1,5},{2,6},{3,10},{4,13},{5,1},{6,2},{7,14},{8,12},{9,0},{1... | collective-permute-start | bytes 196616 | tf_op jit(solution)/shard_map/ppermute | solution.py:276
  14.5 0.7 %collective-permute-done.4.got_ref = bf16[256,128]{1,0:T(8,128)(2,1)S(1)} collective-permute-done((bf16[256,128]{1,0:T(8,128)(2,1)S(1)}, bf16[256,128]{1,0:T(8,128)(2,1)S(1)}, u32[]{:S(2)}, u32[]{:S(2)}) %collective-permute-start.4) | collective-permute-done | bytes 65568 | tf_op jit(solution)/shard_map/ppermute | solution.py:276
  15.2 0.0 copy-start.1
  15.2 0.0 copy-start.2
  15.2 0.0 copy-start.3
  15.2 0.0 copy-start.4
  15.2 1.7 %collective-permute-start.6 = (bf16[256,128]{1,0:T(8,128)(2,1)S(1)}, bf16[256,128]{1,0:T(8,128)(2,1)S(1)}, u32[]{:S(2)}, u32[]{:S(2)}) collective-permute-start(bf16[256,128]{1,0:T(8,128)(2,1)S(1)} %get-tuple-element.39.refs_0_), channel_id=1, source_target_pairs={{0,3},{1,5},{2,6},{3,0},{4,7},{5,1},{6,2},{7,4},{8,12},{9,10},{10,... | collective-permute-start | bytes 196616 | tf_op jit(solution)/shard_map/ppermute | solution.py:276
  16.9 0.0 copy-done.1
  16.9 0.0 copy-done.2
  16.9 0.0 copy-done.3
  16.9 0.0 copy-done.4
  17.0 0.3 %inverse.1.refs_0_.refs_4_ = f32[256,1024]{1,0:T(8,128)S(1)} custom-call(f32[8,16]{1,0:T(8,128)S(1)} %copy-done.1, s32[1,1024]{1,0:T(1,128)S(1)} %bitcast.3, s32[1,1024]{1,0:T(1,128)S(1)} %bitcast.4, f32[1,256]{1,0:T(1,128)S(1)} %bitcast.5, bf16[256,128]{1,0:T(8,128)(2,1)S(1)} %get-tuple-element.39.refs_0_), custom_call_target="tpu_custom_call" | custom-call | flops 2097152 | bytes 524288 | tf_op jit(solution)/shard_map/inverse/pallas_call | solution.py:163
  17.3 0.7 %collective-permute-done.7.got_ref = bf16[256,128]{1,0:T(8,128)(2,1)S(1)} collective-permute-done((bf16[256,128]{1,0:T(8,128)(2,1)S(1)}, bf16[256,128]{1,0:T(8,128)(2,1)S(1)}, u32[]{:S(2)}, u32[]{:S(2)}) %collective-permute-start.7) | collective-permute-done | bytes 65568 | tf_op jit(solution)/shard_map/ppermute | solution.py:276
  17.9 1.6 %collective-permute-start.10 = (bf16[256,128]{1,0:T(8,128)(2,1)S(1)}, bf16[256,128]{1,0:T(8,128)(2,1)S(1)}, u32[]{:S(2)}, u32[]{:S(2)}) collective-permute-start(bf16[256,128]{1,0:T(8,128)(2,1)S(1)} %add.14.refs_0_), channel_id=1, source_target_pairs={{0,17},{1,16},{2,19},{3,18},{4,21},{5,20},{6,23},{7,22},{8,25},{9,... | collective-permute-start | bytes 196616 | tf_op jit(solution)/shard_map/ppermute | solution.py:276
  19.6 0.0 collective-permute-done.6.got_ref
  19.6 0.0 copy-start
  19.6 1.4 %collective-permute-start.8 = (bf16[256,128]{1,0:T(8,128)(2,1)S(1)}, bf16[256,128]{1,0:T(8,128)(2,1)S(1)}, u32[]{:S(2)}, u32[]{:S(2)}) collective-permute-start(bf16[256,128]{1,0:T(8,128)(2,1)S(1)} %add.15.refs_2_), channel_id=1, source_target_pairs={{0,17},{1,16},{2,19},{3,18},{4,21},{5,20},{6,23},{7,22},{8,25},{9,... | collective-permute-start | bytes 196616 | tf_op jit(solution)/shard_map/ppermute | solution.py:276
  21.0 0.8 %collective-permute-start.13 = (bf16[256,128]{1,0:T(8,128)(2,1)S(1)}, bf16[256,128]{1,0:T(8,128)(2,1)S(1)}, u32[]{:S(2)}, u32[]{:S(2)}) collective-permute-start(bf16[256,128]{1,0:T(8,128)(2,1)S(1)} %add.15.refs_2_), channel_id=1, source_target_pairs={{0,1},{1,0},{2,3},{3,2},{4,5},{5,4},{6,7},{7,6},{8,9},{9,8},{10,11... | collective-permute-start | bytes 196616 | tf_op jit(solution)/shard_map/ppermute | solution.py:276
  21.8 0.0 collective-permute-start.12
  21.8 0.4 %collective-permute-done.10.refs_0_ = bf16[256,128]{1,0:T(8,128)(2,1)S(1)} collective-permute-done((bf16[256,128]{1,0:T(8,128)(2,1)S(1)}, bf16[256,128]{1,0:T(8,128)(2,1)S(1)}, u32[]{:S(2)}, u32[]{:S(2)}) %collective-permute-start.10) | collective-permute-done | bytes 65568 | tf_op jit(solution)/shard_map/ppermute | solution.py:276
  22.2 0.1 collective-permute-start.11
  22.3 1.2 %collective-permute-done.8.refs_0_ = bf16[256,128]{1,0:T(8,128)(2,1)S(1)} collective-permute-done((bf16[256,128]{1,0:T(8,128)(2,1)S(1)}, bf16[256,128]{1,0:T(8,128)(2,1)S(1)}, u32[]{:S(2)}, u32[]{:S(2)}) %collective-permute-start.8) | collective-permute-done | bytes 65568 | tf_op jit(solution)/shard_map/ppermute | solution.py:276
  23.6 0.3 %collective-permute-start.9 = (bf16[256,128]{1,0:T(8,128)(2,1)S(1)}, bf16[256,128]{1,0:T(8,128)(2,1)S(1)}, u32[]{:S(2)}, u32[]{:S(2)}) collective-permute-start(bf16[256,128]{1,0:T(8,128)(2,1)S(1)} %collective-permute-done.8.refs_0_), channel_id=1, source_target_pairs={{0,1},{1,0},{2,3},{3,2},{4,5},{5,4},{6,7},{7,6},{8,9},{9,8},{10,11... | collective-permute-start | bytes 196616 | tf_op jit(solution)/shard_map/ppermute | solution.py:276
  23.9 0.0 collective-permute-done.13.refs_3_
  23.9 0.0 collective-permute-done.12.refs_1_
  23.9 0.0 copy-done
  23.9 0.5 %share.3.refs_3_ = f32[256,1024]{1,0:T(8,128)S(1)} custom-call(bf16[256,128]{1,0:T(8,128)(2,1)S(1)} %add.14.refs_0_, bf16[256,128]{1,0:T(8,128)(2,1)S(1)} %collective-permute-done.12.refs_1_, bf16[256,128]{1,0:T(8,128)(2,1)S(1)} %add.15.refs_2_, bf16[256,128]{1,0:T(8,128)(2,1)S(1)} %collective-permute-done.13.refs_3_, bf16[1024,1024]{1,0:T(8,128)(2,1)S(1)} %copy-done), custom_call_target="tpu_custom_call" | custom-call | flops 268435456 | bytes 524288 | tf_op jit(solution)/shard_map/share/pallas_call | solution.py:227
  24.4 0.0 collective-permute-done.11.refs_1_
  24.4 0.4 %share.4.refs_3_ = f32[256,1024]{1,0:T(8,128)S(1)} custom-call(bf16[256,128]{1,0:T(8,128)(2,1)S(1)} %collective-permute-done.10.refs_0_, bf16[256,128]{1,0:T(8,128)(2,1)S(1)} %collective-permute-done.11.refs_1_, bf16[1024,1024]{1,0:T(8,128)(2,1)S(1)} %copy-done, f32[256,1024]{1,0:T(8,128)S(1)} %share.3.refs_3_), custom_call_target="tpu_custom_call" | custom-call | flops 134217728 | bytes 524288 | tf_op jit(solution)/shard_map/share/pallas_call | solution.py:227
  24.8 0.1 collective-permute-done.9.refs_1_
  24.8 0.3 %share.5.s_ref = bf16[256,1024]{1,0:T(8,128)(2,1)S(1)} custom-call(bf16[256,128]{1,0:T(8,128)(2,1)S(1)} %collective-permute-done.8.refs_0_, bf16[256,128]{1,0:T(8,128)(2,1)S(1)} %collective-permute-done.9.refs_1_, bf16[1024,1024]{1,0:T(8,128)(2,1)S(1)} %copy-done, f32[256,1024]{1,0:T(8,128)S(1)} %share.4.refs_3_, f32[256,1024]{1,0:T(8,128)S(1)} %inverse.1.refs_0_.refs_4_), custom_call_target="tpu_custom_call" | custom-call | flops 134217728 | bytes 524288 | tf_op jit(solution)/shard_map/share/pallas_call | solution.py:227
  25.2 2.4 %weights.1 = bf16[2048,1024]{1,0:T(8,128)(2,1)} custom-call(bf16[2048,256]{1,0:T(8,128)(2,1)S(1)} %get-tuple-element.23.b_ref, bf16[256,1024]{1,0:T(8,128)(2,1)S(1)} %share.5.s_ref), custom_call_target="tpu_custom_call" | custom-call | flops 1073741824 | bytes 4194304 | tf_op jit(solution)/shard_map/weights/pallas_call | solution.py:256
  (8 shorter events, 0.1 us)
Async XLA Ops:
  2.0 1.4 %collective-permute-start.1 = (bf16[256,128]{1,0:T(8,128)(2,1)S(1)}, bf16[256,128]{1,0:T(8,128)(2,1)S(1)}, u32[]{:S(2)}, u32[]{:S(2)}) collective-permute-start(bf16[256,128]{1,0:T(8,128)(2,1)S(1)} %get-tuple-element.25.refs_0_), channel_id=1, source_target_pairs={{0,1},{1,0},{2,3},{3,2},{4,5},{5,4},{6,7},{7,6},{8,9},{9,8},{10,11... | collective-permute-start | bytes 196616 | tf_op jit(solution)/shard_map/ppermute | solution.py:276
  3.0 3.2 %collective-permute-start = (bf16[256,128]{1,0:T(8,128)(2,1)S(1)}, bf16[256,128]{1,0:T(8,128)(2,1)S(1)}, u32[]{:S(2)}, u32[]{:S(2)}) collective-permute-start(bf16[256,128]{1,0:T(8,128)(2,1)S(1)} %get-tuple-element.27.refs_0_), channel_id=1, source_target_pairs={{0,1},{1,0},{2,3},{3,2},{4,5},{5,4},{6,7},{7,6},{8,9},{9,8},{10,11... | collective-permute-start | bytes 196616 | tf_op jit(solution)/shard_map/ppermute | solution.py:276
  3.4 4.6 %collective-permute-start.3 = (bf16[256,128]{1,0:T(8,128)(2,1)S(1)}, bf16[256,128]{1,0:T(8,128)(2,1)S(1)}, u32[]{:S(2)}, u32[]{:S(2)}) collective-permute-start(bf16[256,128]{1,0:T(8,128)(2,1)S(1)} %get-tuple-element.29.refs_0_), channel_id=1, source_target_pairs={{0,3},{1,8},{2,11},{3,0},{4,7},{5,12},{6,15},{7,4},{8,1},{9,10},{1... | collective-permute-start | bytes 196616 | tf_op jit(solution)/shard_map/ppermute | solution.py:276
  6.2 4.3 %collective-permute-start.2 = (bf16[256,128]{1,0:T(8,128)(2,1)S(1)}, bf16[256,128]{1,0:T(8,128)(2,1)S(1)}, u32[]{:S(2)}, u32[]{:S(2)}) collective-permute-start(bf16[256,128]{1,0:T(8,128)(2,1)S(1)} %get-tuple-element.31.refs_0_), channel_id=1, source_target_pairs={{0,4},{1,8},{2,11},{3,7},{4,0},{5,12},{6,15},{7,3},{8,1},{9,13},{1... | collective-permute-start | bytes 196616 | tf_op jit(solution)/shard_map/ppermute | solution.py:276
  8.1 5.0 %collective-permute-start.5 = (bf16[256,128]{1,0:T(8,128)(2,1)S(1)}, bf16[256,128]{1,0:T(8,128)(2,1)S(1)}, u32[]{:S(2)}, u32[]{:S(2)}) collective-permute-start(bf16[256,128]{1,0:T(8,128)(2,1)S(1)} %get-tuple-element.33.refs_0_), channel_id=1, source_target_pairs={{0,4},{1,2},{2,1},{3,7},{4,0},{5,6},{6,5},{7,3},{8,11},{9,13},{10,... | collective-permute-start | bytes 196616 | tf_op jit(solution)/shard_map/ppermute | solution.py:276
  10.5 4.7 %collective-permute-start.4 = (bf16[256,128]{1,0:T(8,128)(2,1)S(1)}, bf16[256,128]{1,0:T(8,128)(2,1)S(1)}, u32[]{:S(2)}, u32[]{:S(2)}) collective-permute-start(bf16[256,128]{1,0:T(8,128)(2,1)S(1)} %get-tuple-element.35.refs_0_), channel_id=1, source_target_pairs={{0,9},{1,2},{2,1},{3,10},{4,13},{5,6},{6,5},{7,14},{8,11},{9,0},{1... | collective-permute-start | bytes 196616 | tf_op jit(solution)/shard_map/ppermute | solution.py:276
  13.1 4.8 %collective-permute-start.7 = (bf16[256,128]{1,0:T(8,128)(2,1)S(1)}, bf16[256,128]{1,0:T(8,128)(2,1)S(1)}, u32[]{:S(2)}, u32[]{:S(2)}) collective-permute-start(bf16[256,128]{1,0:T(8,128)(2,1)S(1)} %get-tuple-element.37.refs_0_), channel_id=1, source_target_pairs={{0,9},{1,5},{2,6},{3,10},{4,13},{5,1},{6,2},{7,14},{8,12},{9,0},{1... | collective-permute-start | bytes 196616 | tf_op jit(solution)/shard_map/ppermute | solution.py:276
  15.2 1.8 %copy-start.1 = (f32[8,16]{1,0:T(8,128)S(1)}, f32[8,16]{1,0:T(8,128)}, u32[]{:S(2)}) copy-start(f32[8,16]{1,0:T(8,128)} %table_ref.1) | copy-start | bytes 1540
  15.2 1.8 %copy-start.2 = (s32[1024]{0:T(1024)S(1)}, s32[1024]{0:T(1024)}, u32[]{:S(2)}) copy-start(s32[1024]{0:T(1024)} %param.11) | copy-start | bytes 12292
  15.2 1.8 %copy-start.3 = (s32[1024]{0:T(1024)S(1)}, s32[1024]{0:T(1024)}, u32[]{:S(2)}) copy-start(s32[1024]{0:T(1024)} %param.12) | copy-start | bytes 12292
  15.2 1.8 %copy-start.4 = (f32[256]{0:T(256)S(1)}, f32[256]{0:T(256)}, u32[]{:S(2)}) copy-start(f32[256]{0:T(256)} %param.10) | copy-start | bytes 3076
  15.2 4.3 %collective-permute-start.6 = (bf16[256,128]{1,0:T(8,128)(2,1)S(1)}, bf16[256,128]{1,0:T(8,128)(2,1)S(1)}, u32[]{:S(2)}, u32[]{:S(2)}) collective-permute-start(bf16[256,128]{1,0:T(8,128)(2,1)S(1)} %get-tuple-element.39.refs_0_), channel_id=1, source_target_pairs={{0,3},{1,5},{2,6},{3,0},{4,7},{5,1},{6,2},{7,4},{8,12},{9,10},{10,... | collective-permute-start | bytes 196616 | tf_op jit(solution)/shard_map/ppermute | solution.py:276
  17.9 4.3 %collective-permute-start.10 = (bf16[256,128]{1,0:T(8,128)(2,1)S(1)}, bf16[256,128]{1,0:T(8,128)(2,1)S(1)}, u32[]{:S(2)}, u32[]{:S(2)}) collective-permute-start(bf16[256,128]{1,0:T(8,128)(2,1)S(1)} %add.14.refs_0_), channel_id=1, source_target_pairs={{0,17},{1,16},{2,19},{3,18},{4,21},{5,20},{6,23},{7,22},{8,25},{9,... | collective-permute-start | bytes 196616 | tf_op jit(solution)/shard_map/ppermute | solution.py:276
  19.6 4.3 %copy-start = (bf16[1024,1024]{1,0:T(8,128)(2,1)S(1)}, bf16[1024,1024]{1,0:T(8,128)(2,1)}, u32[]{:S(2)}) copy-start(bf16[1024,1024]{1,0:T(8,128)(2,1)} %refs_2_.3) | copy-start | bytes 6291460
  19.6 4.0 %collective-permute-start.8 = (bf16[256,128]{1,0:T(8,128)(2,1)S(1)}, bf16[256,128]{1,0:T(8,128)(2,1)S(1)}, u32[]{:S(2)}, u32[]{:S(2)}) collective-permute-start(bf16[256,128]{1,0:T(8,128)(2,1)S(1)} %add.15.refs_2_), channel_id=1, source_target_pairs={{0,17},{1,16},{2,19},{3,18},{4,21},{5,20},{6,23},{7,22},{8,25},{9,... | collective-permute-start | bytes 196616 | tf_op jit(solution)/shard_map/ppermute | solution.py:276
  21.0 2.9 %collective-permute-start.13 = (bf16[256,128]{1,0:T(8,128)(2,1)S(1)}, bf16[256,128]{1,0:T(8,128)(2,1)S(1)}, u32[]{:S(2)}, u32[]{:S(2)}) collective-permute-start(bf16[256,128]{1,0:T(8,128)(2,1)S(1)} %add.15.refs_2_), channel_id=1, source_target_pairs={{0,1},{1,0},{2,3},{3,2},{4,5},{5,4},{6,7},{7,6},{8,9},{9,8},{10,11... | collective-permute-start | bytes 196616 | tf_op jit(solution)/shard_map/ppermute | solution.py:276
  21.8 2.1 %collective-permute-start.12 = (bf16[256,128]{1,0:T(8,128)(2,1)S(1)}, bf16[256,128]{1,0:T(8,128)(2,1)S(1)}, u32[]{:S(2)}, u32[]{:S(2)}) collective-permute-start(bf16[256,128]{1,0:T(8,128)(2,1)S(1)} %add.14.refs_0_), channel_id=1, source_target_pairs={{0,1},{1,0},{2,3},{3,2},{4,5},{5,4},{6,7},{7,6},{8,9},{9,8},{10,11... | collective-permute-start | bytes 196616 | tf_op jit(solution)/shard_map/ppermute | solution.py:276
  22.2 2.2 %collective-permute-start.11 = (bf16[256,128]{1,0:T(8,128)(2,1)S(1)}, bf16[256,128]{1,0:T(8,128)(2,1)S(1)}, u32[]{:S(2)}, u32[]{:S(2)}) collective-permute-start(bf16[256,128]{1,0:T(8,128)(2,1)S(1)} %collective-permute-done.10.refs_0_), channel_id=1, source_target_pairs={{0,1},{1,0},{2,3},{3,2},{4,5},{5,4},{6,7},{7,6},{8,9},{9,8},{10,11... | collective-permute-start | bytes 196616 | tf_op jit(solution)/shard_map/ppermute | solution.py:276
  23.6 1.3 %collective-permute-start.9 = (bf16[256,128]{1,0:T(8,128)(2,1)S(1)}, bf16[256,128]{1,0:T(8,128)(2,1)S(1)}, u32[]{:S(2)}, u32[]{:S(2)}) collective-permute-start(bf16[256,128]{1,0:T(8,128)(2,1)S(1)} %collective-permute-done.8.refs_0_), channel_id=1, source_target_pairs={{0,1},{1,0},{2,3},{3,2},{4,5},{5,4},{6,7},{7,6},{8,9},{9,8},{10,11... | collective-permute-start | bytes 196616 | tf_op jit(solution)/shard_map/ppermute | solution.py:276

commit v7 on v6

--- a/solution.py
+++ b/solution.py
@@ -11,6 +11,7 @@
 BF16 = jnp.bfloat16
 MIB = 1 << 20
 CHAINS = 2
+BLOCKS = (1, 2, 2, 2, 2, 2, 2, 2, 1)
 EIG_FLIP = 10
 GROUP_FLIP = 1
 FIRST = 8
@@ -235,12 +236,25 @@
     )(*pieces, responses, *extra)
 
 
-def weights_kernel(b_ref, s_ref, out_hbm, out_ref, sems):
-    parts = sems.shape[0]
-    chunk = b_ref.shape[0] // parts
+def weights_kernel(m, at, own_ref, got_ref, r_ref, before_ref, inverse_ref, b_ref, out_hbm, s_ref, out_ref, sems):
+    group = lax.axis_index("groups")
+    first = half_index() == 0
+    own, got = own_ref[...], got_ref[...]
+    piece = jnp.concatenate([jnp.where(first, own, got), jnp.where(first, got, own)], axis=1)
+    times = r_ref.shape[0] // lax.axis_size("groups")
+    start = pl.multiple_of((group ^ m) * times + at, 16)
+    term = lax.dot_general(
+        piece,
+        r_ref[pl.ds(start, piece.shape[0]), :],
+        (((0,), (0,)), ((), ())),
+        preferred_element_type=F32,
+    )
+    s_ref[...] = ((before_ref[...] + term) * inverse_ref[...]).astype(BF16)
     copies = []
-    for i in range(parts):
-        rows = pl.ds(i * chunk, chunk)
+    at = 0
+    for i, size in enumerate(BLOCKS):
+        rows = pl.ds(at * b_ref.shape[0] // 16, size * b_ref.shape[0] // 16)
+        at += size
         out_ref[rows, :] = jnp.dot(b_ref[rows, :], s_ref[...], preferred_element_type=F32).astype(BF16)
         copy = pltpu.make_async_copy(out_ref.at[rows], out_hbm.at[rows], sems.at[i])
         copy.start()
@@ -249,20 +263,23 @@
         copy.wait()
 
 
-def weights(basis, scaled):
+def weights(place, pieces, responses, before, inv, basis):
     feats, k = basis.shape
-    vox = scaled.shape[1]
-    parts = 8
-    return pl.pallas_call(
-        weights_kernel,
-        in_specs=[VMEM, VMEM],
+    vox = responses.shape[1]
+    return pl.pallas_call(
+        functools.partial(weights_kernel, *place),
+        in_specs=[VMEM] * 6,
         out_specs=HBM,
         out_shape=jax.ShapeDtypeStruct((feats, vox), BF16),
-        scratch_shapes=[pltpu.VMEM((feats, vox), BF16), pltpu.SemaphoreType.DMA((parts,))],
-        compiler_params=params(16),
+        scratch_shapes=[
+            pltpu.VMEM((k, vox), BF16),
+            pltpu.VMEM((feats, vox), BF16),
+            pltpu.SemaphoreType.DMA((len(BLOCKS),)),
+        ],
+        compiler_params=params(24),
         cost_estimate=cost(2 * feats * k * vox, 2 * feats * vox),
         name="weights",
-    )(basis, scaled)
+    )(*pieces, responses, before, inv, basis)
 
 
 def swap(value, group_mask, eig_masks):
@@ -323,8 +340,10 @@
         pieces = []
         for m, i in batch:
             pieces += [blocks[m][i], swap(blocks[m][i], 0, (1, 1))]
-        total = share([(m, offsets[i]) for m, i in batch], pieces, responses, total, inv if batch is batches[-1] else None)
-    return weights(panel, total)
+        if batch is not batches[-1]:
+            total = share([(m, offsets[i]) for m, i in batch], pieces, responses, total)
+    (m, i), = batches[-1]
+    return weights((m, offsets[i]), pieces, responses, total, inv, panel)
 
 
 def solution(mesh):

time: 27.7 us -> 27.6 us (level)
    pallas_call x3 -> x2, Pallas kernels: 1.21 us -> 0.87 us  [share(): pl.pallas_call(functools.partial(share_kernel, places, before is not None...]
    pallas_call x1, Pallas kernels: 2.38 us -> 2.66 us  [weights(): pl.pallas_call(functools.partial(weights_kernel, *place), in_specs=[VMEM]...]
where the time goes in v7:
time: 27.6 us; the launch traced here: 27.5 us
  starting transfers between devices  16.5 us (60%)
  Pallas kernels  6.4 us (23%)
  waiting for transfers between devices  4.44 us (16%)
    ppermute x14, starting transfers between devices, swap(): return lax.ppermute(value, ('groups', 'eig'), pairs)  16.5 us
    ppermute x14, waiting for transfers between devices, swap(): return lax.ppermute(value, ('groups', 'eig'), pairs)  4.44 us
    pallas_call x1, Pallas kernels, weights(): pl.pallas_call(functools.partial(weights_kernel, *place), in_specs=[VMEM]...  2.66 us
    pallas_call x1, Pallas kernels, gram_first(): pl.pallas_call(gram_first_kernel, in_specs=[HBM, HBM], out_specs=[VMEM] *...  2 us
    pallas_call x2, Pallas kernels, share(): pl.pallas_call(functools.partial(share_kernel, places, before is not None...  0.87 us
  transfers between devices with their start and end apart: 14, of which 9 were waited for; matrix products, arithmetic and copies ran while one was open for 0% of the time, Pallas kernels for 6%

profile of v7, /device:TPU:0, one launch (start us, length us, event | category | flops | bytes accessed | tf_op | source)
XLA Modules:
  0.0 27.5 jit_solution(6186824187355088072)
XLA Ops:
  0.0 2.0 %gram_first.1 = (f32[256,128]{1,0:T(8,128)S(1)}, bf16[256,128]{1,0:T(8,128)(2,1)S(1)}, bf16[256,2048]{1,0:T(8,128)(2,1)S(1)}, bf16[2048,256]{1,0:T(8,128)(2,1)S(1)}) custom-call(bf16[1024,2048]{1,0:T(8,128)(2,1)} %f_hbm.1, bf16[2048,256]{1,0:T(8,128)(2,1)} %b_hbm.1), custom_call_target="tpu_custom_call" | custom-call | flops 268435456 | bytes 2097152 | tf_op jit(solution)/shard_map/gram_first/pallas_call | solution.py:103
  2.0 0.5 %collective-permute-start.1 = (bf16[256,128]{1,0:T(8,128)(2,1)S(1)}, bf16[256,128]{1,0:T(8,128)(2,1)S(1)}, u32[]{:S(2)}, u32[]{:S(2)}) collective-permute-start(bf16[256,128]{1,0:T(8,128)(2,1)S(1)} %get-tuple-element.25.refs_0_), channel_id=1, source_target_pairs={{0,1},{1,0},{2,3},{3,2},{4,5},{5,4},{6,7},{7,6},{8,9},{9,8},{10,11... | collective-permute-start | bytes 196616 | tf_op jit(solution)/shard_map/ppermute | solution.py:293
  2.5 0.4 %gram_rest.1 = (f32[256,128]{1,0:T(8,128)S(1)}, bf16[256,128]{1,0:T(8,128)(2,1)S(1)}) custom-call(bf16[256,2048]{1,0:T(8,128)(2,1)S(1)} %get-tuple-element.23.f_ref, bf16[2048,256]{1,0:T(8,128)(2,1)S(1)} %get-tuple-element.24.b_ref, bf16[256,128]{1,0:T(8,128)(2,1)S(1)} %get-tuple-element.25.refs_0_), custom_call_target="tpu_custom_call" | custom-call | flops 268435456 | bytes 2097152 | tf_op jit(solution)/shard_map/gram_rest/pallas_call | solution.py:128
  3.0 0.1 collective-permute-start
  3.1 0.3 %collective-permute-done.1.got_ref = bf16[256,128]{1,0:T(8,128)(2,1)S(1)} collective-permute-done((bf16[256,128]{1,0:T(8,128)(2,1)S(1)}, bf16[256,128]{1,0:T(8,128)(2,1)S(1)}, u32[]{:S(2)}, u32[]{:S(2)}) %collective-permute-start.1) | collective-permute-done | bytes 65568 | tf_op jit(solution)/shard_map/ppermute | solution.py:293
  3.4 2.7 %collective-permute-start.3 = (bf16[256,128]{1,0:T(8,128)(2,1)S(1)}, bf16[256,128]{1,0:T(8,128)(2,1)S(1)}, u32[]{:S(2)}, u32[]{:S(2)}) collective-permute-start(bf16[256,128]{1,0:T(8,128)(2,1)S(1)} %get-tuple-element.29.refs_0_), channel_id=1, source_target_pairs={{0,3},{1,8},{2,11},{3,0},{4,7},{5,12},{6,15},{7,4},{8,1},{9,10},{1... | collective-permute-start | bytes 196616 | tf_op jit(solution)/shard_map/ppermute | solution.py:293
  6.1 0.0 collective-permute-done.got_ref
  6.2 1.6 %collective-permute-start.2 = (bf16[256,128]{1,0:T(8,128)(2,1)S(1)}, bf16[256,128]{1,0:T(8,128)(2,1)S(1)}, u32[]{:S(2)}, u32[]{:S(2)}) collective-permute-start(bf16[256,128]{1,0:T(8,128)(2,1)S(1)} %get-tuple-element.31.refs_0_), channel_id=1, source_target_pairs={{0,4},{1,8},{2,11},{3,7},{4,0},{5,12},{6,15},{7,3},{8,1},{9,13},{1... | collective-permute-start | bytes 196616 | tf_op jit(solution)/shard_map/ppermute | solution.py:293
  7.8 0.3 %collective-permute-done.3.got_ref = bf16[256,128]{1,0:T(8,128)(2,1)S(1)} collective-permute-done((bf16[256,128]{1,0:T(8,128)(2,1)S(1)}, bf16[256,128]{1,0:T(8,128)(2,1)S(1)}, u32[]{:S(2)}, u32[]{:S(2)}) %collective-permute-start.3) | collective-permute-done | bytes 65568 | tf_op jit(solution)/shard_map/ppermute | solution.py:293
  8.1 2.1 %collective-permute-start.5 = (bf16[256,128]{1,0:T(8,128)(2,1)S(1)}, bf16[256,128]{1,0:T(8,128)(2,1)S(1)}, u32[]{:S(2)}, u32[]{:S(2)}) collective-permute-start(bf16[256,128]{1,0:T(8,128)(2,1)S(1)} %get-tuple-element.33.refs_0_), channel_id=1, source_target_pairs={{0,4},{1,2},{2,1},{3,7},{4,0},{5,6},{6,5},{7,3},{8,11},{9,13},{10,... | collective-permute-start | bytes 196616 | tf_op jit(solution)/shard_map/ppermute | solution.py:293
  10.2 0.3 %collective-permute-done.2.got_ref = bf16[256,128]{1,0:T(8,128)(2,1)S(1)} collective-permute-done((bf16[256,128]{1,0:T(8,128)(2,1)S(1)}, bf16[256,128]{1,0:T(8,128)(2,1)S(1)}, u32[]{:S(2)}, u32[]{:S(2)}) %collective-permute-start.2) | collective-permute-done | bytes 65568 | tf_op jit(solution)/shard_map/ppermute | solution.py:293
  10.5 2.2 %collective-permute-start.4 = (bf16[256,128]{1,0:T(8,128)(2,1)S(1)}, bf16[256,128]{1,0:T(8,128)(2,1)S(1)}, u32[]{:S(2)}, u32[]{:S(2)}) collective-permute-start(bf16[256,128]{1,0:T(8,128)(2,1)S(1)} %get-tuple-element.35.refs_0_), channel_id=1, source_target_pairs={{0,9},{1,2},{2,1},{3,10},{4,13},{5,6},{6,5},{7,14},{8,11},{9,0},{1... | collective-permute-start | bytes 196616 | tf_op jit(solution)/shard_map/ppermute | solution.py:293
  12.7 0.5 %collective-permute-done.5.got_ref = bf16[256,128]{1,0:T(8,128)(2,1)S(1)} collective-permute-done((bf16[256,128]{1,0:T(8,128)(2,1)S(1)}, bf16[256,128]{1,0:T(8,128)(2,1)S(1)}, u32[]{:S(2)}, u32[]{:S(2)}) %collective-permute-start.5) | collective-permute-done | bytes 65568 | tf_op jit(solution)/shard_map/ppermute | solution.py:293
  13.1 1.3 %collective-permute-start.7 = (bf16[256,128]{1,0:T(8,128)(2,1)S(1)}, bf16[256,128]{1,0:T(8,128)(2,1)S(1)}, u32[]{:S(2)}, u32[]{:S(2)}) collective-permute-start(bf16[256,128]{1,0:T(8,128)(2,1)S(1)} %get-tuple-element.37.refs_0_), channel_id=1, source_target_pairs={{0,9},{1,5},{2,6},{3,10},{4,13},{5,1},{6,2},{7,14},{8,12},{9,0},{1... | collective-permute-start | bytes 196616 | tf_op jit(solution)/shard_map/ppermute | solution.py:293
  14.5 0.7 %collective-permute-done.4.got_ref = bf16[256,128]{1,0:T(8,128)(2,1)S(1)} collective-permute-done((bf16[256,128]{1,0:T(8,128)(2,1)S(1)}, bf16[256,128]{1,0:T(8,128)(2,1)S(1)}, u32[]{:S(2)}, u32[]{:S(2)}) %collective-permute-start.4) | collective-permute-done | bytes 65568 | tf_op jit(solution)/shard_map/ppermute | solution.py:293
  15.2 0.0 copy-start.1
  15.2 0.0 copy-start.2
  15.2 0.0 copy-start.3
  15.2 0.0 copy-start.4
  15.2 1.7 %collective-permute-start.6 = (bf16[256,128]{1,0:T(8,128)(2,1)S(1)}, bf16[256,128]{1,0:T(8,128)(2,1)S(1)}, u32[]{:S(2)}, u32[]{:S(2)}) collective-permute-start(bf16[256,128]{1,0:T(8,128)(2,1)S(1)} %get-tuple-element.39.refs_0_), channel_id=1, source_target_pairs={{0,3},{1,5},{2,6},{3,0},{4,7},{5,1},{6,2},{7,4},{8,12},{9,10},{10,... | collective-permute-start | bytes 196616 | tf_op jit(solution)/shard_map/ppermute | solution.py:293
  16.9 0.0 copy-done.1
  16.9 0.0 copy-done.2
  16.9 0.0 copy-done.3
  16.9 0.0 copy-done.4
  17.0 0.3 %inverse.1.refs_0_.inverse_ref = f32[256,1024]{1,0:T(8,128)S(1)} custom-call(f32[8,16]{1,0:T(8,128)S(1)} %copy-done.1, s32[1,1024]{1,0:T(1,128)S(1)} %bitcast.3, s32[1,1024]{1,0:T(1,128)S(1)} %bitcast.4, f32[1,256]{1,0:T(1,128)S(1)} %bitcast.5, bf16[256,128]{1,0:T(8,128)(2,1)S(1)} %get-tuple-element.39.refs_0_), custom_call_target="tpu_custom_call" | custom-call | flops 2097152 | bytes 524288 | tf_op jit(solution)/shard_map/inverse/pallas_call | solution.py:164
  17.3 0.7 %collective-permute-done.7.got_ref = bf16[256,128]{1,0:T(8,128)(2,1)S(1)} collective-permute-done((bf16[256,128]{1,0:T(8,128)(2,1)S(1)}, bf16[256,128]{1,0:T(8,128)(2,1)S(1)}, u32[]{:S(2)}, u32[]{:S(2)}) %collective-permute-start.7) | collective-permute-done | bytes 65568 | tf_op jit(solution)/shard_map/ppermute | solution.py:293
  17.9 1.6 %collective-permute-start.10 = (bf16[256,128]{1,0:T(8,128)(2,1)S(1)}, bf16[256,128]{1,0:T(8,128)(2,1)S(1)}, u32[]{:S(2)}, u32[]{:S(2)}) collective-permute-start(bf16[256,128]{1,0:T(8,128)(2,1)S(1)} %add.14.refs_0_), channel_id=1, source_target_pairs={{0,17},{1,16},{2,19},{3,18},{4,21},{5,20},{6,23},{7,22},{8,25},{9,... | collective-permute-start | bytes 196616 | tf_op jit(solution)/shard_map/ppermute | solution.py:293
  19.6 0.0 collective-permute-done.6.got_ref
  19.6 0.0 copy-start
  19.6 1.4 %collective-permute-start.8 = (bf16[256,128]{1,0:T(8,128)(2,1)S(1)}, bf16[256,128]{1,0:T(8,128)(2,1)S(1)}, u32[]{:S(2)}, u32[]{:S(2)}) collective-permute-start(bf16[256,128]{1,0:T(8,128)(2,1)S(1)} %add.15.refs_2_), channel_id=1, source_target_pairs={{0,17},{1,16},{2,19},{3,18},{4,21},{5,20},{6,23},{7,22},{8,25},{9,... | collective-permute-start | bytes 196616 | tf_op jit(solution)/shard_map/ppermute | solution.py:293
  21.0 0.8 %collective-permute-start.13 = (bf16[256,128]{1,0:T(8,128)(2,1)S(1)}, bf16[256,128]{1,0:T(8,128)(2,1)S(1)}, u32[]{:S(2)}, u32[]{:S(2)}) collective-permute-start(bf16[256,128]{1,0:T(8,128)(2,1)S(1)} %add.15.refs_2_), channel_id=1, source_target_pairs={{0,1},{1,0},{2,3},{3,2},{4,5},{5,4},{6,7},{7,6},{8,9},{9,8},{10,11... | collective-permute-start | bytes 196616 | tf_op jit(solution)/shard_map/ppermute | solution.py:293
  21.8 0.0 collective-permute-start.12
  21.8 0.4 %collective-permute-done.10.refs_0_ = bf16[256,128]{1,0:T(8,128)(2,1)S(1)} collective-permute-done((bf16[256,128]{1,0:T(8,128)(2,1)S(1)}, bf16[256,128]{1,0:T(8,128)(2,1)S(1)}, u32[]{:S(2)}, u32[]{:S(2)}) %collective-permute-start.10) | collective-permute-done | bytes 65568 | tf_op jit(solution)/shard_map/ppermute | solution.py:293
  22.2 0.1 collective-permute-start.11
  22.3 1.2 %collective-permute-done.8.own_ref = bf16[256,128]{1,0:T(8,128)(2,1)S(1)} collective-permute-done((bf16[256,128]{1,0:T(8,128)(2,1)S(1)}, bf16[256,128]{1,0:T(8,128)(2,1)S(1)}, u32[]{:S(2)}, u32[]{:S(2)}) %collective-permute-start.8) | collective-permute-done | bytes 65568 | tf_op jit(solution)/shard_map/ppermute | solution.py:293
  23.6 0.3 %collective-permute-start.9 = (bf16[256,128]{1,0:T(8,128)(2,1)S(1)}, bf16[256,128]{1,0:T(8,128)(2,1)S(1)}, u32[]{:S(2)}, u32[]{:S(2)}) collective-permute-start(bf16[256,128]{1,0:T(8,128)(2,1)S(1)} %collective-permute-done.8.own_ref), channel_id=1, source_target_pairs={{0,1},{1,0},{2,3},{3,2},{4,5},{5,4},{6,7},{7,6},{8,9},{9,8},{10,11... | collective-permute-start | bytes 196616 | tf_op jit(solution)/shard_map/ppermute | solution.py:293
  23.9 0.0 collective-permute-done.13.refs_3_
  23.9 0.0 collective-permute-done.12.refs_1_
  23.9 0.0 copy-done
  23.9 0.5 %share.2.refs_3_ = f32[256,1024]{1,0:T(8,128)S(1)} custom-call(bf16[256,128]{1,0:T(8,128)(2,1)S(1)} %add.14.refs_0_, bf16[256,128]{1,0:T(8,128)(2,1)S(1)} %collective-permute-done.12.refs_1_, bf16[256,128]{1,0:T(8,128)(2,1)S(1)} %add.15.refs_2_, bf16[256,128]{1,0:T(8,128)(2,1)S(1)} %collective-permute-done.13.refs_3_, bf16[1024,1024]{1,0:T(8,128)(2,1)S(1)} %copy-done), custom_call_target="tpu_custom_call" | custom-call | flops 268435456 | bytes 524288 | tf_op jit(solution)/shard_map/share/pallas_call | solution.py:228
  24.4 0.0 collective-permute-done.11.refs_1_
  24.4 0.4 %share.3.before_ref = f32[256,1024]{1,0:T(8,128)S(1)} custom-call(bf16[256,128]{1,0:T(8,128)(2,1)S(1)} %collective-permute-done.10.refs_0_, bf16[256,128]{1,0:T(8,128)(2,1)S(1)} %collective-permute-done.11.refs_1_, bf16[1024,1024]{1,0:T(8,128)(2,1)S(1)} %copy-done, f32[256,1024]{1,0:T(8,128)S(1)} %share.2.refs_3_), custom_call_target="tpu_custom_call" | custom-call | flops 134217728 | bytes 524288 | tf_op jit(solution)/shard_map/share/pallas_call | solution.py:228
  24.8 0.1 collective-permute-done.9.got_ref
  24.8 2.7 %weights.1 = bf16[2048,1024]{1,0:T(8,128)(2,1)} custom-call(bf16[256,128]{1,0:T(8,128)(2,1)S(1)} %collective-permute-done.8.own_ref, bf16[256,128]{1,0:T(8,128)(2,1)S(1)} %collective-permute-done.9.got_ref, bf16[1024,1024]{1,0:T(8,128)(2,1)S(1)} %copy-done, f32[256,1024]{1,0:T(8,128)S(1)} %share.3.before_ref, f32[256,1024]{1,0:T(8,128)S(1)} %inverse.1.refs_0_.inverse_ref, ...), custom_call_target="tpu_custom_call" | custom-call | flops 1073741824 | bytes 4194304 | tf_op jit(solution)/shard_map/weights/pallas_call | solution.py:269
  (8 shorter events, 0.1 us)
Async XLA Ops:
  2.0 1.4 %collective-permute-start.1 = (bf16[256,128]{1,0:T(8,128)(2,1)S(1)}, bf16[256,128]{1,0:T(8,128)(2,1)S(1)}, u32[]{:S(2)}, u32[]{:S(2)}) collective-permute-start(bf16[256,128]{1,0:T(8,128)(2,1)S(1)} %get-tuple-element.25.refs_0_), channel_id=1, source_target_pairs={{0,1},{1,0},{2,3},{3,2},{4,5},{5,4},{6,7},{7,6},{8,9},{9,8},{10,11... | collective-permute-start | bytes 196616 | tf_op jit(solution)/shard_map/ppermute | solution.py:293
  3.0 3.2 %collective-permute-start = (bf16[256,128]{1,0:T(8,128)(2,1)S(1)}, bf16[256,128]{1,0:T(8,128)(2,1)S(1)}, u32[]{:S(2)}, u32[]{:S(2)}) collective-permute-start(bf16[256,128]{1,0:T(8,128)(2,1)S(1)} %get-tuple-element.27.refs_0_), channel_id=1, source_target_pairs={{0,1},{1,0},{2,3},{3,2},{4,5},{5,4},{6,7},{7,6},{8,9},{9,8},{10,11... | collective-permute-start | bytes 196616 | tf_op jit(solution)/shard_map/ppermute | solution.py:293
  3.4 4.6 %collective-permute-start.3 = (bf16[256,128]{1,0:T(8,128)(2,1)S(1)}, bf16[256,128]{1,0:T(8,128)(2,1)S(1)}, u32[]{:S(2)}, u32[]{:S(2)}) collective-permute-start(bf16[256,128]{1,0:T(8,128)(2,1)S(1)} %get-tuple-element.29.refs_0_), channel_id=1, source_target_pairs={{0,3},{1,8},{2,11},{3,0},{4,7},{5,12},{6,15},{7,4},{8,1},{9,10},{1... | collective-permute-start | bytes 196616 | tf_op jit(solution)/shard_map/ppermute | solution.py:293
  6.2 4.3 %collective-permute-start.2 = (bf16[256,128]{1,0:T(8,128)(2,1)S(1)}, bf16[256,128]{1,0:T(8,128)(2,1)S(1)}, u32[]{:S(2)}, u32[]{:S(2)}) collective-permute-start(bf16[256,128]{1,0:T(8,128)(2,1)S(1)} %get-tuple-element.31.refs_0_), channel_id=1, source_target_pairs={{0,4},{1,8},{2,11},{3,7},{4,0},{5,12},{6,15},{7,3},{8,1},{9,13},{1... | collective-permute-start | bytes 196616 | tf_op jit(solution)/shard_map/ppermute | solution.py:293
  8.1 5.0 %collective-permute-start.5 = (bf16[256,128]{1,0:T(8,128)(2,1)S(1)}, bf16[256,128]{1,0:T(8,128)(2,1)S(1)}, u32[]{:S(2)}, u32[]{:S(2)}) collective-permute-start(bf16[256,128]{1,0:T(8,128)(2,1)S(1)} %get-tuple-element.33.refs_0_), channel_id=1, source_target_pairs={{0,4},{1,2},{2,1},{3,7},{4,0},{5,6},{6,5},{7,3},{8,11},{9,13},{10,... | collective-permute-start | bytes 196616 | tf_op jit(solution)/shard_map/ppermute | solution.py:293
  10.5 4.7 %collective-permute-start.4 = (bf16[256,128]{1,0:T(8,128)(2,1)S(1)}, bf16[256,128]{1,0:T(8,128)(2,1)S(1)}, u32[]{:S(2)}, u32[]{:S(2)}) collective-permute-start(bf16[256,128]{1,0:T(8,128)(2,1)S(1)} %get-tuple-element.35.refs_0_), channel_id=1, source_target_pairs={{0,9},{1,2},{2,1},{3,10},{4,13},{5,6},{6,5},{7,14},{8,11},{9,0},{1... | collective-permute-start | bytes 196616 | tf_op jit(solution)/shard_map/ppermute | solution.py:293
  13.1 4.8 %collective-permute-start.7 = (bf16[256,128]{1,0:T(8,128)(2,1)S(1)}, bf16[256,128]{1,0:T(8,128)(2,1)S(1)}, u32[]{:S(2)}, u32[]{:S(2)}) collective-permute-start(bf16[256,128]{1,0:T(8,128)(2,1)S(1)} %get-tuple-element.37.refs_0_), channel_id=1, source_target_pairs={{0,9},{1,5},{2,6},{3,10},{4,13},{5,1},{6,2},{7,14},{8,12},{9,0},{1... | collective-permute-start | bytes 196616 | tf_op jit(solution)/shard_map/ppermute | solution.py:293
  15.2 1.8 %copy-start.1 = (f32[8,16]{1,0:T(8,128)S(1)}, f32[8,16]{1,0:T(8,128)}, u32[]{:S(2)}) copy-start(f32[8,16]{1,0:T(8,128)} %table_ref.1) | copy-start | bytes 1540
  15.2 1.8 %copy-start.2 = (s32[1024]{0:T(1024)S(1)}, s32[1024]{0:T(1024)}, u32[]{:S(2)}) copy-start(s32[1024]{0:T(1024)} %param.11) | copy-start | bytes 12292
  15.2 1.8 %copy-start.3 = (s32[1024]{0:T(1024)S(1)}, s32[1024]{0:T(1024)}, u32[]{:S(2)}) copy-start(s32[1024]{0:T(1024)} %param.12) | copy-start | bytes 12292
  15.2 1.8 %copy-start.4 = (f32[256]{0:T(256)S(1)}, f32[256]{0:T(256)}, u32[]{:S(2)}) copy-start(f32[256]{0:T(256)} %param.10) | copy-start | bytes 3076
  15.2 4.3 %collective-permute-start.6 = (bf16[256,128]{1,0:T(8,128)(2,1)S(1)}, bf16[256,128]{1,0:T(8,128)(2,1)S(1)}, u32[]{:S(2)}, u32[]{:S(2)}) collective-permute-start(bf16[256,128]{1,0:T(8,128)(2,1)S(1)} %get-tuple-element.39.refs_0_), channel_id=1, source_target_pairs={{0,3},{1,5},{2,6},{3,0},{4,7},{5,1},{6,2},{7,4},{8,12},{9,10},{10,... | collective-permute-start | bytes 196616 | tf_op jit(solution)/shard_map/ppermute | solution.py:293
  17.9 4.3 %collective-permute-start.10 = (bf16[256,128]{1,0:T(8,128)(2,1)S(1)}, bf16[256,128]{1,0:T(8,128)(2,1)S(1)}, u32[]{:S(2)}, u32[]{:S(2)}) collective-permute-start(bf16[256,128]{1,0:T(8,128)(2,1)S(1)} %add.14.refs_0_), channel_id=1, source_target_pairs={{0,17},{1,16},{2,19},{3,18},{4,21},{5,20},{6,23},{7,22},{8,25},{9,... | collective-permute-start | bytes 196616 | tf_op jit(solution)/shard_map/ppermute | solution.py:293
  19.6 4.3 %copy-start = (bf16[1024,1024]{1,0:T(8,128)(2,1)S(1)}, bf16[1024,1024]{1,0:T(8,128)(2,1)}, u32[]{:S(2)}) copy-start(bf16[1024,1024]{1,0:T(8,128)(2,1)} %r_ref.1) | copy-start | bytes 6291460
  19.6 4.0 %collective-permute-start.8 = (bf16[256,128]{1,0:T(8,128)(2,1)S(1)}, bf16[256,128]{1,0:T(8,128)(2,1)S(1)}, u32[]{:S(2)}, u32[]{:S(2)}) collective-permute-start(bf16[256,128]{1,0:T(8,128)(2,1)S(1)} %add.15.refs_2_), channel_id=1, source_target_pairs={{0,17},{1,16},{2,19},{3,18},{4,21},{5,20},{6,23},{7,22},{8,25},{9,... | collective-permute-start | bytes 196616 | tf_op jit(solution)/shard_map/ppermute | solution.py:293
  21.0 2.9 %collective-permute-start.13 = (bf16[256,128]{1,0:T(8,128)(2,1)S(1)}, bf16[256,128]{1,0:T(8,128)(2,1)S(1)}, u32[]{:S(2)}, u32[]{:S(2)}) collective-permute-start(bf16[256,128]{1,0:T(8,128)(2,1)S(1)} %add.15.refs_2_), channel_id=1, source_target_pairs={{0,1},{1,0},{2,3},{3,2},{4,5},{5,4},{6,7},{7,6},{8,9},{9,8},{10,11... | collective-permute-start | bytes 196616 | tf_op jit(solution)/shard_map/ppermute | solution.py:293
  21.8 2.1 %collective-permute-start.12 = (bf16[256,128]{1,0:T(8,128)(2,1)S(1)}, bf16[256,128]{1,0:T(8,128)(2,1)S(1)}, u32[]{:S(2)}, u32[]{:S(2)}) collective-permute-start(bf16[256,128]{1,0:T(8,128)(2,1)S(1)} %add.14.refs_0_), channel_id=1, source_target_pairs={{0,1},{1,0},{2,3},{3,2},{4,5},{5,4},{6,7},{7,6},{8,9},{9,8},{10,11... | collective-permute-start | bytes 196616 | tf_op jit(solution)/shard_map/ppermute | solution.py:293
  22.2 2.2 %collective-permute-start.11 = (bf16[256,128]{1,0:T(8,128)(2,1)S(1)}, bf16[256,128]{1,0:T(8,128)(2,1)S(1)}, u32[]{:S(2)}, u32[]{:S(2)}) collective-permute-start(bf16[256,128]{1,0:T(8,128)(2,1)S(1)} %collective-permute-done.10.refs_0_), channel_id=1, source_target_pairs={{0,1},{1,0},{2,3},{3,2},{4,5},{5,4},{6,7},{7,6},{8,9},{9,8},{10,11... | collective-permute-start | bytes 196616 | tf_op jit(solution)/shard_map/ppermute | solution.py:293
  23.6 1.3 %collective-permute-start.9 = (bf16[256,128]{1,0:T(8,128)(2,1)S(1)}, bf16[256,128]{1,0:T(8,128)(2,1)S(1)}, u32[]{:S(2)}, u32[]{:S(2)}) collective-permute-start(bf16[256,128]{1,0:T(8,128)(2,1)S(1)} %collective-permute-done.8.own_ref), channel_id=1, source_target_pairs={{0,1},{1,0},{2,3},{3,2},{4,5},{5,4},{6,7},{7,6},{8,9},{9,8},{10,11... | collective-permute-start | bytes 196616 | tf_op jit(solution)/shard_map/ppermute | solution.py:293

commit v8 on v7

--- a/solution.py
+++ b/solution.py
@@ -59,7 +59,7 @@
     low, high = total[:, :half], total[:, half:]
     first = half_index() == 0
     kept_ref[...] = jnp.where(first, low, high)
-    sent_ref[...] = jnp.where(first, high, low).astype(BF16)
+    sent_ref[...] = jnp.where(first, high, low).astype(sent_ref.dtype)
 
 
 def gram_first_kernel(f_hbm, b_hbm, kept_ref, sent_ref, rest_ref, b_ref, f_ref, f_sem, b_sem, rest_sem):
@@ -106,7 +106,7 @@
         out_specs=[VMEM] * 4,
         out_shape=[
             jax.ShapeDtypeStruct((rows, k // 2), F32),
-            jax.ShapeDtypeStruct((rows, k // 2), BF16),
+            jax.ShapeDtypeStruct((rows, k // 2), F32),
             jax.ShapeDtypeStruct((more, feats), BF16),
             jax.ShapeDtypeStruct((feats, k), BF16),
         ],
@@ -131,7 +131,7 @@
         out_specs=[VMEM] * 2,
         out_shape=[
             jax.ShapeDtypeStruct((rows, k // 2), F32),
-            jax.ShapeDtypeStruct((rows, k // 2), BF16),
+            jax.ShapeDtypeStruct((rows, k // 2), F32),
         ],
         compiler_params=params(8),
         cost_estimate=cost(2 * rows * feats * k, 2 * (rows + k) * feats),

time: 27.6 us -> 27.7 us (level)
  transfers between devices with their start and end apart: 14 -> 14, of which waited for: 9 -> 8; matrix products, arithmetic and copies ran while one was open for 0% -> 0% of each run, Pallas kernels for 6% -> 6%
where the time goes in v8:
time: 27.7 us; the launch traced here: 27.6 us
  starting transfers between devices  16.5 us (60%)
  Pallas kernels  6.4 us (23%)
  waiting for transfers between devices  4.51 us (16%)
    ppermute x14, starting transfers between devices, swap(): return lax.ppermute(value, ('groups', 'eig'), pairs)  16.5 us
    ppermute x14, waiting for transfers between devices, swap(): return lax.ppermute(value, ('groups', 'eig'), pairs)  4.51 us
    pallas_call x1, Pallas kernels, weights(): pl.pallas_call(functools.partial(weights_kernel, *place), in_specs=[VMEM]...  2.66 us
    pallas_call x1, Pallas kernels, gram_first(): pl.pallas_call(gram_first_kernel, in_specs=[HBM, HBM], out_specs=[VMEM] *...  2 us
    pallas_call x2, Pallas kernels, share(): pl.pallas_call(functools.partial(share_kernel, places, before is not None...  0.87 us
  transfers between devices with their start and end apart: 14, of which 8 were waited for; matrix products, arithmetic and copies ran while one was open for 0% of the time, Pallas kernels for 6%

profile of v8, /device:TPU:0, one launch (start us, length us, event | category | flops | bytes accessed | tf_op | source)
XLA Modules:
  0.0 27.6 jit_solution(12500427911811293183)
XLA Ops:
  0.0 2.0 %gram_first.1 = (f32[256,128]{1,0:T(8,128)S(1)}, f32[256,128]{1,0:T(8,128)S(1)}, bf16[256,2048]{1,0:T(8,128)(2,1)S(1)}, bf16[2048,256]{1,0:T(8,128)(2,1)S(1)}) custom-call(bf16[1024,2048]{1,0:T(8,128)(2,1)} %f_hbm.1, bf16[2048,256]{1,0:T(8,128)(2,1)} %b_hbm.1), custom_call_target="tpu_custom_call" | custom-call | flops 268435456 | bytes 2097152 | tf_op jit(solution)/shard_map/gram_first/pallas_call | solution.py:103
  2.0 0.5 %collective-permute-start.1 = (f32[256,128]{1,0:T(8,128)S(1)}, f32[256,128]{1,0:T(8,128)S(1)}, u32[]{:S(2)}, u32[]{:S(2)}) collective-permute-start(f32[256,128]{1,0:T(8,128)S(1)} %get-tuple-element.25.refs_0_), channel_id=1, source_target_pairs={{0,1},{1,0},{2,3},{3,2},{4,5},{5,4},{6,7},{7,6},{8,9},{9,8},{10,11... | collective-permute-start | bytes 393224 | tf_op jit(solution)/shard_map/ppermute | solution.py:293
  2.5 0.4 %gram_rest.1 = (f32[256,128]{1,0:T(8,128)S(1)}, f32[256,128]{1,0:T(8,128)S(1)}) custom-call(bf16[256,2048]{1,0:T(8,128)(2,1)S(1)} %get-tuple-element.23.f_ref, bf16[2048,256]{1,0:T(8,128)(2,1)S(1)} %get-tuple-element.24.b_ref, f32[256,128]{1,0:T(8,128)S(1)} %get-tuple-element.25.refs_0_), custom_call_target="tpu_custom_call" | custom-call | flops 268435456 | bytes 2097152 | tf_op jit(solution)/shard_map/gram_rest/pallas_call | solution.py:128
  3.0 0.1 collective-permute-start
  3.1 0.4 %collective-permute-done.1.got_ref = f32[256,128]{1,0:T(8,128)S(1)} collective-permute-done((f32[256,128]{1,0:T(8,128)S(1)}, f32[256,128]{1,0:T(8,128)S(1)}, u32[]{:S(2)}, u32[]{:S(2)}) %collective-permute-start.1) | collective-permute-done | bytes 131104 | tf_op jit(solution)/shard_map/ppermute | solution.py:293
  3.5 2.7 %collective-permute-start.3 = (bf16[256,128]{1,0:T(8,128)(2,1)S(1)}, bf16[256,128]{1,0:T(8,128)(2,1)S(1)}, u32[]{:S(2)}, u32[]{:S(2)}) collective-permute-start(bf16[256,128]{1,0:T(8,128)(2,1)S(1)} %get-tuple-element.29.refs_0_), channel_id=1, source_target_pairs={{0,3},{1,8},{2,11},{3,0},{4,7},{5,12},{6,15},{7,4},{8,1},{9,10},{1... | collective-permute-start | bytes 196616 | tf_op jit(solution)/shard_map/ppermute | solution.py:293
  6.2 0.0 collective-permute-done.got_ref
  6.3 1.6 %collective-permute-start.2 = (bf16[256,128]{1,0:T(8,128)(2,1)S(1)}, bf16[256,128]{1,0:T(8,128)(2,1)S(1)}, u32[]{:S(2)}, u32[]{:S(2)}) collective-permute-start(bf16[256,128]{1,0:T(8,128)(2,1)S(1)} %get-tuple-element.31.refs_0_), channel_id=1, source_target_pairs={{0,4},{1,8},{2,11},{3,7},{4,0},{5,12},{6,15},{7,3},{8,1},{9,13},{1... | collective-permute-start | bytes 196616 | tf_op jit(solution)/shard_map/ppermute | solution.py:293
  7.9 0.3 %collective-permute-done.3.got_ref = bf16[256,128]{1,0:T(8,128)(2,1)S(1)} collective-permute-done((bf16[256,128]{1,0:T(8,128)(2,1)S(1)}, bf16[256,128]{1,0:T(8,128)(2,1)S(1)}, u32[]{:S(2)}, u32[]{:S(2)}) %collective-permute-start.3) | collective-permute-done | bytes 65568 | tf_op jit(solution)/shard_map/ppermute | solution.py:293
  8.2 2.1 %collective-permute-start.5 = (bf16[256,128]{1,0:T(8,128)(2,1)S(1)}, bf16[256,128]{1,0:T(8,128)(2,1)S(1)}, u32[]{:S(2)}, u32[]{:S(2)}) collective-permute-start(bf16[256,128]{1,0:T(8,128)(2,1)S(1)} %get-tuple-element.33.refs_0_), channel_id=1, source_target_pairs={{0,4},{1,2},{2,1},{3,7},{4,0},{5,6},{6,5},{7,3},{8,11},{9,13},{10,... | collective-permute-start | bytes 196616 | tf_op jit(solution)/shard_map/ppermute | solution.py:293
  10.3 0.3 collective-permute-done.2.got_ref
  10.6 2.2 %collective-permute-start.4 = (bf16[256,128]{1,0:T(8,128)(2,1)S(1)}, bf16[256,128]{1,0:T(8,128)(2,1)S(1)}, u32[]{:S(2)}, u32[]{:S(2)}) collective-permute-start(bf16[256,128]{1,0:T(8,128)(2,1)S(1)} %get-tuple-element.35.refs_0_), channel_id=1, source_target_pairs={{0,9},{1,2},{2,1},{3,10},{4,13},{5,6},{6,5},{7,14},{8,11},{9,0},{1... | collective-permute-start | bytes 196616 | tf_op jit(solution)/shard_map/ppermute | solution.py:293
  12.8 0.5 %collective-permute-done.5.got_ref = bf16[256,128]{1,0:T(8,128)(2,1)S(1)} collective-permute-done((bf16[256,128]{1,0:T(8,128)(2,1)S(1)}, bf16[256,128]{1,0:T(8,128)(2,1)S(1)}, u32[]{:S(2)}, u32[]{:S(2)}) %collective-permute-start.5) | collective-permute-done | bytes 65568 | tf_op jit(solution)/shard_map/ppermute | solution.py:293
  13.2 1.3 %collective-permute-start.7 = (bf16[256,128]{1,0:T(8,128)(2,1)S(1)}, bf16[256,128]{1,0:T(8,128)(2,1)S(1)}, u32[]{:S(2)}, u32[]{:S(2)}) collective-permute-start(bf16[256,128]{1,0:T(8,128)(2,1)S(1)} %get-tuple-element.37.refs_0_), channel_id=1, source_target_pairs={{0,9},{1,5},{2,6},{3,10},{4,13},{5,1},{6,2},{7,14},{8,12},{9,0},{1... | collective-permute-start | bytes 196616 | tf_op jit(solution)/shard_map/ppermute | solution.py:293
  14.6 0.7 %collective-permute-done.4.got_ref = bf16[256,128]{1,0:T(8,128)(2,1)S(1)} collective-permute-done((bf16[256,128]{1,0:T(8,128)(2,1)S(1)}, bf16[256,128]{1,0:T(8,128)(2,1)S(1)}, u32[]{:S(2)}, u32[]{:S(2)}) %collective-permute-start.4) | collective-permute-done | bytes 65568 | tf_op jit(solution)/shard_map/ppermute | solution.py:293
  15.3 0.0 copy-start.1
  15.3 0.0 copy-start.2
  15.3 0.0 copy-start.3
  15.3 0.0 copy-start.4
  15.3 1.7 %collective-permute-start.6 = (bf16[256,128]{1,0:T(8,128)(2,1)S(1)}, bf16[256,128]{1,0:T(8,128)(2,1)S(1)}, u32[]{:S(2)}, u32[]{:S(2)}) collective-permute-start(bf16[256,128]{1,0:T(8,128)(2,1)S(1)} %get-tuple-element.39.refs_0_), channel_id=1, source_target_pairs={{0,3},{1,5},{2,6},{3,0},{4,7},{5,1},{6,2},{7,4},{8,12},{9,10},{10,... | collective-permute-start | bytes 196616 | tf_op jit(solution)/shard_map/ppermute | solution.py:293
  17.0 0.0 copy-done.1
  17.0 0.0 copy-done.2
  17.0 0.0 copy-done.3
  17.0 0.0 copy-done.4
  17.0 0.3 %inverse.1.refs_0_.inverse_ref = f32[256,1024]{1,0:T(8,128)S(1)} custom-call(f32[8,16]{1,0:T(8,128)S(1)} %copy-done.1, s32[1,1024]{1,0:T(1,128)S(1)} %bitcast.3, s32[1,1024]{1,0:T(1,128)S(1)} %bitcast.4, f32[1,256]{1,0:T(1,128)S(1)} %bitcast.5, bf16[256,128]{1,0:T(8,128)(2,1)S(1)} %get-tuple-element.39.refs_0_), custom_call_target="tpu_custom_call" | custom-call | flops 2097152 | bytes 524288 | tf_op jit(solution)/shard_map/inverse/pallas_call | solution.py:164
  17.4 0.6 %collective-permute-done.7.got_ref = bf16[256,128]{1,0:T(8,128)(2,1)S(1)} collective-permute-done((bf16[256,128]{1,0:T(8,128)(2,1)S(1)}, bf16[256,128]{1,0:T(8,128)(2,1)S(1)}, u32[]{:S(2)}, u32[]{:S(2)}) %collective-permute-start.7) | collective-permute-done | bytes 65568 | tf_op jit(solution)/shard_map/ppermute | solution.py:293
  18.0 1.6 %collective-permute-start.10 = (bf16[256,128]{1,0:T(8,128)(2,1)S(1)}, bf16[256,128]{1,0:T(8,128)(2,1)S(1)}, u32[]{:S(2)}, u32[]{:S(2)}) collective-permute-start(bf16[256,128]{1,0:T(8,128)(2,1)S(1)} %add.14.refs_0_), channel_id=1, source_target_pairs={{0,17},{1,16},{2,19},{3,18},{4,21},{5,20},{6,23},{7,22},{8,25},{9,... | collective-permute-start | bytes 196616 | tf_op jit(solution)/shard_map/ppermute | solution.py:293
  19.6 0.0 collective-permute-done.6.got_ref
  19.6 0.0 copy-start
  19.7 1.4 %collective-permute-start.8 = (bf16[256,128]{1,0:T(8,128)(2,1)S(1)}, bf16[256,128]{1,0:T(8,128)(2,1)S(1)}, u32[]{:S(2)}, u32[]{:S(2)}) collective-permute-start(bf16[256,128]{1,0:T(8,128)(2,1)S(1)} %add.15.refs_2_), channel_id=1, source_target_pairs={{0,17},{1,16},{2,19},{3,18},{4,21},{5,20},{6,23},{7,22},{8,25},{9,... | collective-permute-start | bytes 196616 | tf_op jit(solution)/shard_map/ppermute | solution.py:293
  21.1 0.8 %collective-permute-start.13 = (bf16[256,128]{1,0:T(8,128)(2,1)S(1)}, bf16[256,128]{1,0:T(8,128)(2,1)S(1)}, u32[]{:S(2)}, u32[]{:S(2)}) collective-permute-start(bf16[256,128]{1,0:T(8,128)(2,1)S(1)} %add.15.refs_2_), channel_id=1, source_target_pairs={{0,1},{1,0},{2,3},{3,2},{4,5},{5,4},{6,7},{7,6},{8,9},{9,8},{10,11... | collective-permute-start | bytes 196616 | tf_op jit(solution)/shard_map/ppermute | solution.py:293
  21.8 0.0 collective-permute-start.12
  21.8 0.5 %collective-permute-done.10.refs_0_ = bf16[256,128]{1,0:T(8,128)(2,1)S(1)} collective-permute-done((bf16[256,128]{1,0:T(8,128)(2,1)S(1)}, bf16[256,128]{1,0:T(8,128)(2,1)S(1)}, u32[]{:S(2)}, u32[]{:S(2)}) %collective-permute-start.10) | collective-permute-done | bytes 65568 | tf_op jit(solution)/shard_map/ppermute | solution.py:293
  22.3 0.1 collective-permute-start.11
  22.4 1.2 %collective-permute-done.8.own_ref = bf16[256,128]{1,0:T(8,128)(2,1)S(1)} collective-permute-done((bf16[256,128]{1,0:T(8,128)(2,1)S(1)}, bf16[256,128]{1,0:T(8,128)(2,1)S(1)}, u32[]{:S(2)}, u32[]{:S(2)}) %collective-permute-start.8) | collective-permute-done | bytes 65568 | tf_op jit(solution)/shard_map/ppermute | solution.py:293
  23.6 0.3 %collective-permute-start.9 = (bf16[256,128]{1,0:T(8,128)(2,1)S(1)}, bf16[256,128]{1,0:T(8,128)(2,1)S(1)}, u32[]{:S(2)}, u32[]{:S(2)}) collective-permute-start(bf16[256,128]{1,0:T(8,128)(2,1)S(1)} %collective-permute-done.8.own_ref), channel_id=1, source_target_pairs={{0,1},{1,0},{2,3},{3,2},{4,5},{5,4},{6,7},{7,6},{8,9},{9,8},{10,11... | collective-permute-start | bytes 196616 | tf_op jit(solution)/shard_map/ppermute | solution.py:293
  23.9 0.0 collective-permute-done.13.refs_3_
  23.9 0.0 collective-permute-done.12.refs_1_
  24.0 0.0 copy-done
  24.0 0.5 %share.2.refs_3_ = f32[256,1024]{1,0:T(8,128)S(1)} custom-call(bf16[256,128]{1,0:T(8,128)(2,1)S(1)} %add.14.refs_0_, bf16[256,128]{1,0:T(8,128)(2,1)S(1)} %collective-permute-done.12.refs_1_, bf16[256,128]{1,0:T(8,128)(2,1)S(1)} %add.15.refs_2_, bf16[256,128]{1,0:T(8,128)(2,1)S(1)} %collective-permute-done.13.refs_3_, bf16[1024,1024]{1,0:T(8,128)(2,1)S(1)} %copy-done), custom_call_target="tpu_custom_call" | custom-call | flops 268435456 | bytes 524288 | tf_op jit(solution)/shard_map/share/pallas_call | solution.py:228
  24.5 0.0 collective-permute-done.11.refs_1_
  24.5 0.4 %share.3.before_ref = f32[256,1024]{1,0:T(8,128)S(1)} custom-call(bf16[256,128]{1,0:T(8,128)(2,1)S(1)} %collective-permute-done.10.refs_0_, bf16[256,128]{1,0:T(8,128)(2,1)S(1)} %collective-permute-done.11.refs_1_, bf16[1024,1024]{1,0:T(8,128)(2,1)S(1)} %copy-done, f32[256,1024]{1,0:T(8,128)S(1)} %share.2.refs_3_), custom_call_target="tpu_custom_call" | custom-call | flops 134217728 | bytes 524288 | tf_op jit(solution)/shard_map/share/pallas_call | solution.py:228
  24.8 0.1 collective-permute-done.9.got_ref
  24.9 2.7 %weights.1 = bf16[2048,1024]{1,0:T(8,128)(2,1)} custom-call(bf16[256,128]{1,0:T(8,128)(2,1)S(1)} %collective-permute-done.8.own_ref, bf16[256,128]{1,0:T(8,128)(2,1)S(1)} %collective-permute-done.9.got_ref, bf16[1024,1024]{1,0:T(8,128)(2,1)S(1)} %copy-done, f32[256,1024]{1,0:T(8,128)S(1)} %share.3.before_ref, f32[256,1024]{1,0:T(8,128)S(1)} %inverse.1.refs_0_.inverse_ref, ...), custom_call_target="tpu_custom_call" | custom-call | flops 1073741824 | bytes 4194304 | tf_op jit(solution)/shard_map/weights/pallas_call | solution.py:269
  (8 shorter events, 0.1 us)
Async XLA Ops:
  2.0 1.5 %collective-permute-start.1 = (f32[256,128]{1,0:T(8,128)S(1)}, f32[256,128]{1,0:T(8,128)S(1)}, u32[]{:S(2)}, u32[]{:S(2)}) collective-permute-start(f32[256,128]{1,0:T(8,128)S(1)} %get-tuple-element.25.refs_0_), channel_id=1, source_target_pairs={{0,1},{1,0},{2,3},{3,2},{4,5},{5,4},{6,7},{7,6},{8,9},{9,8},{10,11... | collective-permute-start | bytes 393224 | tf_op jit(solution)/shard_map/ppermute | solution.py:293
  3.0 3.3 %collective-permute-start = (f32[256,128]{1,0:T(8,128)S(1)}, f32[256,128]{1,0:T(8,128)S(1)}, u32[]{:S(2)}, u32[]{:S(2)}) collective-permute-start(f32[256,128]{1,0:T(8,128)S(1)} %get-tuple-element.27.refs_0_), channel_id=1, source_target_pairs={{0,1},{1,0},{2,3},{3,2},{4,5},{5,4},{6,7},{7,6},{8,9},{9,8},{10,11... | collective-permute-start | bytes 393224 | tf_op jit(solution)/shard_map/ppermute | solution.py:293
  3.5 4.6 %collective-permute-start.3 = (bf16[256,128]{1,0:T(8,128)(2,1)S(1)}, bf16[256,128]{1,0:T(8,128)(2,1)S(1)}, u32[]{:S(2)}, u32[]{:S(2)}) collective-permute-start(bf16[256,128]{1,0:T(8,128)(2,1)S(1)} %get-tuple-element.29.refs_0_), channel_id=1, source_target_pairs={{0,3},{1,8},{2,11},{3,0},{4,7},{5,12},{6,15},{7,4},{8,1},{9,10},{1... | collective-permute-start | bytes 196616 | tf_op jit(solution)/shard_map/ppermute | solution.py:293
  6.3 4.3 %collective-permute-start.2 = (bf16[256,128]{1,0:T(8,128)(2,1)S(1)}, bf16[256,128]{1,0:T(8,128)(2,1)S(1)}, u32[]{:S(2)}, u32[]{:S(2)}) collective-permute-start(bf16[256,128]{1,0:T(8,128)(2,1)S(1)} %get-tuple-element.31.refs_0_), channel_id=1, source_target_pairs={{0,4},{1,8},{2,11},{3,7},{4,0},{5,12},{6,15},{7,3},{8,1},{9,13},{1... | collective-permute-start | bytes 196616 | tf_op jit(solution)/shard_map/ppermute | solution.py:293
  8.2 5.0 %collective-permute-start.5 = (bf16[256,128]{1,0:T(8,128)(2,1)S(1)}, bf16[256,128]{1,0:T(8,128)(2,1)S(1)}, u32[]{:S(2)}, u32[]{:S(2)}) collective-permute-start(bf16[256,128]{1,0:T(8,128)(2,1)S(1)} %get-tuple-element.33.refs_0_), channel_id=1, source_target_pairs={{0,4},{1,2},{2,1},{3,7},{4,0},{5,6},{6,5},{7,3},{8,11},{9,13},{10,... | collective-permute-start | bytes 196616 | tf_op jit(solution)/shard_map/ppermute | solution.py:293
  10.6 4.7 %collective-permute-start.4 = (bf16[256,128]{1,0:T(8,128)(2,1)S(1)}, bf16[256,128]{1,0:T(8,128)(2,1)S(1)}, u32[]{:S(2)}, u32[]{:S(2)}) collective-permute-start(bf16[256,128]{1,0:T(8,128)(2,1)S(1)} %get-tuple-element.35.refs_0_), channel_id=1, source_target_pairs={{0,9},{1,2},{2,1},{3,10},{4,13},{5,6},{6,5},{7,14},{8,11},{9,0},{1... | collective-permute-start | bytes 196616 | tf_op jit(solution)/shard_map/ppermute | solution.py:293
  13.2 4.8 %collective-permute-start.7 = (bf16[256,128]{1,0:T(8,128)(2,1)S(1)}, bf16[256,128]{1,0:T(8,128)(2,1)S(1)}, u32[]{:S(2)}, u32[]{:S(2)}) collective-permute-start(bf16[256,128]{1,0:T(8,128)(2,1)S(1)} %get-tuple-element.37.refs_0_), channel_id=1, source_target_pairs={{0,9},{1,5},{2,6},{3,10},{4,13},{5,1},{6,2},{7,14},{8,12},{9,0},{1... | collective-permute-start | bytes 196616 | tf_op jit(solution)/shard_map/ppermute | solution.py:293
  15.3 1.8 %copy-start.1 = (f32[8,16]{1,0:T(8,128)S(1)}, f32[8,16]{1,0:T(8,128)}, u32[]{:S(2)}) copy-start(f32[8,16]{1,0:T(8,128)} %table_ref.1) | copy-start | bytes 1540
  15.3 1.8 %copy-start.2 = (s32[1024]{0:T(1024)S(1)}, s32[1024]{0:T(1024)}, u32[]{:S(2)}) copy-start(s32[1024]{0:T(1024)} %param.11) | copy-start | bytes 12292
  15.3 1.8 %copy-start.3 = (s32[1024]{0:T(1024)S(1)}, s32[1024]{0:T(1024)}, u32[]{:S(2)}) copy-start(s32[1024]{0:T(1024)} %param.12) | copy-start | bytes 12292
  15.3 1.8 %copy-start.4 = (f32[256]{0:T(256)S(1)}, f32[256]{0:T(256)}, u32[]{:S(2)}) copy-start(f32[256]{0:T(256)} %param.10) | copy-start | bytes 3076
  15.3 4.3 %collective-permute-start.6 = (bf16[256,128]{1,0:T(8,128)(2,1)S(1)}, bf16[256,128]{1,0:T(8,128)(2,1)S(1)}, u32[]{:S(2)}, u32[]{:S(2)}) collective-permute-start(bf16[256,128]{1,0:T(8,128)(2,1)S(1)} %get-tuple-element.39.refs_0_), channel_id=1, source_target_pairs={{0,3},{1,5},{2,6},{3,0},{4,7},{5,1},{6,2},{7,4},{8,12},{9,10},{10,... | collective-permute-start | bytes 196616 | tf_op jit(solution)/shard_map/ppermute | solution.py:293
  18.0 4.3 %collective-permute-start.10 = (bf16[256,128]{1,0:T(8,128)(2,1)S(1)}, bf16[256,128]{1,0:T(8,128)(2,1)S(1)}, u32[]{:S(2)}, u32[]{:S(2)}) collective-permute-start(bf16[256,128]{1,0:T(8,128)(2,1)S(1)} %add.14.refs_0_), channel_id=1, source_target_pairs={{0,17},{1,16},{2,19},{3,18},{4,21},{5,20},{6,23},{7,22},{8,25},{9,... | collective-permute-start | bytes 196616 | tf_op jit(solution)/shard_map/ppermute | solution.py:293
  19.6 4.3 %copy-start = (bf16[1024,1024]{1,0:T(8,128)(2,1)S(1)}, bf16[1024,1024]{1,0:T(8,128)(2,1)}, u32[]{:S(2)}) copy-start(bf16[1024,1024]{1,0:T(8,128)(2,1)} %r_ref.1) | copy-start | bytes 6291460
  19.7 4.0 %collective-permute-start.8 = (bf16[256,128]{1,0:T(8,128)(2,1)S(1)}, bf16[256,128]{1,0:T(8,128)(2,1)S(1)}, u32[]{:S(2)}, u32[]{:S(2)}) collective-permute-start(bf16[256,128]{1,0:T(8,128)(2,1)S(1)} %add.15.refs_2_), channel_id=1, source_target_pairs={{0,17},{1,16},{2,19},{3,18},{4,21},{5,20},{6,23},{7,22},{8,25},{9,... | collective-permute-start | bytes 196616 | tf_op jit(solution)/shard_map/ppermute | solution.py:293
  21.1 2.9 %collective-permute-start.13 = (bf16[256,128]{1,0:T(8,128)(2,1)S(1)}, bf16[256,128]{1,0:T(8,128)(2,1)S(1)}, u32[]{:S(2)}, u32[]{:S(2)}) collective-permute-start(bf16[256,128]{1,0:T(8,128)(2,1)S(1)} %add.15.refs_2_), channel_id=1, source_target_pairs={{0,1},{1,0},{2,3},{3,2},{4,5},{5,4},{6,7},{7,6},{8,9},{9,8},{10,11... | collective-permute-start | bytes 196616 | tf_op jit(solution)/shard_map/ppermute | solution.py:293
  21.8 2.1 %collective-permute-start.12 = (bf16[256,128]{1,0:T(8,128)(2,1)S(1)}, bf16[256,128]{1,0:T(8,128)(2,1)S(1)}, u32[]{:S(2)}, u32[]{:S(2)}) collective-permute-start(bf16[256,128]{1,0:T(8,128)(2,1)S(1)} %add.14.refs_0_), channel_id=1, source_target_pairs={{0,1},{1,0},{2,3},{3,2},{4,5},{5,4},{6,7},{7,6},{8,9},{9,8},{10,11... | collective-permute-start | bytes 196616 | tf_op jit(solution)/shard_map/ppermute | solution.py:293
  22.3 2.1 %collective-permute-start.11 = (bf16[256,128]{1,0:T(8,128)(2,1)S(1)}, bf16[256,128]{1,0:T(8,128)(2,1)S(1)}, u32[]{:S(2)}, u32[]{:S(2)}) collective-permute-start(bf16[256,128]{1,0:T(8,128)(2,1)S(1)} %collective-permute-done.10.refs_0_), channel_id=1, source_target_pairs={{0,1},{1,0},{2,3},{3,2},{4,5},{5,4},{6,7},{7,6},{8,9},{9,8},{10,11... | collective-permute-start | bytes 196616 | tf_op jit(solution)/shard_map/ppermute | solution.py:293
  23.6 1.3 %collective-permute-start.9 = (bf16[256,128]{1,0:T(8,128)(2,1)S(1)}, bf16[256,128]{1,0:T(8,128)(2,1)S(1)}, u32[]{:S(2)}, u32[]{:S(2)}) collective-permute-start(bf16[256,128]{1,0:T(8,128)(2,1)S(1)} %collective-permute-done.8.own_ref), channel_id=1, source_target_pairs={{0,1},{1,0},{2,3},{3,2},{4,5},{5,4},{6,7},{7,6},{8,9},{9,8},{10,11... | collective-permute-start | bytes 196616 | tf_op jit(solution)/shard_map/ppermute | solution.py:293

commit v9 on v8

--- a/solution.py
+++ b/solution.py
@@ -318,7 +318,7 @@
     masks = orders(lax.axis_size("eig"))
     count = len(masks[0][0])
     for at in range(count + 1):
-        if at == count:
+        if at == 1:
             inv = inverse(alpha_table, reg_index, subject, eigenvalues, last)
             last = (inv,)
         for i in range(CHAINS):

time: 27.7 us -> 27.7 us (level)
  no operation moved by 1% of the time
where the time goes in v9:
time: 27.7 us; the launch traced here: 27.6 us
  starting transfers between devices  16.3 us (59%)
  Pallas kernels  6.4 us (23%)
  waiting for transfers between devices  4.73 us (17%)
    ppermute x14, starting transfers between devices, swap(): return lax.ppermute(value, ('groups', 'eig'), pairs)  16.3 us
    ppermute x14, waiting for transfers between devices, swap(): return lax.ppermute(value, ('groups', 'eig'), pairs)  4.73 us
    pallas_call x1, Pallas kernels, weights(): pl.pallas_call(functools.partial(weights_kernel, *place), in_specs=[VMEM]...  2.66 us
    pallas_call x1, Pallas kernels, gram_first(): pl.pallas_call(gram_first_kernel, in_specs=[HBM, HBM], out_specs=[VMEM] *...  2 us
    pallas_call x2, Pallas kernels, share(): pl.pallas_call(functools.partial(share_kernel, places, before is not None...  0.87 us
  transfers between devices with their start and end apart: 14, of which 8 were waited for; matrix products, arithmetic and copies ran while one was open for 0% of the time, Pallas kernels for 6%

profile of v9, /device:TPU:0, one launch (start us, length us, event | category | flops | bytes accessed | tf_op | source)
XLA Modules:
  0.0 27.6 jit_solution(10579963849207304684)
XLA Ops:
  0.0 2.0 %gram_first.1 = (f32[256,128]{1,0:T(8,128)S(1)}, f32[256,128]{1,0:T(8,128)S(1)}, bf16[256,2048]{1,0:T(8,128)(2,1)S(1)}, bf16[2048,256]{1,0:T(8,128)(2,1)S(1)}) custom-call(bf16[1024,2048]{1,0:T(8,128)(2,1)} %f_hbm.1, bf16[2048,256]{1,0:T(8,128)(2,1)} %b_hbm.1), custom_call_target="tpu_custom_call" | custom-call | flops 268435456 | bytes 2097152 | tf_op jit(solution)/shard_map/gram_first/pallas_call | solution.py:103
  2.0 0.5 %collective-permute-start.1 = (f32[256,128]{1,0:T(8,128)S(1)}, f32[256,128]{1,0:T(8,128)S(1)}, u32[]{:S(2)}, u32[]{:S(2)}) collective-permute-start(f32[256,128]{1,0:T(8,128)S(1)} %get-tuple-element.25.refs_0_), channel_id=1, source_target_pairs={{0,1},{1,0},{2,3},{3,2},{4,5},{5,4},{6,7},{7,6},{8,9},{9,8},{10,11... | collective-permute-start | bytes 393224 | tf_op jit(solution)/shard_map/ppermute | solution.py:293
  2.5 0.4 %gram_rest.1 = (f32[256,128]{1,0:T(8,128)S(1)}, f32[256,128]{1,0:T(8,128)S(1)}) custom-call(bf16[256,2048]{1,0:T(8,128)(2,1)S(1)} %get-tuple-element.23.f_ref, bf16[2048,256]{1,0:T(8,128)(2,1)S(1)} %get-tuple-element.24.b_ref, f32[256,128]{1,0:T(8,128)S(1)} %get-tuple-element.25.refs_0_), custom_call_target="tpu_custom_call" | custom-call | flops 268435456 | bytes 2097152 | tf_op jit(solution)/shard_map/gram_rest/pallas_call | solution.py:128
  3.0 0.1 collective-permute-start
  3.1 0.4 %collective-permute-done.1.got_ref = f32[256,128]{1,0:T(8,128)S(1)} collective-permute-done((f32[256,128]{1,0:T(8,128)S(1)}, f32[256,128]{1,0:T(8,128)S(1)}, u32[]{:S(2)}, u32[]{:S(2)}) %collective-permute-start.1) | collective-permute-done | bytes 131104 | tf_op jit(solution)/shard_map/ppermute | solution.py:293
  3.5 2.7 %collective-permute-start.3 = (bf16[256,128]{1,0:T(8,128)(2,1)S(1)}, bf16[256,128]{1,0:T(8,128)(2,1)S(1)}, u32[]{:S(2)}, u32[]{:S(2)}) collective-permute-start(bf16[256,128]{1,0:T(8,128)(2,1)S(1)} %get-tuple-element.29.refs_0_), channel_id=1, source_target_pairs={{0,3},{1,8},{2,11},{3,0},{4,7},{5,12},{6,15},{7,4},{8,1},{9,10},{1... | collective-permute-start | bytes 196616 | tf_op jit(solution)/shard_map/ppermute | solution.py:293
  6.2 0.0 collective-permute-done.got_ref
  6.2 0.0 copy-start.1
  6.2 0.0 copy-start.2
  6.2 0.0 copy-start.3
  6.2 0.0 copy-start.4
  6.3 1.6 %collective-permute-start.2 = (bf16[256,128]{1,0:T(8,128)(2,1)S(1)}, bf16[256,128]{1,0:T(8,128)(2,1)S(1)}, u32[]{:S(2)}, u32[]{:S(2)}) collective-permute-start(bf16[256,128]{1,0:T(8,128)(2,1)S(1)} %get-tuple-element.31.refs_0_), channel_id=1, source_target_pairs={{0,4},{1,8},{2,11},{3,7},{4,0},{5,12},{6,15},{7,3},{8,1},{9,13},{1... | collective-permute-start | bytes 196616 | tf_op jit(solution)/shard_map/ppermute | solution.py:293
  7.9 0.0 copy-done.1
  7.9 0.0 copy-done.2
  7.9 0.0 copy-done.3
  7.9 0.0 copy-done.4
  7.9 0.3 %inverse.1.refs_0_.inverse_ref = f32[256,1024]{1,0:T(8,128)S(1)} custom-call(f32[8,16]{1,0:T(8,128)S(1)} %copy-done.1, s32[1,1024]{1,0:T(1,128)S(1)} %bitcast.3, s32[1,1024]{1,0:T(1,128)S(1)} %bitcast.4, f32[1,256]{1,0:T(1,128)S(1)} %bitcast.5, bf16[256,128]{1,0:T(8,128)(2,1)S(1)} %get-tuple-element.31.refs_0_), custom_call_target="tpu_custom_call" | custom-call | flops 2097152 | bytes 524288 | tf_op jit(solution)/shard_map/inverse/pallas_call | solution.py:164
  8.2 0.0 collective-permute-done.3.got_ref
  8.3 2.0 %collective-permute-start.5 = (bf16[256,128]{1,0:T(8,128)(2,1)S(1)}, bf16[256,128]{1,0:T(8,128)(2,1)S(1)}, u32[]{:S(2)}, u32[]{:S(2)}) collective-permute-start(bf16[256,128]{1,0:T(8,128)(2,1)S(1)} %get-tuple-element.33.refs_0_), channel_id=1, source_target_pairs={{0,4},{1,2},{2,1},{3,7},{4,0},{5,6},{6,5},{7,3},{8,11},{9,13},{10,... | collective-permute-start | bytes 196616 | tf_op jit(solution)/shard_map/ppermute | solution.py:293
  10.3 0.3 %collective-permute-done.2.got_ref = bf16[256,128]{1,0:T(8,128)(2,1)S(1)} collective-permute-done((bf16[256,128]{1,0:T(8,128)(2,1)S(1)}, bf16[256,128]{1,0:T(8,128)(2,1)S(1)}, u32[]{:S(2)}, u32[]{:S(2)}) %collective-permute-start.2) | collective-permute-done | bytes 65568 | tf_op jit(solution)/shard_map/ppermute | solution.py:293
  10.6 2.1 %collective-permute-start.4 = (bf16[256,128]{1,0:T(8,128)(2,1)S(1)}, bf16[256,128]{1,0:T(8,128)(2,1)S(1)}, u32[]{:S(2)}, u32[]{:S(2)}) collective-permute-start(bf16[256,128]{1,0:T(8,128)(2,1)S(1)} %get-tuple-element.35.refs_0_), channel_id=1, source_target_pairs={{0,9},{1,2},{2,1},{3,10},{4,13},{5,6},{6,5},{7,14},{8,11},{9,0},{1... | collective-permute-start | bytes 196616 | tf_op jit(solution)/shard_map/ppermute | solution.py:293
  12.8 0.5 %collective-permute-done.5.got_ref = bf16[256,128]{1,0:T(8,128)(2,1)S(1)} collective-permute-done((bf16[256,128]{1,0:T(8,128)(2,1)S(1)}, bf16[256,128]{1,0:T(8,128)(2,1)S(1)}, u32[]{:S(2)}, u32[]{:S(2)}) %collective-permute-start.5) | collective-permute-done | bytes 65568 | tf_op jit(solution)/shard_map/ppermute | solution.py:293
  13.3 1.3 %collective-permute-start.7 = (bf16[256,128]{1,0:T(8,128)(2,1)S(1)}, bf16[256,128]{1,0:T(8,128)(2,1)S(1)}, u32[]{:S(2)}, u32[]{:S(2)}) collective-permute-start(bf16[256,128]{1,0:T(8,128)(2,1)S(1)} %get-tuple-element.37.refs_0_), channel_id=1, source_target_pairs={{0,9},{1,5},{2,6},{3,10},{4,13},{5,1},{6,2},{7,14},{8,12},{9,0},{1... | collective-permute-start | bytes 196616 | tf_op jit(solution)/shard_map/ppermute | solution.py:293
  14.6 0.7 %collective-permute-done.4.got_ref = bf16[256,128]{1,0:T(8,128)(2,1)S(1)} collective-permute-done((bf16[256,128]{1,0:T(8,128)(2,1)S(1)}, bf16[256,128]{1,0:T(8,128)(2,1)S(1)}, u32[]{:S(2)}, u32[]{:S(2)}) %collective-permute-start.4) | collective-permute-done | bytes 65568 | tf_op jit(solution)/shard_map/ppermute | solution.py:293
  15.3 1.7 %collective-permute-start.6 = (bf16[256,128]{1,0:T(8,128)(2,1)S(1)}, bf16[256,128]{1,0:T(8,128)(2,1)S(1)}, u32[]{:S(2)}, u32[]{:S(2)}) collective-permute-start(bf16[256,128]{1,0:T(8,128)(2,1)S(1)} %get-tuple-element.39.refs_0_), channel_id=1, source_target_pairs={{0,3},{1,5},{2,6},{3,0},{4,7},{5,1},{6,2},{7,4},{8,12},{9,10},{10,... | collective-permute-start | bytes 196616 | tf_op jit(solution)/shard_map/ppermute | solution.py:293
  17.0 1.0 %collective-permute-done.7.got_ref = bf16[256,128]{1,0:T(8,128)(2,1)S(1)} collective-permute-done((bf16[256,128]{1,0:T(8,128)(2,1)S(1)}, bf16[256,128]{1,0:T(8,128)(2,1)S(1)}, u32[]{:S(2)}, u32[]{:S(2)}) %collective-permute-start.7) | collective-permute-done | bytes 65568 | tf_op jit(solution)/shard_map/ppermute | solution.py:293
  18.0 1.6 %collective-permute-start.10 = (bf16[256,128]{1,0:T(8,128)(2,1)S(1)}, bf16[256,128]{1,0:T(8,128)(2,1)S(1)}, u32[]{:S(2)}, u32[]{:S(2)}) collective-permute-start(bf16[256,128]{1,0:T(8,128)(2,1)S(1)} %add.14.refs_0_), channel_id=1, source_target_pairs={{0,17},{1,16},{2,19},{3,18},{4,21},{5,20},{6,23},{7,22},{8,25},{9,... | collective-permute-start | bytes 196616 | tf_op jit(solution)/shard_map/ppermute | solution.py:293
  19.7 0.0 collective-permute-done.6.got_ref
  19.7 0.0 copy-start
  19.7 1.4 %collective-permute-start.8 = (bf16[256,128]{1,0:T(8,128)(2,1)S(1)}, bf16[256,128]{1,0:T(8,128)(2,1)S(1)}, u32[]{:S(2)}, u32[]{:S(2)}) collective-permute-start(bf16[256,128]{1,0:T(8,128)(2,1)S(1)} %add.15.refs_2_), channel_id=1, source_target_pairs={{0,17},{1,16},{2,19},{3,18},{4,21},{5,20},{6,23},{7,22},{8,25},{9,... | collective-permute-start | bytes 196616 | tf_op jit(solution)/shard_map/ppermute | solution.py:293
  21.0 0.8 %collective-permute-start.13 = (bf16[256,128]{1,0:T(8,128)(2,1)S(1)}, bf16[256,128]{1,0:T(8,128)(2,1)S(1)}, u32[]{:S(2)}, u32[]{:S(2)}) collective-permute-start(bf16[256,128]{1,0:T(8,128)(2,1)S(1)} %add.15.refs_2_), channel_id=1, source_target_pairs={{0,1},{1,0},{2,3},{3,2},{4,5},{5,4},{6,7},{7,6},{8,9},{9,8},{10,11... | collective-permute-start | bytes 196616 | tf_op jit(solution)/shard_map/ppermute | solution.py:293
  21.9 0.0 collective-permute-start.12
  21.9 0.6 %collective-permute-done.10.refs_0_ = bf16[256,128]{1,0:T(8,128)(2,1)S(1)} collective-permute-done((bf16[256,128]{1,0:T(8,128)(2,1)S(1)}, bf16[256,128]{1,0:T(8,128)(2,1)S(1)}, u32[]{:S(2)}, u32[]{:S(2)}) %collective-permute-start.10) | collective-permute-done | bytes 65568 | tf_op jit(solution)/shard_map/ppermute | solution.py:293
  22.5 0.1 collective-permute-start.11
  22.6 1.1 %collective-permute-done.8.own_ref = bf16[256,128]{1,0:T(8,128)(2,1)S(1)} collective-permute-done((bf16[256,128]{1,0:T(8,128)(2,1)S(1)}, bf16[256,128]{1,0:T(8,128)(2,1)S(1)}, u32[]{:S(2)}, u32[]{:S(2)}) %collective-permute-start.8) | collective-permute-done | bytes 65568 | tf_op jit(solution)/shard_map/ppermute | solution.py:293
  23.7 0.3 %collective-permute-start.9 = (bf16[256,128]{1,0:T(8,128)(2,1)S(1)}, bf16[256,128]{1,0:T(8,128)(2,1)S(1)}, u32[]{:S(2)}, u32[]{:S(2)}) collective-permute-start(bf16[256,128]{1,0:T(8,128)(2,1)S(1)} %collective-permute-done.8.own_ref), channel_id=1, source_target_pairs={{0,1},{1,0},{2,3},{3,2},{4,5},{5,4},{6,7},{7,6},{8,9},{9,8},{10,11... | collective-permute-start | bytes 196616 | tf_op jit(solution)/shard_map/ppermute | solution.py:293
  24.0 0.0 collective-permute-done.13.refs_3_
  24.0 0.0 collective-permute-done.12.refs_1_
  24.0 0.0 copy-done
  24.0 0.5 %share.2.refs_3_ = f32[256,1024]{1,0:T(8,128)S(1)} custom-call(bf16[256,128]{1,0:T(8,128)(2,1)S(1)} %add.14.refs_0_, bf16[256,128]{1,0:T(8,128)(2,1)S(1)} %collective-permute-done.12.refs_1_, bf16[256,128]{1,0:T(8,128)(2,1)S(1)} %add.15.refs_2_, bf16[256,128]{1,0:T(8,128)(2,1)S(1)} %collective-permute-done.13.refs_3_, bf16[1024,1024]{1,0:T(8,128)(2,1)S(1)} %copy-done), custom_call_target="tpu_custom_call" | custom-call | flops 268435456 | bytes 524288 | tf_op jit(solution)/shard_map/share/pallas_call | solution.py:228
  24.5 0.0 collective-permute-done.11.refs_1_
  24.5 0.4 %share.3.before_ref = f32[256,1024]{1,0:T(8,128)S(1)} custom-call(bf16[256,128]{1,0:T(8,128)(2,1)S(1)} %collective-permute-done.10.refs_0_, bf16[256,128]{1,0:T(8,128)(2,1)S(1)} %collective-permute-done.11.refs_1_, bf16[1024,1024]{1,0:T(8,128)(2,1)S(1)} %copy-done, f32[256,1024]{1,0:T(8,128)S(1)} %share.2.refs_3_), custom_call_target="tpu_custom_call" | custom-call | flops 134217728 | bytes 524288 | tf_op jit(solution)/shard_map/share/pallas_call | solution.py:228
  24.9 0.1 collective-permute-done.9.got_ref
  24.9 2.7 %weights.1 = bf16[2048,1024]{1,0:T(8,128)(2,1)} custom-call(bf16[256,128]{1,0:T(8,128)(2,1)S(1)} %collective-permute-done.8.own_ref, bf16[256,128]{1,0:T(8,128)(2,1)S(1)} %collective-permute-done.9.got_ref, bf16[1024,1024]{1,0:T(8,128)(2,1)S(1)} %copy-done, f32[256,1024]{1,0:T(8,128)S(1)} %share.3.before_ref, f32[256,1024]{1,0:T(8,128)S(1)} %inverse.1.refs_0_.inverse_ref, ...), custom_call_target="tpu_custom_call" | custom-call | flops 1073741824 | bytes 4194304 | tf_op jit(solution)/shard_map/weights/pallas_call | solution.py:269
  (8 shorter events, 0.1 us)
Async XLA Ops:
  2.0 1.5 %collective-permute-start.1 = (f32[256,128]{1,0:T(8,128)S(1)}, f32[256,128]{1,0:T(8,128)S(1)}, u32[]{:S(2)}, u32[]{:S(2)}) collective-permute-start(f32[256,128]{1,0:T(8,128)S(1)} %get-tuple-element.25.refs_0_), channel_id=1, source_target_pairs={{0,1},{1,0},{2,3},{3,2},{4,5},{5,4},{6,7},{7,6},{8,9},{9,8},{10,11... | collective-permute-start | bytes 393224 | tf_op jit(solution)/shard_map/ppermute | solution.py:293
  3.0 3.3 %collective-permute-start = (f32[256,128]{1,0:T(8,128)S(1)}, f32[256,128]{1,0:T(8,128)S(1)}, u32[]{:S(2)}, u32[]{:S(2)}) collective-permute-start(f32[256,128]{1,0:T(8,128)S(1)} %get-tuple-element.27.refs_0_), channel_id=1, source_target_pairs={{0,1},{1,0},{2,3},{3,2},{4,5},{5,4},{6,7},{7,6},{8,9},{9,8},{10,11... | collective-permute-start | bytes 393224 | tf_op jit(solution)/shard_map/ppermute | solution.py:293
  3.5 4.7 %collective-permute-start.3 = (bf16[256,128]{1,0:T(8,128)(2,1)S(1)}, bf16[256,128]{1,0:T(8,128)(2,1)S(1)}, u32[]{:S(2)}, u32[]{:S(2)}) collective-permute-start(bf16[256,128]{1,0:T(8,128)(2,1)S(1)} %get-tuple-element.29.refs_0_), channel_id=1, source_target_pairs={{0,3},{1,8},{2,11},{3,0},{4,7},{5,12},{6,15},{7,4},{8,1},{9,10},{1... | collective-permute-start | bytes 196616 | tf_op jit(solution)/shard_map/ppermute | solution.py:293
  6.2 1.7 %copy-start.1 = (f32[8,16]{1,0:T(8,128)S(1)}, f32[8,16]{1,0:T(8,128)}, u32[]{:S(2)}) copy-start(f32[8,16]{1,0:T(8,128)} %table_ref.1) | copy-start | bytes 1540
  6.2 1.7 %copy-start.2 = (s32[1024]{0:T(1024)S(1)}, s32[1024]{0:T(1024)}, u32[]{:S(2)}) copy-start(s32[1024]{0:T(1024)} %param.11) | copy-start | bytes 12292
  6.2 1.7 %copy-start.3 = (s32[1024]{0:T(1024)S(1)}, s32[1024]{0:T(1024)}, u32[]{:S(2)}) copy-start(s32[1024]{0:T(1024)} %param.12) | copy-start | bytes 12292
  6.2 1.7 %copy-start.4 = (f32[256]{0:T(256)S(1)}, f32[256]{0:T(256)}, u32[]{:S(2)}) copy-start(f32[256]{0:T(256)} %param.10) | copy-start | bytes 3076
  6.3 4.3 %collective-permute-start.2 = (bf16[256,128]{1,0:T(8,128)(2,1)S(1)}, bf16[256,128]{1,0:T(8,128)(2,1)S(1)}, u32[]{:S(2)}, u32[]{:S(2)}) collective-permute-start(bf16[256,128]{1,0:T(8,128)(2,1)S(1)} %get-tuple-element.31.refs_0_), channel_id=1, source_target_pairs={{0,4},{1,8},{2,11},{3,7},{4,0},{5,12},{6,15},{7,3},{8,1},{9,13},{1... | collective-permute-start | bytes 196616 | tf_op jit(solution)/shard_map/ppermute | solution.py:293
  8.3 5.0 %collective-permute-start.5 = (bf16[256,128]{1,0:T(8,128)(2,1)S(1)}, bf16[256,128]{1,0:T(8,128)(2,1)S(1)}, u32[]{:S(2)}, u32[]{:S(2)}) collective-permute-start(bf16[256,128]{1,0:T(8,128)(2,1)S(1)} %get-tuple-element.33.refs_0_), channel_id=1, source_target_pairs={{0,4},{1,2},{2,1},{3,7},{4,0},{5,6},{6,5},{7,3},{8,11},{9,13},{10,... | collective-permute-start | bytes 196616 | tf_op jit(solution)/shard_map/ppermute | solution.py:293
  10.6 4.7 %collective-permute-start.4 = (bf16[256,128]{1,0:T(8,128)(2,1)S(1)}, bf16[256,128]{1,0:T(8,128)(2,1)S(1)}, u32[]{:S(2)}, u32[]{:S(2)}) collective-permute-start(bf16[256,128]{1,0:T(8,128)(2,1)S(1)} %get-tuple-element.35.refs_0_), channel_id=1, source_target_pairs={{0,9},{1,2},{2,1},{3,10},{4,13},{5,6},{6,5},{7,14},{8,11},{9,0},{1... | collective-permute-start | bytes 196616 | tf_op jit(solution)/shard_map/ppermute | solution.py:293
  13.3 4.7 %collective-permute-start.7 = (bf16[256,128]{1,0:T(8,128)(2,1)S(1)}, bf16[256,128]{1,0:T(8,128)(2,1)S(1)}, u32[]{:S(2)}, u32[]{:S(2)}) collective-permute-start(bf16[256,128]{1,0:T(8,128)(2,1)S(1)} %get-tuple-element.37.refs_0_), channel_id=1, source_target_pairs={{0,9},{1,5},{2,6},{3,10},{4,13},{5,1},{6,2},{7,14},{8,12},{9,0},{1... | collective-permute-start | bytes 196616 | tf_op jit(solution)/shard_map/ppermute | solution.py:293
  15.3 4.4 %collective-permute-start.6 = (bf16[256,128]{1,0:T(8,128)(2,1)S(1)}, bf16[256,128]{1,0:T(8,128)(2,1)S(1)}, u32[]{:S(2)}, u32[]{:S(2)}) collective-permute-start(bf16[256,128]{1,0:T(8,128)(2,1)S(1)} %get-tuple-element.39.refs_0_), channel_id=1, source_target_pairs={{0,3},{1,5},{2,6},{3,0},{4,7},{5,1},{6,2},{7,4},{8,12},{9,10},{10,... | collective-permute-start | bytes 196616 | tf_op jit(solution)/shard_map/ppermute | solution.py:293
  18.0 4.5 %collective-permute-start.10 = (bf16[256,128]{1,0:T(8,128)(2,1)S(1)}, bf16[256,128]{1,0:T(8,128)(2,1)S(1)}, u32[]{:S(2)}, u32[]{:S(2)}) collective-permute-start(bf16[256,128]{1,0:T(8,128)(2,1)S(1)} %add.14.refs_0_), channel_id=1, source_target_pairs={{0,17},{1,16},{2,19},{3,18},{4,21},{5,20},{6,23},{7,22},{8,25},{9,... | collective-permute-start | bytes 196616 | tf_op jit(solution)/shard_map/ppermute | solution.py:293
  19.7 4.3 %copy-start = (bf16[1024,1024]{1,0:T(8,128)(2,1)S(1)}, bf16[1024,1024]{1,0:T(8,128)(2,1)}, u32[]{:S(2)}) copy-start(bf16[1024,1024]{1,0:T(8,128)(2,1)} %r_ref.1) | copy-start | bytes 6291460
  19.7 4.0 %collective-permute-start.8 = (bf16[256,128]{1,0:T(8,128)(2,1)S(1)}, bf16[256,128]{1,0:T(8,128)(2,1)S(1)}, u32[]{:S(2)}, u32[]{:S(2)}) collective-permute-start(bf16[256,128]{1,0:T(8,128)(2,1)S(1)} %add.15.refs_2_), channel_id=1, source_target_pairs={{0,17},{1,16},{2,19},{3,18},{4,21},{5,20},{6,23},{7,22},{8,25},{9,... | collective-permute-start | bytes 196616 | tf_op jit(solution)/shard_map/ppermute | solution.py:293
  21.0 2.9 %collective-permute-start.13 = (bf16[256,128]{1,0:T(8,128)(2,1)S(1)}, bf16[256,128]{1,0:T(8,128)(2,1)S(1)}, u32[]{:S(2)}, u32[]{:S(2)}) collective-permute-start(bf16[256,128]{1,0:T(8,128)(2,1)S(1)} %add.15.refs_2_), channel_id=1, source_target_pairs={{0,1},{1,0},{2,3},{3,2},{4,5},{5,4},{6,7},{7,6},{8,9},{9,8},{10,11... | collective-permute-start | bytes 196616 | tf_op jit(solution)/shard_map/ppermute | solution.py:293
  21.9 2.1 %collective-permute-start.12 = (bf16[256,128]{1,0:T(8,128)(2,1)S(1)}, bf16[256,128]{1,0:T(8,128)(2,1)S(1)}, u32[]{:S(2)}, u32[]{:S(2)}) collective-permute-start(bf16[256,128]{1,0:T(8,128)(2,1)S(1)} %add.14.refs_0_), channel_id=1, source_target_pairs={{0,1},{1,0},{2,3},{3,2},{4,5},{5,4},{6,7},{7,6},{8,9},{9,8},{10,11... | collective-permute-start | bytes 196616 | tf_op jit(solution)/shard_map/ppermute | solution.py:293
  22.5 2.0 %collective-permute-start.11 = (bf16[256,128]{1,0:T(8,128)(2,1)S(1)}, bf16[256,128]{1,0:T(8,128)(2,1)S(1)}, u32[]{:S(2)}, u32[]{:S(2)}) collective-permute-start(bf16[256,128]{1,0:T(8,128)(2,1)S(1)} %collective-permute-done.10.refs_0_), channel_id=1, source_target_pairs={{0,1},{1,0},{2,3},{3,2},{4,5},{5,4},{6,7},{7,6},{8,9},{9,8},{10,11... | collective-permute-start | bytes 196616 | tf_op jit(solution)/shard_map/ppermute | solution.py:293
  23.7 1.3 %collective-permute-start.9 = (bf16[256,128]{1,0:T(8,128)(2,1)S(1)}, bf16[256,128]{1,0:T(8,128)(2,1)S(1)}, u32[]{:S(2)}, u32[]{:S(2)}) collective-permute-start(bf16[256,128]{1,0:T(8,128)(2,1)S(1)} %collective-permute-done.8.own_ref), channel_id=1, source_target_pairs={{0,1},{1,0},{2,3},{3,2},{4,5},{5,4},{6,7},{7,6},{8,9},{9,8},{10,11... | collective-permute-start | bytes 196616 | tf_op jit(solution)/shard_map/ppermute | solution.py:293

commit v10 on v9

--- a/solution.py
+++ b/solution.py
@@ -11,7 +11,7 @@
 BF16 = jnp.bfloat16
 MIB = 1 << 20
 CHAINS = 2
-BLOCKS = (1, 2, 2, 2, 2, 2, 2, 2, 1)
+BLOCKS = (1, 3, 4, 4, 3, 1)
 EIG_FLIP = 10
 GROUP_FLIP = 1
 FIRST = 8

time: 27.7 us -> 27.8 us (level)
  no operation moved by 1% of the time
where the time goes in v10:
time: 27.8 us; the launch traced here: 27.7 us
  starting transfers between devices  16.3 us (59%)
  Pallas kernels  6.46 us (23%)
  waiting for transfers between devices  4.73 us (17%)
    ppermute x14, starting transfers between devices, swap(): return lax.ppermute(value, ('groups', 'eig'), pairs)  16.3 us
    ppermute x14, waiting for transfers between devices, swap(): return lax.ppermute(value, ('groups', 'eig'), pairs)  4.73 us
    pallas_call x1, Pallas kernels, weights(): pl.pallas_call(functools.partial(weights_kernel, *place), in_specs=[VMEM]...  2.71 us
    pallas_call x1, Pallas kernels, gram_first(): pl.pallas_call(gram_first_kernel, in_specs=[HBM, HBM], out_specs=[VMEM] *...  2 us
    pallas_call x2, Pallas kernels, share(): pl.pallas_call(functools.partial(share_kernel, places, before is not None...  0.87 us
  transfers between devices with their start and end apart: 14, of which 8 were waited for; matrix products, arithmetic and copies ran while one was open for 0% of the time, Pallas kernels for 6%

profile of v10, /device:TPU:0, one launch (start us, length us, event | category | flops | bytes accessed | tf_op | source)
XLA Modules:
  0.0 27.7 jit_solution(17757473638869092490)
XLA Ops:
  0.0 2.0 %gram_first.1 = (f32[256,128]{1,0:T(8,128)S(1)}, f32[256,128]{1,0:T(8,128)S(1)}, bf16[256,2048]{1,0:T(8,128)(2,1)S(1)}, bf16[2048,256]{1,0:T(8,128)(2,1)S(1)}) custom-call(bf16[1024,2048]{1,0:T(8,128)(2,1)} %f_hbm.1, bf16[2048,256]{1,0:T(8,128)(2,1)} %b_hbm.1), custom_call_target="tpu_custom_call" | custom-call | flops 268435456 | bytes 2097152 | tf_op jit(solution)/shard_map/gram_first/pallas_call | solution.py:103
  2.0 0.5 %collective-permute-start.1 = (f32[256,128]{1,0:T(8,128)S(1)}, f32[256,128]{1,0:T(8,128)S(1)}, u32[]{:S(2)}, u32[]{:S(2)}) collective-permute-start(f32[256,128]{1,0:T(8,128)S(1)} %get-tuple-element.25.refs_0_), channel_id=1, source_target_pairs={{0,1},{1,0},{2,3},{3,2},{4,5},{5,4},{6,7},{7,6},{8,9},{9,8},{10,11... | collective-permute-start | bytes 393224 | tf_op jit(solution)/shard_map/ppermute | solution.py:293
  2.5 0.4 %gram_rest.1 = (f32[256,128]{1,0:T(8,128)S(1)}, f32[256,128]{1,0:T(8,128)S(1)}) custom-call(bf16[256,2048]{1,0:T(8,128)(2,1)S(1)} %get-tuple-element.23.f_ref, bf16[2048,256]{1,0:T(8,128)(2,1)S(1)} %get-tuple-element.24.b_ref, f32[256,128]{1,0:T(8,128)S(1)} %get-tuple-element.25.refs_0_), custom_call_target="tpu_custom_call" | custom-call | flops 268435456 | bytes 2097152 | tf_op jit(solution)/shard_map/gram_rest/pallas_call | solution.py:128
  3.0 0.1 collective-permute-start
  3.1 0.4 %collective-permute-done.1.got_ref = f32[256,128]{1,0:T(8,128)S(1)} collective-permute-done((f32[256,128]{1,0:T(8,128)S(1)}, f32[256,128]{1,0:T(8,128)S(1)}, u32[]{:S(2)}, u32[]{:S(2)}) %collective-permute-start.1) | collective-permute-done | bytes 131104 | tf_op jit(solution)/shard_map/ppermute | solution.py:293
  3.5 2.7 %collective-permute-start.3 = (bf16[256,128]{1,0:T(8,128)(2,1)S(1)}, bf16[256,128]{1,0:T(8,128)(2,1)S(1)}, u32[]{:S(2)}, u32[]{:S(2)}) collective-permute-start(bf16[256,128]{1,0:T(8,128)(2,1)S(1)} %get-tuple-element.29.refs_0_), channel_id=1, source_target_pairs={{0,3},{1,8},{2,11},{3,0},{4,7},{5,12},{6,15},{7,4},{8,1},{9,10},{1... | collective-permute-start | bytes 196616 | tf_op jit(solution)/shard_map/ppermute | solution.py:293
  6.2 0.0 collective-permute-done.got_ref
  6.2 0.0 copy-start.1
  6.2 0.0 copy-start.2
  6.2 0.0 copy-start.3
  6.2 0.0 copy-start.4
  6.3 1.6 %collective-permute-start.2 = (bf16[256,128]{1,0:T(8,128)(2,1)S(1)}, bf16[256,128]{1,0:T(8,128)(2,1)S(1)}, u32[]{:S(2)}, u32[]{:S(2)}) collective-permute-start(bf16[256,128]{1,0:T(8,128)(2,1)S(1)} %get-tuple-element.31.refs_0_), channel_id=1, source_target_pairs={{0,4},{1,8},{2,11},{3,7},{4,0},{5,12},{6,15},{7,3},{8,1},{9,13},{1... | collective-permute-start | bytes 196616 | tf_op jit(solution)/shard_map/ppermute | solution.py:293
  7.9 0.0 copy-done.1
  7.9 0.0 copy-done.2
  7.9 0.0 copy-done.3
  7.9 0.0 copy-done.4
  7.9 0.3 %inverse.1.refs_0_.inverse_ref = f32[256,1024]{1,0:T(8,128)S(1)} custom-call(f32[8,16]{1,0:T(8,128)S(1)} %copy-done.1, s32[1,1024]{1,0:T(1,128)S(1)} %bitcast.3, s32[1,1024]{1,0:T(1,128)S(1)} %bitcast.4, f32[1,256]{1,0:T(1,128)S(1)} %bitcast.5, bf16[256,128]{1,0:T(8,128)(2,1)S(1)} %get-tuple-element.31.refs_0_), custom_call_target="tpu_custom_call" | custom-call | flops 2097152 | bytes 524288 | tf_op jit(solution)/shard_map/inverse/pallas_call | solution.py:164
  8.2 0.0 collective-permute-done.3.got_ref
  8.3 2.0 %collective-permute-start.5 = (bf16[256,128]{1,0:T(8,128)(2,1)S(1)}, bf16[256,128]{1,0:T(8,128)(2,1)S(1)}, u32[]{:S(2)}, u32[]{:S(2)}) collective-permute-start(bf16[256,128]{1,0:T(8,128)(2,1)S(1)} %get-tuple-element.33.refs_0_), channel_id=1, source_target_pairs={{0,4},{1,2},{2,1},{3,7},{4,0},{5,6},{6,5},{7,3},{8,11},{9,13},{10,... | collective-permute-start | bytes 196616 | tf_op jit(solution)/shard_map/ppermute | solution.py:293
  10.3 0.3 %collective-permute-done.2.got_ref = bf16[256,128]{1,0:T(8,128)(2,1)S(1)} collective-permute-done((bf16[256,128]{1,0:T(8,128)(2,1)S(1)}, bf16[256,128]{1,0:T(8,128)(2,1)S(1)}, u32[]{:S(2)}, u32[]{:S(2)}) %collective-permute-start.2) | collective-permute-done | bytes 65568 | tf_op jit(solution)/shard_map/ppermute | solution.py:293
  10.6 2.1 %collective-permute-start.4 = (bf16[256,128]{1,0:T(8,128)(2,1)S(1)}, bf16[256,128]{1,0:T(8,128)(2,1)S(1)}, u32[]{:S(2)}, u32[]{:S(2)}) collective-permute-start(bf16[256,128]{1,0:T(8,128)(2,1)S(1)} %get-tuple-element.35.refs_0_), channel_id=1, source_target_pairs={{0,9},{1,2},{2,1},{3,10},{4,13},{5,6},{6,5},{7,14},{8,11},{9,0},{1... | collective-permute-start | bytes 196616 | tf_op jit(solution)/shard_map/ppermute | solution.py:293
  12.8 0.5 %collective-permute-done.5.got_ref = bf16[256,128]{1,0:T(8,128)(2,1)S(1)} collective-permute-done((bf16[256,128]{1,0:T(8,128)(2,1)S(1)}, bf16[256,128]{1,0:T(8,128)(2,1)S(1)}, u32[]{:S(2)}, u32[]{:S(2)}) %collective-permute-start.5) | collective-permute-done | bytes 65568 | tf_op jit(solution)/shard_map/ppermute | solution.py:293
  13.3 1.3 %collective-permute-start.7 = (bf16[256,128]{1,0:T(8,128)(2,1)S(1)}, bf16[256,128]{1,0:T(8,128)(2,1)S(1)}, u32[]{:S(2)}, u32[]{:S(2)}) collective-permute-start(bf16[256,128]{1,0:T(8,128)(2,1)S(1)} %get-tuple-element.37.refs_0_), channel_id=1, source_target_pairs={{0,9},{1,5},{2,6},{3,10},{4,13},{5,1},{6,2},{7,14},{8,12},{9,0},{1... | collective-permute-start | bytes 196616 | tf_op jit(solution)/shard_map/ppermute | solution.py:293
  14.6 0.7 %collective-permute-done.4.got_ref = bf16[256,128]{1,0:T(8,128)(2,1)S(1)} collective-permute-done((bf16[256,128]{1,0:T(8,128)(2,1)S(1)}, bf16[256,128]{1,0:T(8,128)(2,1)S(1)}, u32[]{:S(2)}, u32[]{:S(2)}) %collective-permute-start.4) | collective-permute-done | bytes 65568 | tf_op jit(solution)/shard_map/ppermute | solution.py:293
  15.3 1.7 %collective-permute-start.6 = (bf16[256,128]{1,0:T(8,128)(2,1)S(1)}, bf16[256,128]{1,0:T(8,128)(2,1)S(1)}, u32[]{:S(2)}, u32[]{:S(2)}) collective-permute-start(bf16[256,128]{1,0:T(8,128)(2,1)S(1)} %get-tuple-element.39.refs_0_), channel_id=1, source_target_pairs={{0,3},{1,5},{2,6},{3,0},{4,7},{5,1},{6,2},{7,4},{8,12},{9,10},{10,... | collective-permute-start | bytes 196616 | tf_op jit(solution)/shard_map/ppermute | solution.py:293
  17.0 1.0 %collective-permute-done.7.got_ref = bf16[256,128]{1,0:T(8,128)(2,1)S(1)} collective-permute-done((bf16[256,128]{1,0:T(8,128)(2,1)S(1)}, bf16[256,128]{1,0:T(8,128)(2,1)S(1)}, u32[]{:S(2)}, u32[]{:S(2)}) %collective-permute-start.7) | collective-permute-done | bytes 65568 | tf_op jit(solution)/shard_map/ppermute | solution.py:293
  18.0 1.6 %collective-permute-start.10 = (bf16[256,128]{1,0:T(8,128)(2,1)S(1)}, bf16[256,128]{1,0:T(8,128)(2,1)S(1)}, u32[]{:S(2)}, u32[]{:S(2)}) collective-permute-start(bf16[256,128]{1,0:T(8,128)(2,1)S(1)} %add.14.refs_0_), channel_id=1, source_target_pairs={{0,17},{1,16},{2,19},{3,18},{4,21},{5,20},{6,23},{7,22},{8,25},{9,... | collective-permute-start | bytes 196616 | tf_op jit(solution)/shard_map/ppermute | solution.py:293
  19.7 0.0 collective-permute-done.6.got_ref
  19.7 0.0 copy-start
  19.7 1.4 %collective-permute-start.8 = (bf16[256,128]{1,0:T(8,128)(2,1)S(1)}, bf16[256,128]{1,0:T(8,128)(2,1)S(1)}, u32[]{:S(2)}, u32[]{:S(2)}) collective-permute-start(bf16[256,128]{1,0:T(8,128)(2,1)S(1)} %add.15.refs_2_), channel_id=1, source_target_pairs={{0,17},{1,16},{2,19},{3,18},{4,21},{5,20},{6,23},{7,22},{8,25},{9,... | collective-permute-start | bytes 196616 | tf_op jit(solution)/shard_map/ppermute | solution.py:293
  21.0 0.8 %collective-permute-start.13 = (bf16[256,128]{1,0:T(8,128)(2,1)S(1)}, bf16[256,128]{1,0:T(8,128)(2,1)S(1)}, u32[]{:S(2)}, u32[]{:S(2)}) collective-permute-start(bf16[256,128]{1,0:T(8,128)(2,1)S(1)} %add.15.refs_2_), channel_id=1, source_target_pairs={{0,1},{1,0},{2,3},{3,2},{4,5},{5,4},{6,7},{7,6},{8,9},{9,8},{10,11... | collective-permute-start | bytes 196616 | tf_op jit(solution)/shard_map/ppermute | solution.py:293
  21.9 0.0 collective-permute-start.12
  21.9 0.6 %collective-permute-done.10.refs_0_ = bf16[256,128]{1,0:T(8,128)(2,1)S(1)} collective-permute-done((bf16[256,128]{1,0:T(8,128)(2,1)S(1)}, bf16[256,128]{1,0:T(8,128)(2,1)S(1)}, u32[]{:S(2)}, u32[]{:S(2)}) %collective-permute-start.10) | collective-permute-done | bytes 65568 | tf_op jit(solution)/shard_map/ppermute | solution.py:293
  22.5 0.1 collective-permute-start.11
  22.6 1.1 %collective-permute-done.8.own_ref = bf16[256,128]{1,0:T(8,128)(2,1)S(1)} collective-permute-done((bf16[256,128]{1,0:T(8,128)(2,1)S(1)}, bf16[256,128]{1,0:T(8,128)(2,1)S(1)}, u32[]{:S(2)}, u32[]{:S(2)}) %collective-permute-start.8) | collective-permute-done | bytes 65568 | tf_op jit(solution)/shard_map/ppermute | solution.py:293
  23.7 0.3 %collective-permute-start.9 = (bf16[256,128]{1,0:T(8,128)(2,1)S(1)}, bf16[256,128]{1,0:T(8,128)(2,1)S(1)}, u32[]{:S(2)}, u32[]{:S(2)}) collective-permute-start(bf16[256,128]{1,0:T(8,128)(2,1)S(1)} %collective-permute-done.8.own_ref), channel_id=1, source_target_pairs={{0,1},{1,0},{2,3},{3,2},{4,5},{5,4},{6,7},{7,6},{8,9},{9,8},{10,11... | collective-permute-start | bytes 196616 | tf_op jit(solution)/shard_map/ppermute | solution.py:293
  24.0 0.0 collective-permute-done.13.refs_3_
  24.0 0.0 collective-permute-done.12.refs_1_
  24.0 0.0 copy-done
  24.0 0.5 %share.2.refs_3_ = f32[256,1024]{1,0:T(8,128)S(1)} custom-call(bf16[256,128]{1,0:T(8,128)(2,1)S(1)} %add.14.refs_0_, bf16[256,128]{1,0:T(8,128)(2,1)S(1)} %collective-permute-done.12.refs_1_, bf16[256,128]{1,0:T(8,128)(2,1)S(1)} %add.15.refs_2_, bf16[256,128]{1,0:T(8,128)(2,1)S(1)} %collective-permute-done.13.refs_3_, bf16[1024,1024]{1,0:T(8,128)(2,1)S(1)} %copy-done), custom_call_target="tpu_custom_call" | custom-call | flops 268435456 | bytes 524288 | tf_op jit(solution)/shard_map/share/pallas_call | solution.py:228
  24.5 0.0 collective-permute-done.11.refs_1_
  24.5 0.4 %share.3.before_ref = f32[256,1024]{1,0:T(8,128)S(1)} custom-call(bf16[256,128]{1,0:T(8,128)(2,1)S(1)} %collective-permute-done.10.refs_0_, bf16[256,128]{1,0:T(8,128)(2,1)S(1)} %collective-permute-done.11.refs_1_, bf16[1024,1024]{1,0:T(8,128)(2,1)S(1)} %copy-done, f32[256,1024]{1,0:T(8,128)S(1)} %share.2.refs_3_), custom_call_target="tpu_custom_call" | custom-call | flops 134217728 | bytes 524288 | tf_op jit(solution)/shard_map/share/pallas_call | solution.py:228
  24.9 0.1 collective-permute-done.9.got_ref
  24.9 2.7 %weights.1 = bf16[2048,1024]{1,0:T(8,128)(2,1)} custom-call(bf16[256,128]{1,0:T(8,128)(2,1)S(1)} %collective-permute-done.8.own_ref, bf16[256,128]{1,0:T(8,128)(2,1)S(1)} %collective-permute-done.9.got_ref, bf16[1024,1024]{1,0:T(8,128)(2,1)S(1)} %copy-done, f32[256,1024]{1,0:T(8,128)S(1)} %share.3.before_ref, f32[256,1024]{1,0:T(8,128)S(1)} %inverse.1.refs_0_.inverse_ref, ...), custom_call_target="tpu_custom_call" | custom-call | flops 1073741824 | bytes 4194304 | tf_op jit(solution)/shard_map/weights/pallas_call | solution.py:269
  (8 shorter events, 0.1 us)
Async XLA Ops:
  2.0 1.5 %collective-permute-start.1 = (f32[256,128]{1,0:T(8,128)S(1)}, f32[256,128]{1,0:T(8,128)S(1)}, u32[]{:S(2)}, u32[]{:S(2)}) collective-permute-start(f32[256,128]{1,0:T(8,128)S(1)} %get-tuple-element.25.refs_0_), channel_id=1, source_target_pairs={{0,1},{1,0},{2,3},{3,2},{4,5},{5,4},{6,7},{7,6},{8,9},{9,8},{10,11... | collective-permute-start | bytes 393224 | tf_op jit(solution)/shard_map/ppermute | solution.py:293
  3.0 3.3 %collective-permute-start = (f32[256,128]{1,0:T(8,128)S(1)}, f32[256,128]{1,0:T(8,128)S(1)}, u32[]{:S(2)}, u32[]{:S(2)}) collective-permute-start(f32[256,128]{1,0:T(8,128)S(1)} %get-tuple-element.27.refs_0_), channel_id=1, source_target_pairs={{0,1},{1,0},{2,3},{3,2},{4,5},{5,4},{6,7},{7,6},{8,9},{9,8},{10,11... | collective-permute-start | bytes 393224 | tf_op jit(solution)/shard_map/ppermute | solution.py:293
  3.5 4.7 %collective-permute-start.3 = (bf16[256,128]{1,0:T(8,128)(2,1)S(1)}, bf16[256,128]{1,0:T(8,128)(2,1)S(1)}, u32[]{:S(2)}, u32[]{:S(2)}) collective-permute-start(bf16[256,128]{1,0:T(8,128)(2,1)S(1)} %get-tuple-element.29.refs_0_), channel_id=1, source_target_pairs={{0,3},{1,8},{2,11},{3,0},{4,7},{5,12},{6,15},{7,4},{8,1},{9,10},{1... | collective-permute-start | bytes 196616 | tf_op jit(solution)/shard_map/ppermute | solution.py:293
  6.2 1.7 %copy-start.1 = (f32[8,16]{1,0:T(8,128)S(1)}, f32[8,16]{1,0:T(8,128)}, u32[]{:S(2)}) copy-start(f32[8,16]{1,0:T(8,128)} %table_ref.1) | copy-start | bytes 1540
  6.2 1.7 %copy-start.2 = (s32[1024]{0:T(1024)S(1)}, s32[1024]{0:T(1024)}, u32[]{:S(2)}) copy-start(s32[1024]{0:T(1024)} %param.11) | copy-start | bytes 12292
  6.2 1.7 %copy-start.3 = (s32[1024]{0:T(1024)S(1)}, s32[1024]{0:T(1024)}, u32[]{:S(2)}) copy-start(s32[1024]{0:T(1024)} %param.12) | copy-start | bytes 12292
  6.2 1.7 %copy-start.4 = (f32[256]{0:T(256)S(1)}, f32[256]{0:T(256)}, u32[]{:S(2)}) copy-start(f32[256]{0:T(256)} %param.10) | copy-start | bytes 3076
  6.3 4.3 %collective-permute-start.2 = (bf16[256,128]{1,0:T(8,128)(2,1)S(1)}, bf16[256,128]{1,0:T(8,128)(2,1)S(1)}, u32[]{:S(2)}, u32[]{:S(2)}) collective-permute-start(bf16[256,128]{1,0:T(8,128)(2,1)S(1)} %get-tuple-element.31.refs_0_), channel_id=1, source_target_pairs={{0,4},{1,8},{2,11},{3,7},{4,0},{5,12},{6,15},{7,3},{8,1},{9,13},{1... | collective-permute-start | bytes 196616 | tf_op jit(solution)/shard_map/ppermute | solution.py:293
  8.3 5.0 %collective-permute-start.5 = (bf16[256,128]{1,0:T(8,128)(2,1)S(1)}, bf16[256,128]{1,0:T(8,128)(2,1)S(1)}, u32[]{:S(2)}, u32[]{:S(2)}) collective-permute-start(bf16[256,128]{1,0:T(8,128)(2,1)S(1)} %get-tuple-element.33.refs_0_), channel_id=1, source_target_pairs={{0,4},{1,2},{2,1},{3,7},{4,0},{5,6},{6,5},{7,3},{8,11},{9,13},{10,... | collective-permute-start | bytes 196616 | tf_op jit(solution)/shard_map/ppermute | solution.py:293
  10.6 4.7 %collective-permute-start.4 = (bf16[256,128]{1,0:T(8,128)(2,1)S(1)}, bf16[256,128]{1,0:T(8,128)(2,1)S(1)}, u32[]{:S(2)}, u32[]{:S(2)}) collective-permute-start(bf16[256,128]{1,0:T(8,128)(2,1)S(1)} %get-tuple-element.35.refs_0_), channel_id=1, source_target_pairs={{0,9},{1,2},{2,1},{3,10},{4,13},{5,6},{6,5},{7,14},{8,11},{9,0},{1... | collective-permute-start | bytes 196616 | tf_op jit(solution)/shard_map/ppermute | solution.py:293
  13.3 4.7 %collective-permute-start.7 = (bf16[256,128]{1,0:T(8,128)(2,1)S(1)}, bf16[256,128]{1,0:T(8,128)(2,1)S(1)}, u32[]{:S(2)}, u32[]{:S(2)}) collective-permute-start(bf16[256,128]{1,0:T(8,128)(2,1)S(1)} %get-tuple-element.37.refs_0_), channel_id=1, source_target_pairs={{0,9},{1,5},{2,6},{3,10},{4,13},{5,1},{6,2},{7,14},{8,12},{9,0},{1... | collective-permute-start | bytes 196616 | tf_op jit(solution)/shard_map/ppermute | solution.py:293
  15.3 4.4 %collective-permute-start.6 = (bf16[256,128]{1,0:T(8,128)(2,1)S(1)}, bf16[256,128]{1,0:T(8,128)(2,1)S(1)}, u32[]{:S(2)}, u32[]{:S(2)}) collective-permute-start(bf16[256,128]{1,0:T(8,128)(2,1)S(1)} %get-tuple-element.39.refs_0_), channel_id=1, source_target_pairs={{0,3},{1,5},{2,6},{3,0},{4,7},{5,1},{6,2},{7,4},{8,12},{9,10},{10,... | collective-permute-start | bytes 196616 | tf_op jit(solution)/shard_map/ppermute | solution.py:293
  18.0 4.5 %collective-permute-start.10 = (bf16[256,128]{1,0:T(8,128)(2,1)S(1)}, bf16[256,128]{1,0:T(8,128)(2,1)S(1)}, u32[]{:S(2)}, u32[]{:S(2)}) collective-permute-start(bf16[256,128]{1,0:T(8,128)(2,1)S(1)} %add.14.refs_0_), channel_id=1, source_target_pairs={{0,17},{1,16},{2,19},{3,18},{4,21},{5,20},{6,23},{7,22},{8,25},{9,... | collective-permute-start | bytes 196616 | tf_op jit(solution)/shard_map/ppermute | solution.py:293
  19.7 4.3 %copy-start = (bf16[1024,1024]{1,0:T(8,128)(2,1)S(1)}, bf16[1024,1024]{1,0:T(8,128)(2,1)}, u32[]{:S(2)}) copy-start(bf16[1024,1024]{1,0:T(8,128)(2,1)} %r_ref.1) | copy-start | bytes 6291460
  19.7 4.0 %collective-permute-start.8 = (bf16[256,128]{1,0:T(8,128)(2,1)S(1)}, bf16[256,128]{1,0:T(8,128)(2,1)S(1)}, u32[]{:S(2)}, u32[]{:S(2)}) collective-permute-start(bf16[256,128]{1,0:T(8,128)(2,1)S(1)} %add.15.refs_2_), channel_id=1, source_target_pairs={{0,17},{1,16},{2,19},{3,18},{4,21},{5,20},{6,23},{7,22},{8,25},{9,... | collective-permute-start | bytes 196616 | tf_op jit(solution)/shard_map/ppermute | solution.py:293
  21.0 2.9 %collective-permute-start.13 = (bf16[256,128]{1,0:T(8,128)(2,1)S(1)}, bf16[256,128]{1,0:T(8,128)(2,1)S(1)}, u32[]{:S(2)}, u32[]{:S(2)}) collective-permute-start(bf16[256,128]{1,0:T(8,128)(2,1)S(1)} %add.15.refs_2_), channel_id=1, source_target_pairs={{0,1},{1,0},{2,3},{3,2},{4,5},{5,4},{6,7},{7,6},{8,9},{9,8},{10,11... | collective-permute-start | bytes 196616 | tf_op jit(solution)/shard_map/ppermute | solution.py:293
  21.9 2.1 %collective-permute-start.12 = (bf16[256,128]{1,0:T(8,128)(2,1)S(1)}, bf16[256,128]{1,0:T(8,128)(2,1)S(1)}, u32[]{:S(2)}, u32[]{:S(2)}) collective-permute-start(bf16[256,128]{1,0:T(8,128)(2,1)S(1)} %add.14.refs_0_), channel_id=1, source_target_pairs={{0,1},{1,0},{2,3},{3,2},{4,5},{5,4},{6,7},{7,6},{8,9},{9,8},{10,11... | collective-permute-start | bytes 196616 | tf_op jit(solution)/shard_map/ppermute | solution.py:293
  22.5 2.0 %collective-permute-start.11 = (bf16[256,128]{1,0:T(8,128)(2,1)S(1)}, bf16[256,128]{1,0:T(8,128)(2,1)S(1)}, u32[]{:S(2)}, u32[]{:S(2)}) collective-permute-start(bf16[256,128]{1,0:T(8,128)(2,1)S(1)} %collective-permute-done.10.refs_0_), channel_id=1, source_target_pairs={{0,1},{1,0},{2,3},{3,2},{4,5},{5,4},{6,7},{7,6},{8,9},{9,8},{10,11... | collective-permute-start | bytes 196616 | tf_op jit(solution)/shard_map/ppermute | solution.py:293
  23.7 1.3 %collective-permute-start.9 = (bf16[256,128]{1,0:T(8,128)(2,1)S(1)}, bf16[256,128]{1,0:T(8,128)(2,1)S(1)}, u32[]{:S(2)}, u32[]{:S(2)}) collective-permute-start(bf16[256,128]{1,0:T(8,128)(2,1)S(1)} %collective-permute-done.8.own_ref), channel_id=1, source_target_pairs={{0,1},{1,0},{2,3},{3,2},{4,5},{5,4},{6,7},{7,6},{8,9},{9,8},{10,11... | collective-permute-start | bytes 196616 | tf_op jit(solution)/shard_map/ppermute | solution.py:293
